TPU v7x, 32 devices: a whole 2x2x4 slice. The times are simulated.
32 devices in a mesh: pool: 16 (over z, y, x), tensor: 2 (over core).
Axes of the slice: x: 2, y: 2, z: 4, core: 2. Of those that a mesh axis runs over, the one named last changes fastest.
Arguments:
- tokens: bfloat16 [2, 256, 8192], P(None, None, 'tensor'), may hold values from -6 to 6
- gate_up_weight: bfloat16 [8192, 2, 28672], P('tensor', None, 'pool'), may hold values from -0.0625 to 0.0625
- down_weight: bfloat16 [28672, 8192], P('pool', 'tensor'), may hold values from -0.03125 to 0.03125
- shrink_store: bfloat16 [16, 2, 8192, 64], P('pool', None, 'tensor'), may hold values from -0.0625 to 0.0625
- expand_store: bfloat16 [16, 2, 64, 28672], P('pool', None, 'tensor'), may hold values from -0.75 to 0.75
- block_adapter: int32 [2, 2], replicated, may hold values from 0 to 15
- block_live: int32 [2, 2], replicated, may hold values from 1 to 128, 192 in all within a row
- adapter_slot: int32 [16], replicated, may hold values from 0 to 15, each once
Outputs:
- layer_out: bfloat16 [2, 256, 8192], P(None, 'pool', 'tensor')
Inputs may be any that keep to these rules, and one draw needn't show every extreme that they name: Each storage slot holds exactly one adapter; adapter a is stored on index adapter_slot[a] of pool; each index of pool holds exactly one storage slot. `block_live`: rows of a block after its live rows are padding; the live rows of one decode step sum to 192.
All inputs are finite; a program needn't handle non-finite values.
Results may differ from a plain program's by a relative error of at most 0.0049.
Values may be sent and summed in bfloat16 or wider, within the bound.
No kernel may reach another device: no remote copies, remote signals or barrier semaphores. Data moves between devices by JAX's collectives and lax.ppermute only.
A program may use at most 192 MiB of HBM per device.

v0:
```python
import jax
import jax.numpy as jnp
from jax import lax
from jax.sharding import PartitionSpec as P

BLK = 128
NBLK = 2


def bit_pairs(axis_name, bit):
    return [(i, i ^ (1 << bit)) for i in range(lax.axis_size(axis_name))]


def halve(array, axis_name, bit, axis, wire=None):
    mine = (lax.axis_index(axis_name) >> bit) & 1
    keep = lax.dynamic_index_in_dim(array, mine, axis, keepdims=False)
    send = lax.dynamic_index_in_dim(array, 1 - mine, axis, keepdims=False)
    if wire is not None:
        send = send.astype(wire)
    return keep, send


def swap(array, axis_name, bit):
    return lax.ppermute(array, axis_name, bit_pairs(axis_name, bit))


def bits_of(axis_name):
    return lax.axis_size(axis_name).bit_length() - 1


def scatter_sum(array, axis_name, axis):
    count = bits_of(axis_name)
    shape = array.shape
    length = shape[axis] >> count
    current = array.reshape(shape[:axis] + (2,) * count + (length,) + shape[axis + 1 :])
    for bit in reversed(range(count)):
        keep, send = halve(current, axis_name, bit, axis)
        current = keep + swap(send, axis_name, bit)
    return current


def gather(array, axis_name, axis):
    for bit in range(bits_of(axis_name)):
        mine = (lax.axis_index(axis_name) >> bit) & 1
        got = swap(array, axis_name, bit)
        array = jnp.where(
            mine == 0,
            jnp.concatenate([array, got], axis=axis),
            jnp.concatenate([got, array], axis=axis),
        )
    return array


def after(array, arrived):
    return lax.optimization_barrier((array, arrived))[0]


def shards(
    tokens,
    gate_up_weight,
    down_weight,
    shrink_store,
    expand_store,
    block_adapter,
    block_live,
    adapter_slot,
):
    steps, total_rows, width_local = tokens.shape
    units = gate_up_weight.shape[2]
    pool_count = lax.axis_size("pool")
    tensor_count = lax.axis_size("tensor")
    me = lax.axis_index("pool")
    core = lax.axis_index("tensor")
    kinds = gate_up_weight.shape[1]
    ranks_local = expand_store.shape[2]
    rank = ranks_local * tensor_count
    units_here = units // tensor_count
    rows_here = total_rows // pool_count
    slots = adapter_slot[block_adapter]

    second = []
    outgoing = []
    for kind in range(kinds):
        columns = expand_store[0, kind].reshape(ranks_local, pool_count * tensor_count, units_here)
        columns = columns.transpose(1, 0, 2)
        if second:
            columns = after(columns, second[-1])
        outgoing.append(columns)
        second.append(
            lax.all_to_all(columns, ("pool", "tensor"), split_axis=0, concat_axis=0, tiled=True)
        )
    pages = [one.reshape(pool_count, rank, units_here) for one in second]

    first = jnp.einsum(
        "snd,kdc->snkc",
        after(tokens, outgoing[0]),
        shrink_store[0],
        preferred_element_type=jnp.float32,
    )
    mine = jnp.repeat((slots == me).astype(jnp.float32), total_rows // NBLK, axis=1)
    first = first * mine[:, :, None, None]
    first = first.reshape(steps * total_rows, kinds * rank)
    shrunk = scatter_sum(first, "tensor", 0)

    def sum_over(shrunk, some_bits):
        for bit in some_bits:
            shrunk = shrunk + swap(shrunk, "pool", bit)
        return shrunk

    middle = bits_of("pool") // 2
    shrunk = sum_over(shrunk, range(middle))

    flat_tokens = tokens.reshape(steps * total_rows, width_local)

    weights = after(gate_up_weight, outgoing[0])
    weights = jnp.transpose(weights, (1, 0, 2))
    weights, shrunk, flat_tokens, _ = lax.optimization_barrier(
        (weights, shrunk, flat_tokens, second[0])
    )
    shrunk = sum_over(shrunk, range(middle, bits_of("pool")))
    products = [
        jnp.dot(flat_tokens, weights[kind], preferred_element_type=jnp.float32)
        for kind in range(kinds)
    ]
    products[-1] = after(products[-1], second[-1])
    main = []
    for product in products:
        if tensor_count == 2:
            low_share, high_share = product[:, :units_here], product[:, units_here:]
            got = swap(jnp.where(core == 0, high_share, low_share), "tensor", 0)
            main.append(jnp.where(core == 0, low_share, high_share) + got)
        else:
            main.append(scatter_sum(product, "tensor", 1))

    shrunk = gather(shrunk, "tensor", 0)
    high = shrunk.astype(jnp.bfloat16)
    low = (shrunk - high.astype(jnp.float32)).astype(jnp.bfloat16)

    bits = bits_of("pool")
    positions = me * rows_here + jnp.arange(rows_here)
    owners = positions // BLK
    half = down_weight.shape[1] // 2
    orders = [list(range(bits)), [1, 0] + list(range(2, bits))]
    parts = []
    for step in range(steps):
        hidden_blocks = []
        for block in range(NBLK):
            page = [
                lax.dynamic_index_in_dim(one, slots[step, block], 0, keepdims=False)
                for one in pages
            ]
            rows = slice(step * total_rows + block * BLK, step * total_rows + (block + 1) * BLK)
            gate, up = [
                main[kind][rows]
                + jnp.dot(
                    jnp.concatenate(
                        [part[rows, kind * rank : (kind + 1) * rank] for part in (high, low)], axis=1
                    ),
                    jnp.concatenate([page[kind], page[kind]], axis=0),
                    preferred_element_type=jnp.float32,
                )
                for kind in range(kinds)
            ]
            hidden_blocks.append((jax.nn.silu(gate) * up).astype(jnp.bfloat16))
        hidden = gather(jnp.concatenate(hidden_blocks, axis=0), "tensor", 1)
        parts.append(
            [
                jnp.dot(
                    hidden,
                    down_weight[:, piece * half : (piece + 1) * half],
                    preferred_element_type=jnp.float32,
                ).reshape((2,) * bits + (rows_here, half))
                for piece in range(2)
            ]
        )

    kept = [[None] * 2 for _ in range(steps)]
    sends = [[None] * 2 for _ in range(steps)]
    arrived = [None] * steps

    def prepare(step, stage):
        for piece in range(2):
            left = sorted(orders[piece][stage:], reverse=True)
            bit = orders[piece][stage]
            kept[step][piece], sends[step][piece] = halve(
                parts[step][piece], "pool", bit, left.index(bit), jnp.bfloat16
            )

    def exchange_rows(step, stage):
        arrived[step] = [
            swap(sends[step][piece], "pool", orders[piece][stage]) for piece in range(2)
        ]
        parts[step] = [
            kept[step][piece] + arrived[step][piece].astype(jnp.float32) for piece in range(2)
        ]

    for stage in range(bits):
        for step in range(steps):
            prepare(step, stage)
            if stage == 0 and step:
                sends[step] = after(sends[step], arrived[step - 1])
            if stage == bits - 1 and step == 0:
                sends[step] = after(sends[step], later_sends)
            if stage == 1 and step == steps - 1:
                later_sends = list(sends[step])
            exchange_rows(step, stage)
    results = []
    for step in range(steps):
        live = jnp.sum(
            (owners[:, None] == jnp.arange(NBLK)[None, :]) * block_live[step][None, :], axis=1
        )
        keep = (positions % BLK < live).astype(jnp.float32)
        summed = jnp.concatenate(parts[step], axis=1)
        results.append((summed * keep[:, None]).astype(jnp.bfloat16))
    return jnp.stack(results)


def solution(mesh):
    return jax.shard_map(
        shards,
        mesh=mesh,
        in_specs=(
            P(None, None, "tensor"),
            P("tensor", None, "pool"),
            P("pool", "tensor"),
            P("pool", None, "tensor", None),
            P("pool", None, "tensor", None),
            P(),
            P(),
            P(),
        ),
        out_specs=P(None, "pool", "tensor"),
        check_vma=False,
    )
```

profile of v0, /device:TPU:0, one launch (start us, length us, event | category | flops | bytes accessed | tf_op | source)
XLA Modules:
  0.0 199.1 jit_solution(11783686460951820148)
XLA Ops:
  0.0 2.4 %fusion.123 = (bf16[1,1,32,28672]{3,2,1,0:T(8,128)(2,1)S(1)}, bf16[1,1,32,28672]{3,2,1,0:T(8,128)(2,1)S(1)}) fusion(bf16[1,2,32,28672]{3,2,1,0:T(8,128)(2,1)} %param.12), kind=kLoop, calls=%fused_computation.204 | loop fusion | bytes 7340032 | tf_op jit(solution)/shard_map/slice | solution.py:84
  4.4 7.4 %all-to-all-start = ((bf16[32,32,896]{2,1,0:T(8,128)(2,1)}), bf16[32,32,896]{2,1,0:T(8,128)(2,1)}, u32[]{:S(2)}, u32[]{:S(2)}) async-start(bf16[32,32,896]{2,1,0:T(8,128)(2,1)} %copy.49), calls=%async_computation | async-start | bytes 3670016 | tf_op jit(solution)/shard_map/all_to_all | solution.py:90
  12.8 3.7 %fusion.16 = f32[2,256,2,64]{1,3,2,0:T(8,128)S(1)} fusion(bf16[2,256,4096]{2,1,0:T(8,128)(2,1)} %param.8, bf16[1,2,4096,64]{2,3,1,0:T(8,128)(2,1)S(1)} %copy-done, f32[2,256]{1,0:T(2,128)S(1)} %bitcast.172), kind=kOutput, calls=%fused_computation.22 | convolution fusion | flops 536936448 | bytes 5507072 | tf_op jit(solution)/shard_map/snd,kdc->snkc/dot_general | solution.py:94
  21.2 20.4 %copy.85 = bf16[4096,2,1792]{2,0,1:T(8,128)(2,1)} copy(bf16[4096,2,1792]{2,1,0:T(2,128)(2,1)} %param.9) | data formatting | bytes 58720256 | tf_op jit(solution)/shard_map/optimization_barrier | solution.py:55
  43.2 5.0 %collective-permute-done.2 = f32[256,128]{0,1:T(8,128)S(1)} collective-permute-done((f32[256,128]{0,1:T(8,128)S(1)}, f32[256,128]{0,1:T(8,128)S(1)}, u32[]{:S(2)}, u32[]{:S(2)}) %collective-permute-start.2) | collective-permute-done | bytes 131104 | tf_op jit(solution)/shard_map/ppermute | solution.py:24
  48.3 6.8 %all-to-all-done = bf16[32,32,896]{2,1,0:T(8,128)(2,1)} async-done(((bf16[32,32,896]{2,1,0:T(8,128)(2,1)}), bf16[32,32,896]{2,1,0:T(8,128)(2,1)}, u32[]{:S(2)}, u32[]{:S(2)}) %all-to-all-start) | async-done | bytes 1835040 | tf_op jit(solution)/shard_map/all_to_all | solution.py:90
  56.9 4.0 %all-to-all-start.1 = ((bf16[32,32,896]{2,1,0:T(8,128)(2,1)}), bf16[32,32,896]{2,1,0:T(8,128)(2,1)S(1)}, u32[]{:S(2)}, u32[]{:S(2)}) async-start(bf16[32,32,896]{2,1,0:T(8,128)(2,1)} %copy.50), calls=%async_computation.1 | async-start | bytes 3670016 | tf_op jit(solution)/shard_map/all_to_all | solution.py:90
  62.8 11.7 %fusion.2 = f32[512,1792]{1,0:T(8,128)S(1)} fusion(bf16[512,4096]{1,0:T(8,128)(2,1)} %bitcast.175, bf16[2,4096,1792]{2,1,0:T(8,128)(2,1)} %bitcast.155), kind=kOutput, calls=%fused_computation.4 | convolution fusion | flops 7516192768 | bytes 22544384 | tf_op jit(solution)/shard_map/dot_general | solution.py:122
  78.6 13.3 %fusion = f32[512,1792]{1,0:T(8,128)} fusion(bf16[512,4096]{1,0:T(8,128)(2,1)S(1)} %bitcast.176, bf16[2,4096,1792]{2,1,0:T(8,128)(2,1)} %bitcast.156), kind=kOutput, calls=%fused_computation.2 | convolution fusion | flops 7516192768 | bytes 22544384 | tf_op jit(solution)/shard_map/dot_general | solution.py:122
  92.0 2.7 %collective-permute-done.4 = f32[256,128]{0,1:T(8,128)S(1)} collective-permute-done((f32[256,128]{0,1:T(8,128)S(1)}, f32[256,128]{0,1:T(8,128)S(1)}, u32[]{:S(2)}, u32[]{:S(2)}) %collective-permute-start.4) | collective-permute-done | bytes 131104 | tf_op jit(solution)/shard_map/ppermute | solution.py:24
  94.7 4.0 %collective-permute-start.5 = (f32[256,128]{0,1:T(8,128)S(1)}, f32[256,128]{0,1:T(8,128)S(1)}, u32[]{:S(2)}, u32[]{:S(2)}) collective-permute-start(f32[256,128]{0,1:T(8,128)S(1)} %add.234), channel_id=1, source_target_pairs={{0,16},{2,18},{4,20},{6,22},{8,24},{10,26},{12,28},{14,30},{16,0},... | collective-permute-start | bytes 393224 | tf_op jit(solution)/shard_map/ppermute | solution.py:24
  98.6 8.8 %all-to-all-done.1 = bf16[32,32,896]{2,1,0:T(8,128)(2,1)S(1)} async-done(((bf16[32,32,896]{2,1,0:T(8,128)(2,1)}), bf16[32,32,896]{2,1,0:T(8,128)(2,1)S(1)}, u32[]{:S(2)}, u32[]{:S(2)}) %all-to-all-start.1) | async-done | bytes 1835040 | tf_op jit(solution)/shard_map/all_to_all | solution.py:90
  107.4 3.5 %slice_select_fusion.1 = f32[512,896]{1,0:T(8,128)} fusion(f32[512,1792]{1,0:T(8,128)} %fusion, pred[]{:T(512)S(6)} %eq.18), kind=kLoop, calls=%fused_computation.21 | loop fusion | flops 458752 | bytes 5505025 | tf_op jit(solution)/shard_map/jit(_where)/select_n | solution.py:130
  121.2 3.0 %select_add_fusion.1 = f32[512,896]{1,0:T(8,128)S(1)} fusion(f32[512,896]{1,0:T(8,128)} %collective-permute-done.3, f32[512,1792]{1,0:T(8,128)} %copy-done.4, pred[]{:T(512)S(6)} %eq.18), kind=kLoop, calls=%fused_computation.19 | loop fusion | flops 917504 | bytes 7340033 | tf_op jit(solution)/shard_map/add | solution.py:131
  125.3 2.6 %select_add_fusion = f32[512,896]{1,0:T(8,128)S(1)} fusion(f32[512,896]{1,0:T(8,128)} %collective-permute-done.7, f32[512,1792]{1,0:T(8,128)S(1)} %copy-done.3, pred[]{:T(512)S(6)} %eq.18), kind=kLoop, calls=%fused_computation.18 | loop fusion | flops 917504 | bytes 7340033 | tf_op jit(solution)/shard_map/add | solution.py:131
  130.6 2.1 %fusion.12 = f32[256,2048]{1,0:T(8,128)S(1)} fusion(bf16[1792,4096]{1,0:T(8,128)(2,1)S(1)} %bitcast.174, bf16[256,896]{1,0:T(8,128)(2,1)S(1)} %collective-permute-done.8, bf16[128,896]{1,0:T(8,128)(2,1)S(1)} %fusion.29, bf16[128,896]{1,0:T(8,128)(2,1)S(1)} %fusion.31, pred[]{:T(512)S(6)} %eq.16), kind=kOutput, calls=%fused_computation.14 | convolution fusion | flops 1885011968 | bytes 10354689 | tf_op jit(solution)/shard_map/dot_general | solution.py:168
  134.3 2.1 %fusion.8 = f32[256,2048]{1,0:T(8,128)S(1)} fusion(bf16[1792,4096]{1,0:T(8,128)(2,1)S(1)} %bitcast.174, bf16[256,896]{1,0:T(8,128)(2,1)S(1)} %collective-permute-done.8, bf16[128,896]{1,0:T(8,128)(2,1)S(1)} %fusion.29, bf16[128,896]{1,0:T(8,128)(2,1)S(1)} %fusion.31, pred[]{:T(512)S(6)} %eq.16), kind=kOutput, calls=%fused_computation.10 | convolution fusion | flops 1885011968 | bytes 10354689 | tf_op jit(solution)/shard_map/dot_general | solution.py:168
  142.4 4.4 %collective-permute-done.9 = bf16[2,2,2,16,2048]{4,3,0,1,2:T(8,128)(2,1)S(1)} collective-permute-done((bf16[2,2,2,16,2048]{4,3,0,1,2:T(8,128)(2,1)S(1)}, bf16[2,2,2,16,2048]{4,3,0,1,2:T(8,128)(2,1)S(1)}, u32[]{:S(2)}, u32[]{:S(2)}) %collective-permute-start.9) | collective-permute-done | bytes 524320 | tf_op jit(solution)/shard_map/ppermute | solution.py:24
  146.8 3.4 %collective-permute-done.12 = bf16[2,2,2,16,2048]{4,3,0,1,2:T(8,128)(2,1)S(1)} collective-permute-done((bf16[2,2,2,16,2048]{4,3,0,1,2:T(8,128)(2,1)S(1)}, bf16[2,2,2,16,2048]{4,3,0,1,2:T(8,128)(2,1)S(1)}, u32[]{:S(2)}, u32[]{:S(2)}) %collective-permute-start.12) | collective-permute-done | bytes 524320 | tf_op jit(solution)/shard_map/ppermute | solution.py:24
  154.8 13.9 %collective-permute-done.10 = bf16[2,2,16,2048]{3,2,0,1:T(8,128)(2,1)S(1)} collective-permute-done((bf16[2,2,16,2048]{3,2,0,1:T(8,128)(2,1)S(1)}, bf16[2,2,16,2048]{3,2,0,1:T(8,128)(2,1)S(1)}, u32[]{:S(2)}, u32[]{:S(2)}) %collective-permute-start.10) | collective-permute-done | bytes 262176 | tf_op jit(solution)/shard_map/ppermute | solution.py:24
  171.0 2.8 %collective-permute-done.11 = bf16[2,16,2048]{2,1,0:T(8,128)(2,1)S(1)} collective-permute-done((bf16[2,16,2048]{2,1,0:T(8,128)(2,1)S(1)}, bf16[2,16,2048]{2,1,0:T(8,128)(2,1)S(1)}, u32[]{:S(2)}, u32[]{:S(2)}) %collective-permute-start.11) | collective-permute-done | bytes 131104 | tf_op jit(solution)/shard_map/ppermute | solution.py:24
  186.3 2.8 %collective-permute-done.24 = bf16[2,16,2048]{2,1,0:T(8,128)(2,1)S(1)} collective-permute-done((bf16[2,16,2048]{2,1,0:T(8,128)(2,1)S(1)}, bf16[2,16,2048]{2,1,0:T(8,128)(2,1)S(1)}, u32[]{:S(2)}, u32[]{:S(2)}) %collective-permute-start.24) | collective-permute-done | bytes 131104 | tf_op jit(solution)/shard_map/ppermute | solution.py:24
  189.1 3.1 %collective-permute-start.25 = (bf16[16,2048]{1,0:T(8,128)(2,1)S(1)}, bf16[16,2048]{1,0:T(8,128)(2,1)S(1)}, u32[]{:S(2)}, u32[]{:S(2)}) collective-permute-start(bf16[16,2048]{1,0:T(8,128)(2,1)S(1)} %fusion.90), channel_id=1, source_target_pairs={{0,16},{2,18},{4,20},{6,22},{8,24},{10,26},{12,28},{14,30},{16,0},... | collective-permute-start | bytes 196616 | tf_op jit(solution)/shard_map/ppermute | solution.py:24
  194.5 3.7 %collective-permute-done.22 = bf16[16,2048]{1,0:T(8,128)(2,1)S(1)} collective-permute-done((bf16[16,2048]{1,0:T(8,128)(2,1)S(1)}, bf16[16,2048]{1,0:T(8,128)(2,1)S(1)}, u32[]{:S(2)}, u32[]{:S(2)}) %collective-permute-start.22) | collective-permute-done | bytes 65568 | tf_op jit(solution)/shard_map/ppermute | solution.py:24
  (145 shorter events, 53.1 us)
Async XLA Ops:
  4.4 50.7 %all-to-all-start = ((bf16[32,32,896]{2,1,0:T(8,128)(2,1)}), bf16[32,32,896]{2,1,0:T(8,128)(2,1)}, u32[]{:S(2)}, u32[]{:S(2)}) async-start(bf16[32,32,896]{2,1,0:T(8,128)(2,1)} %copy.49), calls=%async_computation | async-start | bytes 3670016 | tf_op jit(solution)/shard_map/all_to_all | solution.py:90
  18.0 23.7 %collective-permute-start.1 = (f32[256,128]{0,1:T(8,128)S(1)}, f32[256,128]{0,1:T(8,128)S(1)}, u32[]{:S(2)}, u32[]{:S(2)}) collective-permute-start(f32[256,128]{0,1:T(8,128)S(1)} %bitcast_add_fusion.16), channel_id=1, source_target_pairs={{0,2},{2,0},{4,6},{6,4},{8,10},{10,8},{12,14},{14,12},{16,18},{18,... | collective-permute-start | bytes 393224 | tf_op jit(solution)/shard_map/ppermute | solution.py:24
  41.7 6.6 %collective-permute-start.2 = (f32[256,128]{0,1:T(8,128)S(1)}, f32[256,128]{0,1:T(8,128)S(1)}, u32[]{:S(2)}, u32[]{:S(2)}) collective-permute-start(f32[256,128]{0,1:T(8,128)S(1)} %add.231), channel_id=1, source_target_pairs={{0,4},{2,6},{4,0},{6,2},{8,12},{10,14},{12,8},{14,10},{16,20},{18,... | collective-permute-start | bytes 393224 | tf_op jit(solution)/shard_map/ppermute | solution.py:24
  56.9 50.5 %all-to-all-start.1 = ((bf16[32,32,896]{2,1,0:T(8,128)(2,1)}), bf16[32,32,896]{2,1,0:T(8,128)(2,1)S(1)}, u32[]{:S(2)}, u32[]{:S(2)}) async-start(bf16[32,32,896]{2,1,0:T(8,128)(2,1)} %copy.50), calls=%async_computation.1 | async-start | bytes 3670016 | tf_op jit(solution)/shard_map/all_to_all | solution.py:90
  60.9 33.7 %collective-permute-start.4 = (f32[256,128]{0,1:T(8,128)S(1)}, f32[256,128]{0,1:T(8,128)S(1)}, u32[]{:S(2)}, u32[]{:S(2)}) collective-permute-start(f32[256,128]{0,1:T(8,128)S(1)} %add.232), channel_id=1, source_target_pairs={{0,8},{2,10},{4,12},{6,14},{8,0},{10,2},{12,4},{14,6},{16,24},{18,... | collective-permute-start | bytes 393224 | tf_op jit(solution)/shard_map/ppermute | solution.py:24
  77.2 43.9 %collective-permute-start.3 = (f32[512,896]{1,0:T(8,128)}, f32[512,896]{1,0:T(8,128)}, u32[]{:S(2)}, u32[]{:S(2)}) collective-permute-start(f32[512,896]{1,0:T(8,128)} %slice_select_fusion), channel_id=1, source_target_pairs={{0,1},{1,0},{2,3},{3,2},{4,5},{5,4},{6,7},{7,6},{8,9},{9,8},{10,11... | collective-permute-start | bytes 5505032 | tf_op jit(solution)/shard_map/ppermute | solution.py:24
  94.7 16.3 %collective-permute-start.5 = (f32[256,128]{0,1:T(8,128)S(1)}, f32[256,128]{0,1:T(8,128)S(1)}, u32[]{:S(2)}, u32[]{:S(2)}) collective-permute-start(f32[256,128]{0,1:T(8,128)S(1)} %add.234), channel_id=1, source_target_pairs={{0,16},{2,18},{4,20},{6,22},{8,24},{10,26},{12,28},{14,30},{16,0},... | collective-permute-start | bytes 393224 | tf_op jit(solution)/shard_map/ppermute | solution.py:24
  110.9 14.4 %collective-permute-start.7 = (f32[512,896]{1,0:T(8,128)}, f32[512,896]{1,0:T(8,128)}, u32[]{:S(2)}, u32[]{:S(2)}) collective-permute-start(f32[512,896]{1,0:T(8,128)} %slice_select_fusion.1), channel_id=1, source_target_pairs={{0,1},{1,0},{2,3},{3,2},{4,5},{5,4},{6,7},{7,6},{8,9},{9,8},{10,11... | collective-permute-start | bytes 5505032 | tf_op jit(solution)/shard_map/ppermute | solution.py:24
  111.0 9.9 %collective-permute-start.6 = (f32[256,128]{0,1:T(8,128)S(1)}, f32[256,128]{0,1:T(8,128)S(1)}, u32[]{:S(2)}, u32[]{:S(2)}) collective-permute-start(f32[256,128]{0,1:T(8,128)S(1)} %add.235), channel_id=1, source_target_pairs={{0,1},{1,0},{2,3},{3,2},{4,5},{5,4},{6,7},{7,6},{8,9},{9,8},{10,11... | collective-permute-start | bytes 393224 | tf_op jit(solution)/shard_map/ppermute | solution.py:24
  129.5 8.6 %collective-permute-start.15 = (bf16[256,896]{1,0:T(8,128)(2,1)S(1)}, bf16[256,896]{1,0:T(8,128)(2,1)S(1)}, u32[]{:S(2)}, u32[]{:S(2)}) collective-permute-start(bf16[256,896]{1,0:T(8,128)(2,1)S(1)} %pad_maximum_fusion.1), channel_id=1, source_target_pairs={{0,1},{1,0},{2,3},{3,2},{4,5},{5,4},{6,7},{7,6},{8,9},{9,8},{10,11... | collective-permute-start | bytes 1376264 | tf_op jit(solution)/shard_map/ppermute | solution.py:24
  132.8 14.0 %collective-permute-start.9 = (bf16[2,2,2,16,2048]{4,3,0,1,2:T(8,128)(2,1)S(1)}, bf16[2,2,2,16,2048]{4,3,0,1,2:T(8,128)(2,1)S(1)}, u32[]{:S(2)}, u32[]{:S(2)}) collective-permute-start(bf16[2,2,2,16,2048]{4,3,0,1,2:T(8,128)(2,1)S(1)} %fusion.20), channel_id=1, source_target_pairs={{0,2},{2,0},{4,6},{6,4},{8,10},{10,8},{12,14},{14,12},{16,18},{18,... | collective-permute-start | bytes 1572872 | tf_op jit(solution)/shard_map/ppermute | solution.py:24
  136.5 13.7 %collective-permute-start.12 = (bf16[2,2,2,16,2048]{4,3,0,1,2:T(8,128)(2,1)S(1)}, bf16[2,2,2,16,2048]{4,3,0,1,2:T(8,128)(2,1)S(1)}, u32[]{:S(2)}, u32[]{:S(2)}) collective-permute-start(bf16[2,2,2,16,2048]{4,3,0,1,2:T(8,128)(2,1)S(1)} %fusion.21), channel_id=1, source_target_pairs={{0,4},{2,6},{4,0},{6,2},{8,12},{10,14},{12,8},{14,10},{16,20},{18,... | collective-permute-start | bytes 1572872 | tf_op jit(solution)/shard_map/ppermute | solution.py:24
  150.2 25.0 %collective-permute-start.17 = (bf16[2,2,2,16,2048]{4,3,0,1,2:T(8,128)(2,1)S(1)}, bf16[2,2,2,16,2048]{4,3,0,1,2:T(8,128)(2,1)S(1)}, u32[]{:S(2)}, u32[]{:S(2)}) collective-permute-start(bf16[2,2,2,16,2048]{4,3,0,1,2:T(8,128)(2,1)S(1)} %fusion.23), channel_id=1, source_target_pairs={{0,4},{2,6},{4,0},{6,2},{8,12},{10,14},{12,8},{14,10},{16,20},{18,... | collective-permute-start | bytes 1572872 | tf_op jit(solution)/shard_map/ppermute | solution.py:24
  151.7 23.7 %collective-permute-start.16 = (bf16[2,2,2,16,2048]{4,3,0,1,2:T(8,128)(2,1)S(1)}, bf16[2,2,2,16,2048]{4,3,0,1,2:T(8,128)(2,1)S(1)}, u32[]{:S(2)}, u32[]{:S(2)}) collective-permute-start(bf16[2,2,2,16,2048]{4,3,0,1,2:T(8,128)(2,1)S(1)} %fusion.22), channel_id=1, source_target_pairs={{0,2},{2,0},{4,6},{6,4},{8,10},{10,8},{12,14},{14,12},{16,18},{18,... | collective-permute-start | bytes 1572872 | tf_op jit(solution)/shard_map/ppermute | solution.py:24
  152.4 16.3 %collective-permute-start.10 = (bf16[2,2,16,2048]{3,2,0,1:T(8,128)(2,1)S(1)}, bf16[2,2,16,2048]{3,2,0,1:T(8,128)(2,1)S(1)}, u32[]{:S(2)}, u32[]{:S(2)}) collective-permute-start(bf16[2,2,16,2048]{3,2,0,1:T(8,128)(2,1)S(1)} %fusion.32), channel_id=1, source_target_pairs={{0,4},{2,6},{4,0},{6,2},{8,12},{10,14},{12,8},{14,10},{16,20},{18,... | collective-permute-start | bytes 786440 | tf_op jit(solution)/shard_map/ppermute | solution.py:24
  153.3 16.6 %collective-permute-start.13 = (bf16[2,2,16,2048]{3,2,0,1:T(8,128)(2,1)S(1)}, bf16[2,2,16,2048]{3,2,0,1:T(8,128)(2,1)S(1)}, u32[]{:S(2)}, u32[]{:S(2)}) collective-permute-start(bf16[2,2,16,2048]{3,2,0,1:T(8,128)(2,1)S(1)} %fusion.33), channel_id=1, source_target_pairs={{0,2},{2,0},{4,6},{6,4},{8,10},{10,8},{12,14},{14,12},{16,18},{18,... | collective-permute-start | bytes 786440 | tf_op jit(solution)/shard_map/ppermute | solution.py:24
  170.0 5.2 %collective-permute-start.14 = (bf16[2,16,2048]{2,1,0:T(8,128)(2,1)S(1)}, bf16[2,16,2048]{2,1,0:T(8,128)(2,1)S(1)}, u32[]{:S(2)}, u32[]{:S(2)}) collective-permute-start(bf16[2,16,2048]{2,1,0:T(8,128)(2,1)S(1)} %fusion.80), channel_id=1, source_target_pairs={{0,8},{2,10},{4,12},{6,14},{8,0},{10,2},{12,4},{14,6},{16,24},{18,... | collective-permute-start | bytes 393224 | tf_op jit(solution)/shard_map/ppermute | solution.py:24
  175.6 6.3 %collective-permute-start.19 = (bf16[16,2048]{1,0:T(8,128)(2,1)S(1)}, bf16[16,2048]{1,0:T(8,128)(2,1)S(1)}, u32[]{:S(2)}, u32[]{:S(2)}) collective-permute-start(bf16[16,2048]{1,0:T(8,128)(2,1)S(1)} %fusion.88), channel_id=1, source_target_pairs={{0,16},{2,18},{4,20},{6,22},{8,24},{10,26},{12,28},{14,30},{16,0},... | collective-permute-start | bytes 196616 | tf_op jit(solution)/shard_map/ppermute | solution.py:24
  176.5 7.4 %collective-permute-start.23 = (bf16[2,2,16,2048]{3,2,0,1:T(8,128)(2,1)S(1)}, bf16[2,2,16,2048]{3,2,0,1:T(8,128)(2,1)S(1)}, u32[]{:S(2)}, u32[]{:S(2)}) collective-permute-start(bf16[2,2,16,2048]{3,2,0,1:T(8,128)(2,1)S(1)} %fusion.35), channel_id=1, source_target_pairs={{0,2},{2,0},{4,6},{6,4},{8,10},{10,8},{12,14},{14,12},{16,18},{18,... | collective-permute-start | bytes 786440 | tf_op jit(solution)/shard_map/ppermute | solution.py:24
  177.6 8.0 %collective-permute-start.20 = (bf16[2,2,16,2048]{3,2,0,1:T(8,128)(2,1)S(1)}, bf16[2,2,16,2048]{3,2,0,1:T(8,128)(2,1)S(1)}, u32[]{:S(2)}, u32[]{:S(2)}) collective-permute-start(bf16[2,2,16,2048]{3,2,0,1:T(8,128)(2,1)S(1)} %fusion.34), channel_id=1, source_target_pairs={{0,4},{2,6},{4,0},{6,2},{8,12},{10,14},{12,8},{14,10},{16,20},{18,... | collective-permute-start | bytes 786440 | tf_op jit(solution)/shard_map/ppermute | solution.py:24
  178.6 5.2 %collective-permute-start.18 = (bf16[16,2048]{1,0:T(8,128)(2,1)S(1)}, bf16[16,2048]{1,0:T(8,128)(2,1)S(1)}, u32[]{:S(2)}, u32[]{:S(2)}) collective-permute-start(bf16[16,2048]{1,0:T(8,128)(2,1)S(1)} %fusion.87), channel_id=1, source_target_pairs={{0,16},{2,18},{4,20},{6,22},{8,24},{10,26},{12,28},{14,30},{16,0},... | collective-permute-start | bytes 196616 | tf_op jit(solution)/shard_map/ppermute | solution.py:24
  185.7 6.6 %collective-permute-start.21 = (bf16[2,16,2048]{2,1,0:T(8,128)(2,1)S(1)}, bf16[2,16,2048]{2,1,0:T(8,128)(2,1)S(1)}, u32[]{:S(2)}, u32[]{:S(2)}) collective-permute-start(bf16[2,16,2048]{2,1,0:T(8,128)(2,1)S(1)} %fusion.81), channel_id=1, source_target_pairs={{0,8},{2,10},{4,12},{6,14},{8,0},{10,2},{12,4},{14,6},{16,24},{18,... | collective-permute-start | bytes 393224 | tf_op jit(solution)/shard_map/ppermute | solution.py:24
  189.1 5.4 %collective-permute-start.25 = (bf16[16,2048]{1,0:T(8,128)(2,1)S(1)}, bf16[16,2048]{1,0:T(8,128)(2,1)S(1)}, u32[]{:S(2)}, u32[]{:S(2)}) collective-permute-start(bf16[16,2048]{1,0:T(8,128)(2,1)S(1)} %fusion.90), channel_id=1, source_target_pairs={{0,16},{2,18},{4,20},{6,22},{8,24},{10,26},{12,28},{14,30},{16,0},... | collective-permute-start | bytes 196616 | tf_op jit(solution)/shard_map/ppermute | solution.py:24
  192.3 5.9 %collective-permute-start.22 = (bf16[16,2048]{1,0:T(8,128)(2,1)S(1)}, bf16[16,2048]{1,0:T(8,128)(2,1)S(1)}, u32[]{:S(2)}, u32[]{:S(2)}) collective-permute-start(bf16[16,2048]{1,0:T(8,128)(2,1)S(1)} %fusion.89), channel_id=1, source_target_pairs={{0,16},{2,18},{4,20},{6,22},{8,24},{10,26},{12,28},{14,30},{16,0},... | collective-permute-start | bytes 196616 | tf_op jit(solution)/shard_map/ppermute | solution.py:24
  (17 other events, 145.0 us)
where the time goes:
time: 200 us; the launch traced here: 199 us
  waiting for transfers between devices  61.7 us (31%)
  starting transfers between devices  42.6 us (21%)
  matrix products  39.5 us (20%)
  local copies, waits for them, and re-layouts  34.2 us (17%)
  other arithmetic  12.7 us (6%)
  between operations  8.27 us (4%)
    ppermute x26, waiting for transfers between devices, swap(): return lax.ppermute(array, axis_name, bit_pairs(axis_name, bit))  46.1 us
    ppermute x26, starting transfers between devices, swap(): return lax.ppermute(array, axis_name, bit_pairs(axis_name, bit))  31.3 us
    dot_general x2, matrix products, shards(): jnp.dot(flat_tokens, weights[kind], preferred_element_type=jnp.float32)  25 us
    optimization_barrier x2, local copies, waits for them, and re-layouts, after(): return lax.optimization_barrier((array, arrived))[0]  22.2 us
    all_to_all x2, waiting for transfers between devices, shards(): lax.all_to_all(columns, ('pool', 'tensor'), split_axis=0, concat_axis=0,...  15.6 us
    all_to_all x2, starting transfers between devices, shards(): lax.all_to_all(columns, ('pool', 'tensor'), split_axis=0, concat_axis=0,...  11.4 us
    dot_general x4, matrix products, shards(): jnp.dot(hidden, down_weight[:, piece * half:(piece + 1) * half], preferre...  8.49 us
    add x2, other arithmetic, shards(): main.append(jnp.where(core == 0, low_share, high_share) + got)  5.65 us
  transfers between devices with their start and end apart: 28, of which 17 were waited for; matrix products, arithmetic and copies ran while one was open for 37% of the time, Pallas kernels for 0%

commit v1 on v0

--- a/solution.py
+++ b/solution.py
@@ -78,22 +78,14 @@
     rows_here = total_rows // pool_count
     slots = adapter_slot[block_adapter]
 
-    second = []
-    outgoing = []
-    for kind in range(kinds):
-        columns = expand_store[0, kind].reshape(ranks_local, pool_count * tensor_count, units_here)
-        columns = columns.transpose(1, 0, 2)
-        if second:
-            columns = after(columns, second[-1])
-        outgoing.append(columns)
-        second.append(
-            lax.all_to_all(columns, ("pool", "tensor"), split_axis=0, concat_axis=0, tiled=True)
-        )
-    pages = [one.reshape(pool_count, rank, units_here) for one in second]
+    outgoing = expand_store[0].reshape(kinds, ranks_local, pool_count * tensor_count, units_here)
+    outgoing = outgoing.transpose(2, 0, 1, 3)
+    second = lax.all_to_all(outgoing, ("pool", "tensor"), split_axis=0, concat_axis=0, tiled=True)
+    second = second.reshape(pool_count, tensor_count, kinds, ranks_local, units_here)
 
     first = jnp.einsum(
         "snd,kdc->snkc",
-        after(tokens, outgoing[0]),
+        after(tokens, outgoing),
         shrink_store[0],
         preferred_element_type=jnp.float32,
     )
@@ -112,17 +104,15 @@
 
     flat_tokens = tokens.reshape(steps * total_rows, width_local)
 
-    weights = after(gate_up_weight, outgoing[0])
+    weights = after(gate_up_weight, outgoing)
     weights = jnp.transpose(weights, (1, 0, 2))
-    weights, shrunk, flat_tokens, _ = lax.optimization_barrier(
-        (weights, shrunk, flat_tokens, second[0])
-    )
+    weights, shrunk, flat_tokens = lax.optimization_barrier((weights, shrunk, flat_tokens))
     shrunk = sum_over(shrunk, range(middle, bits_of("pool")))
     products = [
         jnp.dot(flat_tokens, weights[kind], preferred_element_type=jnp.float32)
         for kind in range(kinds)
     ]
-    products[-1] = after(products[-1], second[-1])
+    products = lax.optimization_barrier(products)
     main = []
     for product in products:
         if tensor_count == 2:
@@ -145,10 +135,8 @@
     for step in range(steps):
         hidden_blocks = []
         for block in range(NBLK):
-            page = [
-                lax.dynamic_index_in_dim(one, slots[step, block], 0, keepdims=False)
-                for one in pages
-            ]
+            page = lax.dynamic_index_in_dim(second, slots[step, block], 0, keepdims=False)
+            page = page.transpose(1, 0, 2, 3).reshape(kinds, rank, units_here)
             rows = slice(step * total_rows + block * BLK, step * total_rows + (block + 1) * BLK)
             gate, up = [
                 main[kind][rows]

time: 200 us -> 206 us (1.030)
  waiting for transfers between devices: 61.7 us -> 72.8 us
  starting transfers between devices: 42.6 us -> 37 us
  matrix products: 39.5 us -> 41.7 us
    ppermute x26, waiting for transfers between devices: 46.1 us -> 72.8 us  [swap(): return lax.ppermute(array, axis_name, bit_pairs(axis_name, bit))]
    all_to_all x2 -> x1, waiting for transfers between devices: 15.6 us -> 0.01 us  [shards(): lax.all_to_all(outgoing, ('pool', 'tensor'), split_axis=0, concat_axis=0,...]
    transpose x1 -> x3, local copies, waits for them, and re-layouts: 1.81 us -> 6.73 us  [the longest x2 5.23 us: shards(): outgoing = outgoing.transpose(2, 0, 1, 3)]
    all_to_all x2 -> x1, starting transfers between devices: 11.4 us -> 7.08 us  [shards(): lax.all_to_all(outgoing, ('pool', 'tensor'), split_axis=0, concat_axis=0,...]
    dot_general x4, matrix products: 8.49 us -> 11.8 us  [shards(): jnp.dot(hidden, down_weight[:, piece * half:(piece + 1) * half], preferre...]
    select_n x2, other arithmetic: 4.94 us -> 1.79 us  [shards(): got = swap(jnp.where(core == 0, high_share, low_share), 'tensor', 0)]
    slice x1 -> x2, local copies, waits for them, and re-layouts: 2.38 us -> 0.08 us  [shards(): page[kind]]
    optimization_barrier x2 -> x1, local copies, waits for them, and re-layouts: 22.2 us -> 20.3 us  [after(): return lax.optimization_barrier((array, arrived))[0]]
  transfers between devices with their start and end apart: 28 -> 27, of which waited for: 17 -> 17; matrix products, arithmetic and copies ran while one was open for 37% -> 35% of each run, Pallas kernels for 0% -> 0%
where the time goes in v1:
time: 206 us; the launch traced here: 205 us
  waiting for transfers between devices  72.8 us (35%)
  matrix products  41.7 us (20%)
  starting transfers between devices  37 us (18%)
  local copies, waits for them, and re-layouts  33.9 us (16%)
  other arithmetic  12.1 us (6%)
  between operations  8.1 us (4%)
    ppermute x26, waiting for transfers between devices, swap(): return lax.ppermute(array, axis_name, bit_pairs(axis_name, bit))  72.8 us
    ppermute x26, starting transfers between devices, swap(): return lax.ppermute(array, axis_name, bit_pairs(axis_name, bit))  29.9 us
    dot_general x2, matrix products, shards(): jnp.dot(flat_tokens, weights[kind], preferred_element_type=jnp.float32)  23.7 us
    optimization_barrier x1, local copies, waits for them, and re-layouts, after(): return lax.optimization_barrier((array, arrived))[0]  20.3 us
    dot_general x4, matrix products, shards(): jnp.dot(hidden, down_weight[:, piece * half:(piece + 1) * half], preferre...  11.8 us
    add x2, other arithmetic, shards(): main.append(jnp.where(core == 0, low_share, high_share) + got)  7.39 us
    all_to_all x1, starting transfers between devices, shards(): lax.all_to_all(outgoing, ('pool', 'tensor'), split_axis=0, concat_axis=0,...  7.08 us
    transpose x2, local copies, waits for them, and re-layouts, shards(): outgoing = outgoing.transpose(2, 0, 1, 3)  5.23 us
  transfers between devices with their start and end apart: 27, of which 17 were waited for; matrix products, arithmetic and copies ran while one was open for 35% of the time, Pallas kernels for 0%

profile of v1, /device:TPU:0, one launch (start us, length us, event | category | flops | bytes accessed | tf_op | source)
XLA Modules:
  0.0 205.4 jit_solution(13533281817358989255)
XLA Ops:
  2.3 2.6 %copy.70 = bf16[8,8,32,896]{3,2,1,0:T(8,128)(2,1)S(1)} copy(bf16[8,8,32,896]{3,1,2,0:T(8,128)(2,1)} %bitcast.162) | data formatting | bytes 7340032
  7.1 3.9 %fusion.16 = f32[2,256,2,64]{1,3,2,0:T(8,128)S(1)} fusion(bf16[2,256,4096]{2,1,0:T(8,128)(2,1)} %param.8, bf16[1,2,4096,64]{2,3,1,0:T(8,128)(2,1)S(1)} %copy-done, f32[2,256]{1,0:T(2,128)S(1)} %bitcast.181), kind=kOutput, calls=%fused_computation.23 | convolution fusion | flops 536936448 | bytes 5507072 | tf_op jit(solution)/shard_map/snd,kdc->snkc/dot_general | solution.py:86
  11.5 3.1 %copy.56 = bf16[32,2,32,896]{3,2,1,0:T(8,128)(2,1)} copy(bf16[32,2,32,896]{3,0,2,1:T(8,128)(2,1)S(1)} %copy-done.2) | data formatting | bytes 7340032 | tf_op jit(solution)/shard_map/transpose | solution.py:82
  14.6 7.1 %all-to-all-start = ((bf16[32,2,32,896]{3,2,1,0:T(8,128)(2,1)}), bf16[32,2,32,896]{3,2,1,0:T(8,128)(2,1)}, u32[]{:S(2)}, u32[]{:S(2)}) async-start(bf16[32,2,32,896]{3,2,1,0:T(8,128)(2,1)} %copy.56), calls=%async_computation | async-start | bytes 7340032 | tf_op jit(solution)/shard_map/all_to_all | solution.py:83
  23.5 26.7 %collective-permute-done.1 = f32[256,128]{0,1:T(8,128)S(1)} collective-permute-done((f32[256,128]{0,1:T(8,128)S(1)}, f32[256,128]{0,1:T(8,128)S(1)}, u32[]{:S(2)}, u32[]{:S(2)}) %collective-permute-start.1) | collective-permute-done | bytes 131104 | tf_op jit(solution)/shard_map/ppermute | solution.py:24
  50.3 20.3 %copy.90 = bf16[4096,2,1792]{2,0,1:T(8,128)(2,1)} copy(bf16[4096,2,1792]{2,1,0:T(2,128)(2,1)} %param.9) | data formatting | bytes 58720256 | tf_op jit(solution)/shard_map/optimization_barrier | solution.py:55
  70.7 11.8 %fusion = f32[512,1792]{1,0:T(8,128)S(1)} fusion(bf16[512,4096]{1,0:T(8,128)(2,1)} %bitcast.184, bf16[2,4096,1792]{2,1,0:T(8,128)(2,1)} %bitcast.159), kind=kOutput, calls=%fused_computation.2 | convolution fusion | flops 7516192768 | bytes 22544384 | tf_op jit(solution)/shard_map/dot_general | solution.py:112
  82.5 11.9 %fusion.2 = f32[512,1792]{1,0:T(8,128)S(1)} fusion(bf16[512,4096]{1,0:T(8,128)(2,1)S(1)} %bitcast.185, bf16[2,4096,1792]{2,1,0:T(8,128)(2,1)} %bitcast.160), kind=kOutput, calls=%fused_computation.4 | convolution fusion | flops 7516192768 | bytes 22544384 | tf_op jit(solution)/shard_map/dot_general | solution.py:112
  98.7 8.6 %collective-permute-done.4 = f32[256,128]{0,1:T(8,128)S(1)} collective-permute-done((f32[256,128]{0,1:T(8,128)S(1)}, f32[256,128]{0,1:T(8,128)S(1)}, u32[]{:S(2)}, u32[]{:S(2)}) %collective-permute-start.4) | collective-permute-done | bytes 131104 | tf_op jit(solution)/shard_map/ppermute | solution.py:24
  107.3 3.4 %collective-permute-start.5 = (f32[256,128]{0,1:T(8,128)S(1)}, f32[256,128]{0,1:T(8,128)S(1)}, u32[]{:S(2)}, u32[]{:S(2)}) collective-permute-start(f32[256,128]{0,1:T(8,128)S(1)} %add.230), channel_id=1, source_target_pairs={{0,16},{2,18},{4,20},{6,22},{8,24},{10,26},{12,28},{14,30},{16,0},... | collective-permute-start | bytes 393224 | tf_op jit(solution)/shard_map/ppermute | solution.py:24
  111.4 5.4 %collective-permute-done.5 = f32[256,128]{0,1:T(8,128)S(1)} collective-permute-done((f32[256,128]{0,1:T(8,128)S(1)}, f32[256,128]{0,1:T(8,128)S(1)}, u32[]{:S(2)}, u32[]{:S(2)}) %collective-permute-start.5) | collective-permute-done | bytes 131104 | tf_op jit(solution)/shard_map/ppermute | solution.py:24
  124.6 4.3 %select_add_fusion.1 = f32[512,896]{1,0:T(8,128)} fusion(f32[512,896]{1,0:T(8,128)} %collective-permute-done.3, f32[512,1792]{1,0:T(8,128)} %copy-done.5, pred[]{:T(512)S(6)} %eq.18), kind=kLoop, calls=%fused_computation.20 | loop fusion | flops 917504 | bytes 7340033 | tf_op jit(solution)/shard_map/add | solution.py:121
  128.9 3.1 %select_add_fusion = f32[512,896]{1,0:T(8,128)} fusion(f32[512,896]{1,0:T(8,128)} %collective-permute-done.7, f32[512,1792]{1,0:T(8,128)S(1)} %copy-done.4, pred[]{:T(512)S(6)} %eq.18), kind=kLoop, calls=%fused_computation.19 | loop fusion | flops 917504 | bytes 7340033 | tf_op jit(solution)/shard_map/add | solution.py:121
  137.1 5.5 %fusion.8 = f32[256,2048]{1,0:T(8,128)S(1)} fusion(bf16[1792,4096]{1,0:T(8,128)(2,1)} %param.10, bf16[256,896]{1,0:T(8,128)(2,1)S(1)} %collective-permute-done.8, bf16[128,896]{1,0:T(8,128)(2,1)S(1)} %fusion.29, bf16[128,896]{1,0:T(8,128)(2,1)S(1)} %fusion.31, pred[]{:T(512)S(6)} %eq.16), kind=kOutput, calls=%fused_computation.10 | convolution fusion | flops 1885011968 | bytes 10354689 | tf_op jit(solution)/shard_map/dot_general | solution.py:156
  145.0 2.1 %collective-permute-start.9 = (bf16[2,2,2,16,2048]{4,3,0,1,2:T(8,128)(2,1)S(1)}, bf16[2,2,2,16,2048]{4,3,0,1,2:T(8,128)(2,1)S(1)}, u32[]{:S(2)}, u32[]{:S(2)}) collective-permute-start(bf16[2,2,2,16,2048]{4,3,0,1,2:T(8,128)(2,1)S(1)} %fusion.20), channel_id=1, source_target_pairs={{0,2},{2,0},{4,6},{6,4},{8,10},{10,8},{12,14},{14,12},{16,18},{18,... | collective-permute-start | bytes 1572872 | tf_op jit(solution)/shard_map/ppermute | solution.py:24
  151.5 5.9 %collective-permute-done.12 = bf16[2,2,2,16,2048]{4,3,0,1,2:T(8,128)(2,1)S(1)} collective-permute-done((bf16[2,2,2,16,2048]{4,3,0,1,2:T(8,128)(2,1)S(1)}, bf16[2,2,2,16,2048]{4,3,0,1,2:T(8,128)(2,1)S(1)}, u32[]{:S(2)}, u32[]{:S(2)}) %collective-permute-start.12) | collective-permute-done | bytes 524320 | tf_op jit(solution)/shard_map/ppermute | solution.py:24
  164.1 2.8 %collective-permute-done.13 = bf16[2,2,16,2048]{3,2,0,1:T(8,128)(2,1)S(1)} collective-permute-done((bf16[2,2,16,2048]{3,2,0,1:T(8,128)(2,1)S(1)}, bf16[2,2,16,2048]{3,2,0,1:T(8,128)(2,1)S(1)}, u32[]{:S(2)}, u32[]{:S(2)}) %collective-permute-start.13) | collective-permute-done | bytes 262176 | tf_op jit(solution)/shard_map/ppermute | solution.py:24
  170.1 3.2 %collective-permute-done.14 = bf16[2,16,2048]{2,1,0:T(8,128)(2,1)S(1)} collective-permute-done((bf16[2,16,2048]{2,1,0:T(8,128)(2,1)S(1)}, bf16[2,16,2048]{2,1,0:T(8,128)(2,1)S(1)}, u32[]{:S(2)}, u32[]{:S(2)}) %collective-permute-start.14) | collective-permute-done | bytes 131104 | tf_op jit(solution)/shard_map/ppermute | solution.py:24
  174.7 2.7 %collective-permute-done.16 = bf16[2,2,2,16,2048]{4,3,0,1,2:T(8,128)(2,1)S(1)} collective-permute-done((bf16[2,2,2,16,2048]{4,3,0,1,2:T(8,128)(2,1)S(1)}, bf16[2,2,2,16,2048]{4,3,0,1,2:T(8,128)(2,1)S(1)}, u32[]{:S(2)}, u32[]{:S(2)}) %collective-permute-start.16) | collective-permute-done | bytes 524320 | tf_op jit(solution)/shard_map/ppermute | solution.py:24
  183.3 2.9 %collective-permute-start.19 = (bf16[16,2048]{1,0:T(8,128)(2,1)S(1)}, bf16[16,2048]{1,0:T(8,128)(2,1)S(1)}, u32[]{:S(2)}, u32[]{:S(2)}) collective-permute-start(bf16[16,2048]{1,0:T(8,128)(2,1)S(1)} %fusion.88), channel_id=1, source_target_pairs={{0,16},{2,18},{4,20},{6,22},{8,24},{10,26},{12,28},{14,30},{16,0},... | collective-permute-start | bytes 196616 | tf_op jit(solution)/shard_map/ppermute | solution.py:24
  186.2 2.9 %collective-permute-done.19 = bf16[16,2048]{1,0:T(8,128)(2,1)S(1)} collective-permute-done((bf16[16,2048]{1,0:T(8,128)(2,1)S(1)}, bf16[16,2048]{1,0:T(8,128)(2,1)S(1)}, u32[]{:S(2)}, u32[]{:S(2)}) %collective-permute-start.19) | collective-permute-done | bytes 65568 | tf_op jit(solution)/shard_map/ppermute | solution.py:24
  189.4 4.1 %collective-permute-start.21 = (bf16[2,16,2048]{2,1,0:T(8,128)(2,1)S(1)}, bf16[2,16,2048]{2,1,0:T(8,128)(2,1)S(1)}, u32[]{:S(2)}, u32[]{:S(2)}) collective-permute-start(bf16[2,16,2048]{2,1,0:T(8,128)(2,1)S(1)} %fusion.81), channel_id=1, source_target_pairs={{0,8},{2,10},{4,12},{6,14},{8,0},{10,2},{12,4},{14,6},{16,24},{18,... | collective-permute-start | bytes 393224 | tf_op jit(solution)/shard_map/ppermute | solution.py:24
  193.7 3.8 %collective-permute-done.21 = bf16[2,16,2048]{2,1,0:T(8,128)(2,1)S(1)} collective-permute-done((bf16[2,16,2048]{2,1,0:T(8,128)(2,1)S(1)}, bf16[2,16,2048]{2,1,0:T(8,128)(2,1)S(1)}, u32[]{:S(2)}, u32[]{:S(2)}) %collective-permute-start.21) | collective-permute-done | bytes 131104 | tf_op jit(solution)/shard_map/ppermute | solution.py:24
  200.6 2.1 %collective-permute-done.22 = bf16[16,2048]{1,0:T(8,128)(2,1)S(1)} collective-permute-done((bf16[16,2048]{1,0:T(8,128)(2,1)S(1)}, bf16[16,2048]{1,0:T(8,128)(2,1)S(1)}, u32[]{:S(2)}, u32[]{:S(2)}) %collective-permute-start.22) | collective-permute-done | bytes 65568 | tf_op jit(solution)/shard_map/ppermute | solution.py:24
  (144 shorter events, 47.2 us)
Async XLA Ops:
  11.0 10.7 %collective-permute-start = (f32[256,128]{0,1:T(8,128)S(1)}, f32[256,128]{0,1:T(8,128)S(1)}, u32[]{:S(2)}, u32[]{:S(2)}) collective-permute-start(f32[256,128]{0,1:T(8,128)S(1)} %dynamic-slice_bitcast_fusion.4), channel_id=1, source_target_pairs={{0,1},{1,0},{2,3},{3,2},{4,5},{5,4},{6,7},{7,6},{8,9},{9,8},{10,11... | collective-permute-start | bytes 393224 | tf_op jit(solution)/shard_map/ppermute | solution.py:24
  14.6 117.3 %all-to-all-start = ((bf16[32,2,32,896]{3,2,1,0:T(8,128)(2,1)}), bf16[32,2,32,896]{3,2,1,0:T(8,128)(2,1)}, u32[]{:S(2)}, u32[]{:S(2)}) async-start(bf16[32,2,32,896]{3,2,1,0:T(8,128)(2,1)} %copy.56), calls=%async_computation | async-start | bytes 7340032 | tf_op jit(solution)/shard_map/all_to_all | solution.py:83
  21.7 28.5 %collective-permute-start.1 = (f32[256,128]{0,1:T(8,128)S(1)}, f32[256,128]{0,1:T(8,128)S(1)}, u32[]{:S(2)}, u32[]{:S(2)}) collective-permute-start(f32[256,128]{0,1:T(8,128)S(1)} %bitcast_add_fusion.16), channel_id=1, source_target_pairs={{0,2},{2,0},{4,6},{6,4},{8,10},{10,8},{12,14},{14,12},{16,18},{18,... | collective-permute-start | bytes 393224 | tf_op jit(solution)/shard_map/ppermute | solution.py:24
  50.3 20.4 %collective-permute-start.2 = (f32[256,128]{0,1:T(8,128)S(1)}, f32[256,128]{0,1:T(8,128)S(1)}, u32[]{:S(2)}, u32[]{:S(2)}) collective-permute-start(f32[256,128]{0,1:T(8,128)S(1)} %add.227), channel_id=1, source_target_pairs={{0,4},{2,6},{4,0},{6,2},{8,12},{10,14},{12,8},{14,10},{16,20},{18,... | collective-permute-start | bytes 393224 | tf_op jit(solution)/shard_map/ppermute | solution.py:24
  96.9 27.7 %collective-permute-start.3 = (f32[512,896]{1,0:T(8,128)}, f32[512,896]{1,0:T(8,128)}, u32[]{:S(2)}, u32[]{:S(2)}) collective-permute-start(f32[512,896]{1,0:T(8,128)} %slice_select_fusion.1), channel_id=1, source_target_pairs={{0,1},{1,0},{2,3},{3,2},{4,5},{5,4},{6,7},{7,6},{8,9},{9,8},{10,11... | collective-permute-start | bytes 5505032 | tf_op jit(solution)/shard_map/ppermute | solution.py:24
  97.1 31.8 %collective-permute-start.7 = (f32[512,896]{1,0:T(8,128)S(1)}, f32[512,896]{1,0:T(8,128)}, u32[]{:S(2)}, u32[]{:S(2)}) collective-permute-start(f32[512,896]{1,0:T(8,128)S(1)} %slice_select_fusion), channel_id=1, source_target_pairs={{0,1},{1,0},{2,3},{3,2},{4,5},{5,4},{6,7},{7,6},{8,9},{9,8},{10,11... | collective-permute-start | bytes 5505032 | tf_op jit(solution)/shard_map/ppermute | solution.py:24
  97.7 9.6 %collective-permute-start.4 = (f32[256,128]{0,1:T(8,128)S(1)}, f32[256,128]{0,1:T(8,128)S(1)}, u32[]{:S(2)}, u32[]{:S(2)}) collective-permute-start(f32[256,128]{0,1:T(8,128)S(1)} %add.228), channel_id=1, source_target_pairs={{0,8},{2,10},{4,12},{6,14},{8,0},{10,2},{12,4},{14,6},{16,24},{18,... | collective-permute-start | bytes 393224 | tf_op jit(solution)/shard_map/ppermute | solution.py:24
  107.3 9.5 %collective-permute-start.5 = (f32[256,128]{0,1:T(8,128)S(1)}, f32[256,128]{0,1:T(8,128)S(1)}, u32[]{:S(2)}, u32[]{:S(2)}) collective-permute-start(f32[256,128]{0,1:T(8,128)S(1)} %add.230), channel_id=1, source_target_pairs={{0,16},{2,18},{4,20},{6,22},{8,24},{10,26},{12,28},{14,30},{16,0},... | collective-permute-start | bytes 393224 | tf_op jit(solution)/shard_map/ppermute | solution.py:24
  116.8 7.6 %collective-permute-start.6 = (f32[256,128]{0,1:T(8,128)S(1)}, f32[256,128]{0,1:T(8,128)S(1)}, u32[]{:S(2)}, u32[]{:S(2)}) collective-permute-start(f32[256,128]{0,1:T(8,128)S(1)} %add.231), channel_id=1, source_target_pairs={{0,1},{1,0},{2,3},{3,2},{4,5},{5,4},{6,7},{7,6},{8,9},{9,8},{10,11... | collective-permute-start | bytes 393224 | tf_op jit(solution)/shard_map/ppermute | solution.py:24
  137.0 10.2 %collective-permute-start.15 = (bf16[256,896]{1,0:T(8,128)(2,1)S(1)}, bf16[256,896]{1,0:T(8,128)(2,1)S(1)}, u32[]{:S(2)}, u32[]{:S(2)}) collective-permute-start(bf16[256,896]{1,0:T(8,128)(2,1)S(1)} %pad_maximum_fusion.1), channel_id=1, source_target_pairs={{0,1},{1,0},{2,3},{3,2},{4,5},{5,4},{6,7},{7,6},{8,9},{9,8},{10,11... | collective-permute-start | bytes 1376264 | tf_op jit(solution)/shard_map/ppermute | solution.py:24
  142.7 14.8 %collective-permute-start.12 = (bf16[2,2,2,16,2048]{4,3,0,1,2:T(8,128)(2,1)S(1)}, bf16[2,2,2,16,2048]{4,3,0,1,2:T(8,128)(2,1)S(1)}, u32[]{:S(2)}, u32[]{:S(2)}) collective-permute-start(bf16[2,2,2,16,2048]{4,3,0,1,2:T(8,128)(2,1)S(1)} %fusion.21), channel_id=1, source_target_pairs={{0,4},{2,6},{4,0},{6,2},{8,12},{10,14},{12,8},{14,10},{16,20},{18,... | collective-permute-start | bytes 1572872 | tf_op jit(solution)/shard_map/ppermute | solution.py:24
  145.0 14.8 %collective-permute-start.9 = (bf16[2,2,2,16,2048]{4,3,0,1,2:T(8,128)(2,1)S(1)}, bf16[2,2,2,16,2048]{4,3,0,1,2:T(8,128)(2,1)S(1)}, u32[]{:S(2)}, u32[]{:S(2)}) collective-permute-start(bf16[2,2,2,16,2048]{4,3,0,1,2:T(8,128)(2,1)S(1)} %fusion.20), channel_id=1, source_target_pairs={{0,2},{2,0},{4,6},{6,4},{8,10},{10,8},{12,14},{14,12},{16,18},{18,... | collective-permute-start | bytes 1572872 | tf_op jit(solution)/shard_map/ppermute | solution.py:24
  157.7 9.2 %collective-permute-start.13 = (bf16[2,2,16,2048]{3,2,0,1:T(8,128)(2,1)S(1)}, bf16[2,2,16,2048]{3,2,0,1:T(8,128)(2,1)S(1)}, u32[]{:S(2)}, u32[]{:S(2)}) collective-permute-start(bf16[2,2,16,2048]{3,2,0,1:T(8,128)(2,1)S(1)} %fusion.33), channel_id=1, source_target_pairs={{0,2},{2,0},{4,6},{6,4},{8,10},{10,8},{12,14},{14,12},{16,18},{18,... | collective-permute-start | bytes 786440 | tf_op jit(solution)/shard_map/ppermute | solution.py:24
  160.0 9.2 %collective-permute-start.10 = (bf16[2,2,16,2048]{3,2,0,1:T(8,128)(2,1)S(1)}, bf16[2,2,16,2048]{3,2,0,1:T(8,128)(2,1)S(1)}, u32[]{:S(2)}, u32[]{:S(2)}) collective-permute-start(bf16[2,2,16,2048]{3,2,0,1:T(8,128)(2,1)S(1)} %fusion.32), channel_id=1, source_target_pairs={{0,4},{2,6},{4,0},{6,2},{8,12},{10,14},{12,8},{14,10},{16,20},{18,... | collective-permute-start | bytes 786440 | tf_op jit(solution)/shard_map/ppermute | solution.py:24
  162.1 15.3 %collective-permute-start.16 = (bf16[2,2,2,16,2048]{4,3,0,1,2:T(8,128)(2,1)S(1)}, bf16[2,2,2,16,2048]{4,3,0,1,2:T(8,128)(2,1)S(1)}, u32[]{:S(2)}, u32[]{:S(2)}) collective-permute-start(bf16[2,2,2,16,2048]{4,3,0,1,2:T(8,128)(2,1)S(1)} %fusion.22), channel_id=1, source_target_pairs={{0,2},{2,0},{4,6},{6,4},{8,10},{10,8},{12,14},{14,12},{16,18},{18,... | collective-permute-start | bytes 1572872 | tf_op jit(solution)/shard_map/ppermute | solution.py:24
  164.0 15.7 %collective-permute-start.17 = (bf16[2,2,2,16,2048]{4,3,0,1,2:T(8,128)(2,1)S(1)}, bf16[2,2,2,16,2048]{4,3,0,1,2:T(8,128)(2,1)S(1)}, u32[]{:S(2)}, u32[]{:S(2)}) collective-permute-start(bf16[2,2,2,16,2048]{4,3,0,1,2:T(8,128)(2,1)S(1)} %fusion.23), channel_id=1, source_target_pairs={{0,4},{2,6},{4,0},{6,2},{8,12},{10,14},{12,8},{14,10},{16,20},{18,... | collective-permute-start | bytes 1572872 | tf_op jit(solution)/shard_map/ppermute | solution.py:24
  166.9 6.3 %collective-permute-start.14 = (bf16[2,16,2048]{2,1,0:T(8,128)(2,1)S(1)}, bf16[2,16,2048]{2,1,0:T(8,128)(2,1)S(1)}, u32[]{:S(2)}, u32[]{:S(2)}) collective-permute-start(bf16[2,16,2048]{2,1,0:T(8,128)(2,1)S(1)} %fusion.80), channel_id=1, source_target_pairs={{0,8},{2,10},{4,12},{6,14},{8,0},{10,2},{12,4},{14,6},{16,24},{18,... | collective-permute-start | bytes 393224 | tf_op jit(solution)/shard_map/ppermute | solution.py:24
  169.3 5.3 %collective-permute-start.11 = (bf16[2,16,2048]{2,1,0:T(8,128)(2,1)S(1)}, bf16[2,16,2048]{2,1,0:T(8,128)(2,1)S(1)}, u32[]{:S(2)}, u32[]{:S(2)}) collective-permute-start(bf16[2,16,2048]{2,1,0:T(8,128)(2,1)S(1)} %fusion.79), channel_id=1, source_target_pairs={{0,8},{2,10},{4,12},{6,14},{8,0},{10,2},{12,4},{14,6},{16,24},{18,... | collective-permute-start | bytes 393224 | tf_op jit(solution)/shard_map/ppermute | solution.py:24
  179.8 6.4 %collective-permute-start.18 = (bf16[16,2048]{1,0:T(8,128)(2,1)S(1)}, bf16[16,2048]{1,0:T(8,128)(2,1)S(1)}, u32[]{:S(2)}, u32[]{:S(2)}) collective-permute-start(bf16[16,2048]{1,0:T(8,128)(2,1)S(1)} %fusion.87), channel_id=1, source_target_pairs={{0,16},{2,18},{4,20},{6,22},{8,24},{10,26},{12,28},{14,30},{16,0},... | collective-permute-start | bytes 196616 | tf_op jit(solution)/shard_map/ppermute | solution.py:24
  179.9 9.4 %collective-permute-start.20 = (bf16[2,2,16,2048]{3,2,0,1:T(8,128)(2,1)S(1)}, bf16[2,2,16,2048]{3,2,0,1:T(8,128)(2,1)S(1)}, u32[]{:S(2)}, u32[]{:S(2)}) collective-permute-start(bf16[2,2,16,2048]{3,2,0,1:T(8,128)(2,1)S(1)} %fusion.34), channel_id=1, source_target_pairs={{0,4},{2,6},{4,0},{6,2},{8,12},{10,14},{12,8},{14,10},{16,20},{18,... | collective-permute-start | bytes 786440 | tf_op jit(solution)/shard_map/ppermute | solution.py:24
  181.7 11.8 %collective-permute-start.23 = (bf16[2,2,16,2048]{3,2,0,1:T(8,128)(2,1)S(1)}, bf16[2,2,16,2048]{3,2,0,1:T(8,128)(2,1)S(1)}, u32[]{:S(2)}, u32[]{:S(2)}) collective-permute-start(bf16[2,2,16,2048]{3,2,0,1:T(8,128)(2,1)S(1)} %fusion.35), channel_id=1, source_target_pairs={{0,2},{2,0},{4,6},{6,4},{8,10},{10,8},{12,14},{14,12},{16,18},{18,... | collective-permute-start | bytes 786440 | tf_op jit(solution)/shard_map/ppermute | solution.py:24
  183.3 5.9 %collective-permute-start.19 = (bf16[16,2048]{1,0:T(8,128)(2,1)S(1)}, bf16[16,2048]{1,0:T(8,128)(2,1)S(1)}, u32[]{:S(2)}, u32[]{:S(2)}) collective-permute-start(bf16[16,2048]{1,0:T(8,128)(2,1)S(1)} %fusion.88), channel_id=1, source_target_pairs={{0,16},{2,18},{4,20},{6,22},{8,24},{10,26},{12,28},{14,30},{16,0},... | collective-permute-start | bytes 196616 | tf_op jit(solution)/shard_map/ppermute | solution.py:24
  189.4 8.0 %collective-permute-start.21 = (bf16[2,16,2048]{2,1,0:T(8,128)(2,1)S(1)}, bf16[2,16,2048]{2,1,0:T(8,128)(2,1)S(1)}, u32[]{:S(2)}, u32[]{:S(2)}) collective-permute-start(bf16[2,16,2048]{2,1,0:T(8,128)(2,1)S(1)} %fusion.81), channel_id=1, source_target_pairs={{0,8},{2,10},{4,12},{6,14},{8,0},{10,2},{12,4},{14,6},{16,24},{18,... | collective-permute-start | bytes 393224 | tf_op jit(solution)/shard_map/ppermute | solution.py:24
  193.6 5.7 %collective-permute-start.24 = (bf16[2,16,2048]{2,1,0:T(8,128)(2,1)S(1)}, bf16[2,16,2048]{2,1,0:T(8,128)(2,1)S(1)}, u32[]{:S(2)}, u32[]{:S(2)}) collective-permute-start(bf16[2,16,2048]{2,1,0:T(8,128)(2,1)S(1)} %fusion.82), channel_id=1, source_target_pairs={{0,8},{2,10},{4,12},{6,14},{8,0},{10,2},{12,4},{14,6},{16,24},{18,... | collective-permute-start | bytes 393224 | tf_op jit(solution)/shard_map/ppermute | solution.py:24
  (17 other events, 118.1 us)

commit v2 on v0

--- a/solution.py
+++ b/solution.py
@@ -122,7 +122,7 @@
         jnp.dot(flat_tokens, weights[kind], preferred_element_type=jnp.float32)
         for kind in range(kinds)
     ]
-    products[-1] = after(products[-1], second[-1])
+    products = lax.optimization_barrier(products)
     main = []
     for product in products:
         if tensor_count == 2:
@@ -199,7 +199,7 @@
             prepare(step, stage)
             if stage == 0 and step:
                 sends[step] = after(sends[step], arrived[step - 1])
-            if stage == bits - 1 and step == 0:
+            if stage == 2 and step == 0:
                 sends[step] = after(sends[step], later_sends)
             if stage == 1 and step == steps - 1:
                 later_sends = list(sends[step])

time: 200 us -> 202 us (1.010)
  matrix products: 39.5 us -> 42.5 us
  waiting for transfers between devices: 61.7 us -> 64.2 us
    ppermute x26, waiting for transfers between devices: 46.1 us -> 61.4 us  [swap(): return lax.ppermute(array, axis_name, bit_pairs(axis_name, bit))]
    all_to_all x2, waiting for transfers between devices: 15.6 us -> 2.81 us  [shards(): lax.all_to_all(columns, ('pool', 'tensor'), split_axis=0, concat_axis=0,...]
    dot_general x4, matrix products: 8.49 us -> 11.8 us  [shards(): jnp.dot(hidden, down_weight[:, piece * half:(piece + 1) * half], preferre...]
    unnamed x30 -> x36, local copies, waits for them, and re-layouts: 4.58 us -> 3.37 us
  transfers between devices with their start and end apart: 28 -> 28, of which waited for: 17 -> 19; matrix products, arithmetic and copies ran while one was open for 37% -> 38% of each run, Pallas kernels for 0% -> 0%
where the time goes in v2:
time: 202 us
  waiting for transfers between devices  64.2 us (32%)
  matrix products  42.5 us (21%)
  starting transfers between devices  41.4 us (20%)
  local copies, waits for them, and re-layouts  33.1 us (16%)
  other arithmetic  12.5 us (6%)
  between operations  7.9 us (4%)
    ppermute x26, waiting for transfers between devices, swap(): return lax.ppermute(array, axis_name, bit_pairs(axis_name, bit))  61.4 us
    ppermute x26, starting transfers between devices, swap(): return lax.ppermute(array, axis_name, bit_pairs(axis_name, bit))  30 us
    dot_general x2, matrix products, shards(): jnp.dot(flat_tokens, weights[kind], preferred_element_type=jnp.float32)  23.7 us
    optimization_barrier x2, local copies, waits for them, and re-layouts, after(): return lax.optimization_barrier((array, arrived))[0]  22.3 us
    dot_general x4, matrix products, shards(): jnp.dot(hidden, down_weight[:, piece * half:(piece + 1) * half], preferre...  11.8 us
    all_to_all x2, starting transfers between devices, shards(): lax.all_to_all(columns, ('pool', 'tensor'), split_axis=0, concat_axis=0,...  11.4 us
    add x2, other arithmetic, shards(): main.append(jnp.where(core == 0, low_share, high_share) + got)  7.34 us
  transfers between devices with their start and end apart: 28, of which 19 were waited for; matrix products, arithmetic and copies ran while one was open for 38% of the time, Pallas kernels for 0%

profile of v2, /device:TPU:0, one launch (start us, length us, event | category | flops | bytes accessed | tf_op | source)
XLA Modules:
  0.0 201.6 jit_solution(12003547179466251433)
XLA Ops:
  0.0 2.4 %fusion.123 = (bf16[1,1,32,28672]{3,2,1,0:T(8,128)(2,1)S(1)}, bf16[1,1,32,28672]{3,2,1,0:T(8,128)(2,1)S(1)}) fusion(bf16[1,2,32,28672]{3,2,1,0:T(8,128)(2,1)} %param.12), kind=kLoop, calls=%fused_computation.204 | loop fusion | bytes 7340032 | tf_op jit(solution)/shard_map/slice | solution.py:84
  4.4 7.4 %all-to-all-start = ((bf16[32,32,896]{2,1,0:T(8,128)(2,1)}), bf16[32,32,896]{2,1,0:T(8,128)(2,1)}, u32[]{:S(2)}, u32[]{:S(2)}) async-start(bf16[32,32,896]{2,1,0:T(8,128)(2,1)} %copy.49), calls=%async_computation | async-start | bytes 3670016 | tf_op jit(solution)/shard_map/all_to_all | solution.py:90
  12.8 3.7 %fusion.16 = f32[2,256,2,64]{1,3,2,0:T(8,128)S(1)} fusion(bf16[2,256,4096]{2,1,0:T(8,128)(2,1)} %param.8, bf16[1,2,4096,64]{2,3,1,0:T(8,128)(2,1)S(1)} %copy-done, f32[2,256]{1,0:T(2,128)S(1)} %bitcast.172), kind=kOutput, calls=%fused_computation.22 | convolution fusion | flops 536936448 | bytes 5507072 | tf_op jit(solution)/shard_map/snd,kdc->snkc/dot_general | solution.py:94
  19.8 9.3 %collective-permute-done.1 = f32[256,128]{0,1:T(8,128)S(1)} collective-permute-done((f32[256,128]{0,1:T(8,128)S(1)}, f32[256,128]{0,1:T(8,128)S(1)}, u32[]{:S(2)}, u32[]{:S(2)}) %collective-permute-start.1) | collective-permute-done | bytes 131104 | tf_op jit(solution)/shard_map/ppermute | solution.py:24
  31.8 20.5 %copy.85 = bf16[4096,2,1792]{2,0,1:T(8,128)(2,1)} copy(bf16[4096,2,1792]{2,1,0:T(2,128)(2,1)} %param.9) | data formatting | bytes 58720256 | tf_op jit(solution)/shard_map/optimization_barrier | solution.py:55
  52.3 2.8 %all-to-all-done = bf16[32,32,896]{2,1,0:T(8,128)(2,1)} async-done(((bf16[32,32,896]{2,1,0:T(8,128)(2,1)}), bf16[32,32,896]{2,1,0:T(8,128)(2,1)}, u32[]{:S(2)}, u32[]{:S(2)}) %all-to-all-start) | async-done | bytes 1835040 | tf_op jit(solution)/shard_map/all_to_all | solution.py:90
  56.9 4.0 %all-to-all-start.1 = ((bf16[32,32,896]{2,1,0:T(8,128)(2,1)}), bf16[32,32,896]{2,1,0:T(8,128)(2,1)S(1)}, u32[]{:S(2)}, u32[]{:S(2)}) async-start(bf16[32,32,896]{2,1,0:T(8,128)(2,1)} %copy.50), calls=%async_computation.1 | async-start | bytes 3670016 | tf_op jit(solution)/shard_map/all_to_all | solution.py:90
  60.9 11.8 %fusion = f32[512,1792]{1,0:T(8,128)S(1)} fusion(bf16[512,4096]{1,0:T(8,128)(2,1)} %bitcast.175, bf16[2,4096,1792]{2,1,0:T(8,128)(2,1)} %bitcast.155), kind=kOutput, calls=%fused_computation.2 | convolution fusion | flops 7516192768 | bytes 22544384 | tf_op jit(solution)/shard_map/dot_general | solution.py:122
  72.8 11.9 %fusion.2 = f32[512,1792]{1,0:T(8,128)S(1)} fusion(bf16[512,4096]{1,0:T(8,128)(2,1)S(1)} %bitcast.176, bf16[2,4096,1792]{2,1,0:T(8,128)(2,1)} %bitcast.156), kind=kOutput, calls=%fused_computation.4 | convolution fusion | flops 7516192768 | bytes 22544384 | tf_op jit(solution)/shard_map/dot_general | solution.py:122
  90.5 6.0 %collective-permute-done.4 = f32[256,128]{0,1:T(8,128)S(1)} collective-permute-done((f32[256,128]{0,1:T(8,128)S(1)}, f32[256,128]{0,1:T(8,128)S(1)}, u32[]{:S(2)}, u32[]{:S(2)}) %collective-permute-start.4) | collective-permute-done | bytes 131104 | tf_op jit(solution)/shard_map/ppermute | solution.py:24
  96.5 2.1 %collective-permute-start.5 = (f32[256,128]{0,1:T(8,128)S(1)}, f32[256,128]{0,1:T(8,128)S(1)}, u32[]{:S(2)}, u32[]{:S(2)}) collective-permute-start(f32[256,128]{0,1:T(8,128)S(1)} %add.234), channel_id=1, source_target_pairs={{0,16},{2,18},{4,20},{6,22},{8,24},{10,26},{12,28},{14,30},{16,0},... | collective-permute-start | bytes 393224 | tf_op jit(solution)/shard_map/ppermute | solution.py:24
  98.7 11.0 %collective-permute-done.5 = f32[256,128]{0,1:T(8,128)S(1)} collective-permute-done((f32[256,128]{0,1:T(8,128)S(1)}, f32[256,128]{0,1:T(8,128)S(1)}, u32[]{:S(2)}, u32[]{:S(2)}) %collective-permute-start.5) | collective-permute-done | bytes 131104 | tf_op jit(solution)/shard_map/ppermute | solution.py:24
  119.0 4.2 %select_add_fusion = f32[512,896]{1,0:T(8,128)} fusion(f32[512,896]{1,0:T(8,128)} %collective-permute-done.7, f32[512,1792]{1,0:T(8,128)} %copy-done.5, pred[]{:T(512)S(6)} %eq.18), kind=kLoop, calls=%fused_computation.18 | loop fusion | flops 917504 | bytes 7340033 | tf_op jit(solution)/shard_map/add | solution.py:131
  123.2 3.1 %select_add_fusion.1 = f32[512,896]{1,0:T(8,128)} fusion(f32[512,896]{1,0:T(8,128)} %collective-permute-done.3, f32[512,1792]{1,0:T(8,128)S(1)} %copy-done.4, pred[]{:T(512)S(6)} %eq.18), kind=kLoop, calls=%fused_computation.19 | loop fusion | flops 917504 | bytes 7340033 | tf_op jit(solution)/shard_map/add | solution.py:131
  131.6 5.4 %fusion.8 = f32[256,2048]{1,0:T(8,128)S(1)} fusion(bf16[1792,4096]{1,0:T(8,128)(2,1)} %param.10, bf16[256,896]{1,0:T(8,128)(2,1)S(1)} %collective-permute-done.8, bf16[128,896]{1,0:T(8,128)(2,1)S(1)} %fusion.29, bf16[128,896]{1,0:T(8,128)(2,1)S(1)} %fusion.31, pred[]{:T(512)S(6)} %eq.16), kind=kOutput, calls=%fused_computation.10 | convolution fusion | flops 1885011968 | bytes 10354689 | tf_op jit(solution)/shard_map/dot_general | solution.py:168
  138.6 2.1 %fusion.12 = f32[256,2048]{1,0:T(8,128)S(1)} fusion(bf16[1792,4096]{1,0:T(8,128)(2,1)S(1)} %bitcast.174, bf16[256,896]{1,0:T(8,128)(2,1)S(1)} %collective-permute-done.8, bf16[128,896]{1,0:T(8,128)(2,1)S(1)} %fusion.29, bf16[128,896]{1,0:T(8,128)(2,1)S(1)} %fusion.31, pred[]{:T(512)S(6)} %eq.16), kind=kOutput, calls=%fused_computation.14 | convolution fusion | flops 1885011968 | bytes 10354689 | tf_op jit(solution)/shard_map/dot_general | solution.py:168
  146.8 4.8 %collective-permute-done.11 = bf16[2,2,2,16,2048]{4,3,0,1,2:T(8,128)(2,1)S(1)} collective-permute-done((bf16[2,2,2,16,2048]{4,3,0,1,2:T(8,128)(2,1)S(1)}, bf16[2,2,2,16,2048]{4,3,0,1,2:T(8,128)(2,1)S(1)}, u32[]{:S(2)}, u32[]{:S(2)}) %collective-permute-start.11) | collective-permute-done | bytes 524320 | tf_op jit(solution)/shard_map/ppermute | solution.py:24
  153.2 2.4 %collective-permute-done.9 = bf16[2,2,2,16,2048]{4,3,0,1,2:T(8,128)(2,1)S(1)} collective-permute-done((bf16[2,2,2,16,2048]{4,3,0,1,2:T(8,128)(2,1)S(1)}, bf16[2,2,2,16,2048]{4,3,0,1,2:T(8,128)(2,1)S(1)}, u32[]{:S(2)}, u32[]{:S(2)}) %collective-permute-start.9) | collective-permute-done | bytes 524320 | tf_op jit(solution)/shard_map/ppermute | solution.py:24
  161.3 3.8 %collective-permute-done.10 = bf16[2,2,16,2048]{3,2,0,1:T(8,128)(2,1)S(1)} collective-permute-done((bf16[2,2,16,2048]{3,2,0,1:T(8,128)(2,1)S(1)}, bf16[2,2,16,2048]{3,2,0,1:T(8,128)(2,1)S(1)}, u32[]{:S(2)}, u32[]{:S(2)}) %collective-permute-start.10) | collective-permute-done | bytes 262176 | tf_op jit(solution)/shard_map/ppermute | solution.py:24
  165.2 6.6 %collective-permute-done.14 = bf16[2,2,2,16,2048]{4,3,0,1,2:T(8,128)(2,1)S(1)} collective-permute-done((bf16[2,2,2,16,2048]{4,3,0,1,2:T(8,128)(2,1)S(1)}, bf16[2,2,2,16,2048]{4,3,0,1,2:T(8,128)(2,1)S(1)}, u32[]{:S(2)}, u32[]{:S(2)}) %collective-permute-start.14) | collective-permute-done | bytes 524320 | tf_op jit(solution)/shard_map/ppermute | solution.py:24
  181.8 2.2 %collective-permute-start.19 = (bf16[16,2048]{1,0:T(8,128)(2,1)S(1)}, bf16[16,2048]{1,0:T(8,128)(2,1)S(1)}, u32[]{:S(2)}, u32[]{:S(2)}) collective-permute-start(bf16[16,2048]{1,0:T(8,128)(2,1)S(1)} %fusion.88), channel_id=1, source_target_pairs={{0,16},{2,18},{4,20},{6,22},{8,24},{10,26},{12,28},{14,30},{16,0},... | collective-permute-start | bytes 196616 | tf_op jit(solution)/shard_map/ppermute | solution.py:24
  189.6 3.5 %collective-permute-done.21 = bf16[2,16,2048]{2,1,0:T(8,128)(2,1)S(1)} collective-permute-done((bf16[2,16,2048]{2,1,0:T(8,128)(2,1)S(1)}, bf16[2,16,2048]{2,1,0:T(8,128)(2,1)S(1)}, u32[]{:S(2)}, u32[]{:S(2)}) %collective-permute-start.21) | collective-permute-done | bytes 131104 | tf_op jit(solution)/shard_map/ppermute | solution.py:24
  193.1 2.4 %collective-permute-start.22 = (bf16[16,2048]{1,0:T(8,128)(2,1)S(1)}, bf16[16,2048]{1,0:T(8,128)(2,1)S(1)}, u32[]{:S(2)}, u32[]{:S(2)}) collective-permute-start(bf16[16,2048]{1,0:T(8,128)(2,1)S(1)} %fusion.89), channel_id=1, source_target_pairs={{0,16},{2,18},{4,20},{6,22},{8,24},{10,26},{12,28},{14,30},{16,0},... | collective-permute-start | bytes 196616 | tf_op jit(solution)/shard_map/ppermute | solution.py:24
  198.3 2.4 %collective-permute-done.25 = bf16[16,2048]{1,0:T(8,128)(2,1)S(1)} collective-permute-done((bf16[16,2048]{1,0:T(8,128)(2,1)S(1)}, bf16[16,2048]{1,0:T(8,128)(2,1)S(1)}, u32[]{:S(2)}, u32[]{:S(2)}) %collective-permute-start.25) | collective-permute-done | bytes 65568 | tf_op jit(solution)/shard_map/ppermute | solution.py:24
  (151 shorter events, 57.8 us)
Async XLA Ops:
  4.4 50.7 %all-to-all-start = ((bf16[32,32,896]{2,1,0:T(8,128)(2,1)}), bf16[32,32,896]{2,1,0:T(8,128)(2,1)}, u32[]{:S(2)}, u32[]{:S(2)}) async-start(bf16[32,32,896]{2,1,0:T(8,128)(2,1)} %copy.49), calls=%async_computation | async-start | bytes 3670016 | tf_op jit(solution)/shard_map/all_to_all | solution.py:90
  18.0 11.1 %collective-permute-start.1 = (f32[256,128]{0,1:T(8,128)S(1)}, f32[256,128]{0,1:T(8,128)S(1)}, u32[]{:S(2)}, u32[]{:S(2)}) collective-permute-start(f32[256,128]{0,1:T(8,128)S(1)} %bitcast_add_fusion.16), channel_id=1, source_target_pairs={{0,2},{2,0},{4,6},{6,4},{8,10},{10,8},{12,14},{14,12},{16,18},{18,... | collective-permute-start | bytes 393224 | tf_op jit(solution)/shard_map/ppermute | solution.py:24
  29.1 23.2 %collective-permute-start.2 = (f32[256,128]{0,1:T(8,128)S(1)}, f32[256,128]{0,1:T(8,128)S(1)}, u32[]{:S(2)}, u32[]{:S(2)}) collective-permute-start(f32[256,128]{0,1:T(8,128)S(1)} %add.231), channel_id=1, source_target_pairs={{0,4},{2,6},{4,0},{6,2},{8,12},{10,14},{12,8},{14,10},{16,20},{18,... | collective-permute-start | bytes 393224 | tf_op jit(solution)/shard_map/ppermute | solution.py:24
  56.9 69.4 %all-to-all-start.1 = ((bf16[32,32,896]{2,1,0:T(8,128)(2,1)}), bf16[32,32,896]{2,1,0:T(8,128)(2,1)S(1)}, u32[]{:S(2)}, u32[]{:S(2)}) async-start(bf16[32,32,896]{2,1,0:T(8,128)(2,1)} %copy.50), calls=%async_computation.1 | async-start | bytes 3670016 | tf_op jit(solution)/shard_map/all_to_all | solution.py:90
  86.2 32.7 %collective-permute-start.7 = (f32[512,896]{1,0:T(8,128)}, f32[512,896]{1,0:T(8,128)}, u32[]{:S(2)}, u32[]{:S(2)}) collective-permute-start(f32[512,896]{1,0:T(8,128)} %slice_select_fusion), channel_id=1, source_target_pairs={{0,1},{1,0},{2,3},{3,2},{4,5},{5,4},{6,7},{7,6},{8,9},{9,8},{10,11... | collective-permute-start | bytes 5505032 | tf_op jit(solution)/shard_map/ppermute | solution.py:24
  88.5 34.7 %collective-permute-start.3 = (f32[512,896]{1,0:T(8,128)}, f32[512,896]{1,0:T(8,128)}, u32[]{:S(2)}, u32[]{:S(2)}) collective-permute-start(f32[512,896]{1,0:T(8,128)} %slice_select_fusion.1), channel_id=1, source_target_pairs={{0,1},{1,0},{2,3},{3,2},{4,5},{5,4},{6,7},{7,6},{8,9},{9,8},{10,11... | collective-permute-start | bytes 5505032 | tf_op jit(solution)/shard_map/ppermute | solution.py:24
  88.8 7.7 %collective-permute-start.4 = (f32[256,128]{0,1:T(8,128)S(1)}, f32[256,128]{0,1:T(8,128)S(1)}, u32[]{:S(2)}, u32[]{:S(2)}) collective-permute-start(f32[256,128]{0,1:T(8,128)S(1)} %add.232), channel_id=1, source_target_pairs={{0,8},{2,10},{4,12},{6,14},{8,0},{10,2},{12,4},{14,6},{16,24},{18,... | collective-permute-start | bytes 393224 | tf_op jit(solution)/shard_map/ppermute | solution.py:24
  96.5 13.2 %collective-permute-start.5 = (f32[256,128]{0,1:T(8,128)S(1)}, f32[256,128]{0,1:T(8,128)S(1)}, u32[]{:S(2)}, u32[]{:S(2)}) collective-permute-start(f32[256,128]{0,1:T(8,128)S(1)} %add.234), channel_id=1, source_target_pairs={{0,16},{2,18},{4,20},{6,22},{8,24},{10,26},{12,28},{14,30},{16,0},... | collective-permute-start | bytes 393224 | tf_op jit(solution)/shard_map/ppermute | solution.py:24
  109.8 9.0 %collective-permute-start.6 = (f32[256,128]{0,1:T(8,128)S(1)}, f32[256,128]{0,1:T(8,128)S(1)}, u32[]{:S(2)}, u32[]{:S(2)}) collective-permute-start(f32[256,128]{0,1:T(8,128)S(1)} %add.235), channel_id=1, source_target_pairs={{0,1},{1,0},{2,3},{3,2},{4,5},{5,4},{6,7},{7,6},{8,9},{9,8},{10,11... | collective-permute-start | bytes 393224 | tf_op jit(solution)/shard_map/ppermute | solution.py:24
  131.4 11.0 %collective-permute-start.13 = (bf16[256,896]{1,0:T(8,128)(2,1)S(1)}, bf16[256,896]{1,0:T(8,128)(2,1)S(1)}, u32[]{:S(2)}, u32[]{:S(2)}) collective-permute-start(bf16[256,896]{1,0:T(8,128)(2,1)S(1)} %pad_maximum_fusion.1), channel_id=1, source_target_pairs={{0,1},{1,0},{2,3},{3,2},{4,5},{5,4},{6,7},{7,6},{8,9},{9,8},{10,11... | collective-permute-start | bytes 1376264 | tf_op jit(solution)/shard_map/ppermute | solution.py:24
  137.1 14.4 %collective-permute-start.11 = (bf16[2,2,2,16,2048]{4,3,0,1,2:T(8,128)(2,1)S(1)}, bf16[2,2,2,16,2048]{4,3,0,1,2:T(8,128)(2,1)S(1)}, u32[]{:S(2)}, u32[]{:S(2)}) collective-permute-start(bf16[2,2,2,16,2048]{4,3,0,1,2:T(8,128)(2,1)S(1)} %fusion.21), channel_id=1, source_target_pairs={{0,4},{2,6},{4,0},{6,2},{8,12},{10,14},{12,8},{14,10},{16,20},{18,... | collective-permute-start | bytes 1572872 | tf_op jit(solution)/shard_map/ppermute | solution.py:24
  140.8 14.8 %collective-permute-start.9 = (bf16[2,2,2,16,2048]{4,3,0,1,2:T(8,128)(2,1)S(1)}, bf16[2,2,2,16,2048]{4,3,0,1,2:T(8,128)(2,1)S(1)}, u32[]{:S(2)}, u32[]{:S(2)}) collective-permute-start(bf16[2,2,2,16,2048]{4,3,0,1,2:T(8,128)(2,1)S(1)} %fusion.20), channel_id=1, source_target_pairs={{0,2},{2,0},{4,6},{6,4},{8,10},{10,8},{12,14},{14,12},{16,18},{18,... | collective-permute-start | bytes 1572872 | tf_op jit(solution)/shard_map/ppermute | solution.py:24
  151.8 9.4 %collective-permute-start.12 = (bf16[2,2,16,2048]{3,2,0,1:T(8,128)(2,1)S(1)}, bf16[2,2,16,2048]{3,2,0,1:T(8,128)(2,1)S(1)}, u32[]{:S(2)}, u32[]{:S(2)}) collective-permute-start(bf16[2,2,16,2048]{3,2,0,1:T(8,128)(2,1)S(1)} %fusion.33), channel_id=1, source_target_pairs={{0,2},{2,0},{4,6},{6,4},{8,10},{10,8},{12,14},{14,12},{16,18},{18,... | collective-permute-start | bytes 786440 | tf_op jit(solution)/shard_map/ppermute | solution.py:24
  155.7 9.3 %collective-permute-start.10 = (bf16[2,2,16,2048]{3,2,0,1:T(8,128)(2,1)S(1)}, bf16[2,2,16,2048]{3,2,0,1:T(8,128)(2,1)S(1)}, u32[]{:S(2)}, u32[]{:S(2)}) collective-permute-start(bf16[2,2,16,2048]{3,2,0,1:T(8,128)(2,1)S(1)} %fusion.32), channel_id=1, source_target_pairs={{0,4},{2,6},{4,0},{6,2},{8,12},{10,14},{12,8},{14,10},{16,20},{18,... | collective-permute-start | bytes 786440 | tf_op jit(solution)/shard_map/ppermute | solution.py:24
  155.8 16.0 %collective-permute-start.14 = (bf16[2,2,2,16,2048]{4,3,0,1,2:T(8,128)(2,1)S(1)}, bf16[2,2,2,16,2048]{4,3,0,1,2:T(8,128)(2,1)S(1)}, u32[]{:S(2)}, u32[]{:S(2)}) collective-permute-start(bf16[2,2,2,16,2048]{4,3,0,1,2:T(8,128)(2,1)S(1)} %fusion.22), channel_id=1, source_target_pairs={{0,2},{2,0},{4,6},{6,4},{8,10},{10,8},{12,14},{14,12},{16,18},{18,... | collective-permute-start | bytes 1572872 | tf_op jit(solution)/shard_map/ppermute | solution.py:24
  157.4 16.6 %collective-permute-start.15 = (bf16[2,2,2,16,2048]{4,3,0,1,2:T(8,128)(2,1)S(1)}, bf16[2,2,2,16,2048]{4,3,0,1,2:T(8,128)(2,1)S(1)}, u32[]{:S(2)}, u32[]{:S(2)}) collective-permute-start(bf16[2,2,2,16,2048]{4,3,0,1,2:T(8,128)(2,1)S(1)} %fusion.23), channel_id=1, source_target_pairs={{0,4},{2,6},{4,0},{6,2},{8,12},{10,14},{12,8},{14,10},{16,20},{18,... | collective-permute-start | bytes 1572872 | tf_op jit(solution)/shard_map/ppermute | solution.py:24
  174.3 5.4 %collective-permute-start.16 = (bf16[2,16,2048]{2,1,0:T(8,128)(2,1)S(1)}, bf16[2,16,2048]{2,1,0:T(8,128)(2,1)S(1)}, u32[]{:S(2)}, u32[]{:S(2)}) collective-permute-start(bf16[2,16,2048]{2,1,0:T(8,128)(2,1)S(1)} %fusion.79), channel_id=1, source_target_pairs={{0,8},{2,10},{4,12},{6,14},{8,0},{10,2},{12,4},{14,6},{16,24},{18,... | collective-permute-start | bytes 393224 | tf_op jit(solution)/shard_map/ppermute | solution.py:24
  174.4 12.8 %collective-permute-start.20 = (bf16[2,2,16,2048]{3,2,0,1:T(8,128)(2,1)S(1)}, bf16[2,2,16,2048]{3,2,0,1:T(8,128)(2,1)S(1)}, u32[]{:S(2)}, u32[]{:S(2)}) collective-permute-start(bf16[2,2,16,2048]{3,2,0,1:T(8,128)(2,1)S(1)} %fusion.34), channel_id=1, source_target_pairs={{0,4},{2,6},{4,0},{6,2},{8,12},{10,14},{12,8},{14,10},{16,20},{18,... | collective-permute-start | bytes 786440 | tf_op jit(solution)/shard_map/ppermute | solution.py:24
  175.1 13.9 %collective-permute-start.23 = (bf16[2,2,16,2048]{3,2,0,1:T(8,128)(2,1)S(1)}, bf16[2,2,16,2048]{3,2,0,1:T(8,128)(2,1)S(1)}, u32[]{:S(2)}, u32[]{:S(2)}) collective-permute-start(bf16[2,2,16,2048]{3,2,0,1:T(8,128)(2,1)S(1)} %fusion.35), channel_id=1, source_target_pairs={{0,2},{2,0},{4,6},{6,4},{8,10},{10,8},{12,14},{14,12},{16,18},{18,... | collective-permute-start | bytes 786440 | tf_op jit(solution)/shard_map/ppermute | solution.py:24
  176.5 5.3 %collective-permute-start.18 = (bf16[2,16,2048]{2,1,0:T(8,128)(2,1)S(1)}, bf16[2,16,2048]{2,1,0:T(8,128)(2,1)S(1)}, u32[]{:S(2)}, u32[]{:S(2)}) collective-permute-start(bf16[2,16,2048]{2,1,0:T(8,128)(2,1)S(1)} %fusion.80), channel_id=1, source_target_pairs={{0,8},{2,10},{4,12},{6,14},{8,0},{10,2},{12,4},{14,6},{16,24},{18,... | collective-permute-start | bytes 393224 | tf_op jit(solution)/shard_map/ppermute | solution.py:24
  179.7 6.2 %collective-permute-start.17 = (bf16[16,2048]{1,0:T(8,128)(2,1)S(1)}, bf16[16,2048]{1,0:T(8,128)(2,1)S(1)}, u32[]{:S(2)}, u32[]{:S(2)}) collective-permute-start(bf16[16,2048]{1,0:T(8,128)(2,1)S(1)} %fusion.87), channel_id=1, source_target_pairs={{0,16},{2,18},{4,20},{6,22},{8,24},{10,26},{12,28},{14,30},{16,0},... | collective-permute-start | bytes 196616 | tf_op jit(solution)/shard_map/ppermute | solution.py:24
  181.8 5.2 %collective-permute-start.19 = (bf16[16,2048]{1,0:T(8,128)(2,1)S(1)}, bf16[16,2048]{1,0:T(8,128)(2,1)S(1)}, u32[]{:S(2)}, u32[]{:S(2)}) collective-permute-start(bf16[16,2048]{1,0:T(8,128)(2,1)S(1)} %fusion.88), channel_id=1, source_target_pairs={{0,16},{2,18},{4,20},{6,22},{8,24},{10,26},{12,28},{14,30},{16,0},... | collective-permute-start | bytes 196616 | tf_op jit(solution)/shard_map/ppermute | solution.py:24
  187.3 5.7 %collective-permute-start.21 = (bf16[2,16,2048]{2,1,0:T(8,128)(2,1)S(1)}, bf16[2,16,2048]{2,1,0:T(8,128)(2,1)S(1)}, u32[]{:S(2)}, u32[]{:S(2)}) collective-permute-start(bf16[2,16,2048]{2,1,0:T(8,128)(2,1)S(1)} %fusion.81), channel_id=1, source_target_pairs={{0,8},{2,10},{4,12},{6,14},{8,0},{10,2},{12,4},{14,6},{16,24},{18,... | collective-permute-start | bytes 393224 | tf_op jit(solution)/shard_map/ppermute | solution.py:24
  189.1 6.4 %collective-permute-start.24 = (bf16[2,16,2048]{2,1,0:T(8,128)(2,1)S(1)}, bf16[2,16,2048]{2,1,0:T(8,128)(2,1)S(1)}, u32[]{:S(2)}, u32[]{:S(2)}) collective-permute-start(bf16[2,16,2048]{2,1,0:T(8,128)(2,1)S(1)} %fusion.82), channel_id=1, source_target_pairs={{0,8},{2,10},{4,12},{6,14},{8,0},{10,2},{12,4},{14,6},{16,24},{18,... | collective-permute-start | bytes 393224 | tf_op jit(solution)/shard_map/ppermute | solution.py:24
  (20 other events, 147.4 us)

commit v3 on v2

--- a/solution.py
+++ b/solution.py
@@ -117,12 +117,15 @@
     weights, shrunk, flat_tokens, _ = lax.optimization_barrier(
         (weights, shrunk, flat_tokens, second[0])
     )
-    shrunk = sum_over(shrunk, range(middle, bits_of("pool")))
-    products = [
-        jnp.dot(flat_tokens, weights[kind], preferred_element_type=jnp.float32)
-        for kind in range(kinds)
-    ]
-    products = lax.optimization_barrier(products)
+    bits = bits_of("pool")
+    products = []
+    for kind in range(kinds):
+        got = swap(shrunk, "pool", middle + kind)
+        products.append(
+            jnp.dot(flat_tokens, weights[kind], preferred_element_type=jnp.float32)
+        )
+        products, got, flat_tokens = lax.optimization_barrier((products, got, flat_tokens))
+        shrunk = shrunk + got
     main = []
     for product in products:
         if tensor_count == 2:
@@ -132,11 +135,11 @@
         else:
             main.append(scatter_sum(product, "tensor", 1))
 
+    shrunk = sum_over(shrunk, range(middle + kinds, bits))
     shrunk = gather(shrunk, "tensor", 0)
     high = shrunk.astype(jnp.bfloat16)
     low = (shrunk - high.astype(jnp.float32)).astype(jnp.bfloat16)
 
-    bits = bits_of("pool")
     positions = me * rows_here + jnp.arange(rows_here)
     owners = positions // BLK
     half = down_weight.shape[1] // 2
@@ -179,7 +182,11 @@
     arrived = [None] * steps
 
     def prepare(step, stage):
-        for piece in range(2):
+        if stage == 2:
+            parts[step] = [jnp.concatenate(parts[step], axis=-1)]
+        kept[step] = [None] * len(parts[step])
+        sends[step] = [None] * len(parts[step])
+        for piece in range(len(parts[step])):
             left = sorted(orders[piece][stage:], reverse=True)
             bit = orders[piece][stage]
             kept[step][piece], sends[step][piece] = halve(
@@ -188,10 +195,11 @@
 
     def exchange_rows(step, stage):
         arrived[step] = [
-            swap(sends[step][piece], "pool", orders[piece][stage]) for piece in range(2)
+            swap(sends[step][piece], "pool", orders[piece][stage])
+            for piece in range(len(sends[step]))
         ]
         parts[step] = [
-            kept[step][piece] + arrived[step][piece].astype(jnp.float32) for piece in range(2)
+            mine + got.astype(jnp.float32) for mine, got in zip(kept[step], arrived[step])
         ]
 
     for stage in range(bits):
@@ -210,7 +218,7 @@
             (owners[:, None] == jnp.arange(NBLK)[None, :]) * block_live[step][None, :], axis=1
         )
         keep = (positions % BLK < live).astype(jnp.float32)
-        summed = jnp.concatenate(parts[step], axis=1)
+        summed = parts[step][0]
         results.append((summed * keep[:, None]).astype(jnp.bfloat16))
     return jnp.stack(results)
 

time: 202 us -> 203 us (level)
  waiting for transfers between devices: 64.2 us -> 75.8 us
  starting transfers between devices: 41.4 us -> 32.1 us
    ppermute x26 -> x22, waiting for transfers between devices: 61.4 us -> 73.1 us  [swap(): return lax.ppermute(array, axis_name, bit_pairs(axis_name, bit))]
    ppermute x26 -> x22, starting transfers between devices: 30 us -> 20.7 us  [swap(): return lax.ppermute(array, axis_name, bit_pairs(axis_name, bit))]
  transfers between devices with their start and end apart: 28 -> 24, of which waited for: 19 -> 18; matrix products, arithmetic and copies ran while one was open for 38% -> 38% of each run, Pallas kernels for 0% -> 0%
where the time goes in v3:
time: 203 us; the launch traced here: 202 us
  waiting for transfers between devices  75.8 us (37%)
  matrix products  41 us (20%)
  local copies, waits for them, and re-layouts  32.5 us (16%)
  starting transfers between devices  32.1 us (16%)
  other arithmetic  12.8 us (6%)
  between operations  8.09 us (4%)
    ppermute x22, waiting for transfers between devices, swap(): return lax.ppermute(array, axis_name, bit_pairs(axis_name, bit))  73.1 us
    optimization_barrier x2, local copies, waits for them, and re-layouts, after(): return lax.optimization_barrier((array, arrived))[0]  22.4 us
    dot_general x2, matrix products, shards(): jnp.dot(flat_tokens, weights[kind], preferred_element_type=jnp.float32)  22.2 us
    ppermute x22, starting transfers between devices, swap(): return lax.ppermute(array, axis_name, bit_pairs(axis_name, bit))  20.7 us
    dot_general x4, matrix products, shards(): jnp.dot(hidden, down_weight[:, piece * half:(piece + 1) * half], preferre...  11.8 us
    all_to_all x2, starting transfers between devices, shards(): lax.all_to_all(columns, ('pool', 'tensor'), split_axis=0, concat_axis=0,...  11.5 us
    add x2, other arithmetic, shards(): main.append(jnp.where(core == 0, low_share, high_share) + got)  7.36 us
  transfers between devices with their start and end apart: 24, of which 18 were waited for; matrix products, arithmetic and copies ran while one was open for 38% of the time, Pallas kernels for 0%

profile of v3, /device:TPU:0, one launch (start us, length us, event | category | flops | bytes accessed | tf_op | source)
XLA Modules:
  0.0 202.3 jit_solution(12164577520547338731)
XLA Ops:
  0.0 2.4 %fusion.129 = (bf16[1,1,32,28672]{3,2,1,0:T(8,128)(2,1)S(1)}, bf16[1,1,32,28672]{3,2,1,0:T(8,128)(2,1)S(1)}) fusion(bf16[1,2,32,28672]{3,2,1,0:T(8,128)(2,1)} %param.12), kind=kLoop, calls=%fused_computation.204 | loop fusion | bytes 7340032 | tf_op jit(solution)/shard_map/slice | solution.py:84
  4.4 7.4 %all-to-all-start = ((bf16[32,32,896]{2,1,0:T(8,128)(2,1)}), bf16[32,32,896]{2,1,0:T(8,128)(2,1)}, u32[]{:S(2)}, u32[]{:S(2)}) async-start(bf16[32,32,896]{2,1,0:T(8,128)(2,1)} %copy.49), calls=%async_computation | async-start | bytes 3670016 | tf_op jit(solution)/shard_map/all_to_all | solution.py:90
  12.8 3.7 %fusion.16 = f32[2,256,2,64]{1,3,2,0:T(8,128)S(1)} fusion(bf16[2,256,4096]{2,1,0:T(8,128)(2,1)} %param.8, bf16[1,2,4096,64]{2,3,1,0:T(8,128)(2,1)S(1)} %copy-done, f32[2,256]{1,0:T(2,128)S(1)} %bitcast.160), kind=kOutput, calls=%fused_computation.30 | convolution fusion | flops 536936448 | bytes 5507072 | tf_op jit(solution)/shard_map/snd,kdc->snkc/dot_general | solution.py:94
  19.7 9.3 %collective-permute-done.1 = f32[256,128]{0,1:T(8,128)S(1)} collective-permute-done((f32[256,128]{0,1:T(8,128)S(1)}, f32[256,128]{0,1:T(8,128)S(1)}, u32[]{:S(2)}, u32[]{:S(2)}) %collective-permute-start.1) | collective-permute-done | bytes 131104 | tf_op jit(solution)/shard_map/ppermute | solution.py:24
  31.8 20.6 %copy.85 = bf16[4096,2,1792]{2,0,1:T(8,128)(2,1)} copy(bf16[4096,2,1792]{2,1,0:T(2,128)(2,1)} %param.9) | data formatting | bytes 58720256 | tf_op jit(solution)/shard_map/optimization_barrier | solution.py:55
  52.4 2.7 %all-to-all-done = bf16[32,32,896]{2,1,0:T(8,128)(2,1)} async-done(((bf16[32,32,896]{2,1,0:T(8,128)(2,1)}), bf16[32,32,896]{2,1,0:T(8,128)(2,1)}, u32[]{:S(2)}, u32[]{:S(2)}) %all-to-all-start) | async-done | bytes 1835040 | tf_op jit(solution)/shard_map/all_to_all | solution.py:90
  56.9 4.0 %all-to-all-start.1 = ((bf16[32,32,896]{2,1,0:T(8,128)(2,1)}), bf16[32,32,896]{2,1,0:T(8,128)(2,1)S(1)}, u32[]{:S(2)}, u32[]{:S(2)}) async-start(bf16[32,32,896]{2,1,0:T(8,128)(2,1)} %copy.50), calls=%async_computation.1 | async-start | bytes 3670016 | tf_op jit(solution)/shard_map/all_to_all | solution.py:90
  62.8 11.7 %fusion.2 = f32[512,1792]{1,0:T(8,128)S(1)} fusion(bf16[512,4096]{1,0:T(8,128)(2,1)} %bitcast.163, bf16[2,4096,1792]{2,1,0:T(8,128)(2,1)} %bitcast.143), kind=kOutput, calls=%fused_computation.4 | convolution fusion | flops 7516192768 | bytes 22544384 | tf_op jit(solution)/shard_map/dot_general | solution.py:125
  74.5 20.2 %collective-permute-done.3 = f32[256,128]{0,1:T(8,128)S(1)} collective-permute-done((f32[256,128]{0,1:T(8,128)S(1)}, f32[256,128]{0,1:T(8,128)S(1)}, u32[]{:S(2)}, u32[]{:S(2)}) %collective-permute-start.3) | collective-permute-done | bytes 131104 | tf_op jit(solution)/shard_map/ppermute | solution.py:24
  94.7 4.0 %collective-permute-start.4 = (f32[256,128]{0,1:T(8,128)S(1)}, f32[256,128]{0,1:T(8,128)S(1)}, u32[]{:S(2)}, u32[]{:S(2)}) collective-permute-start(f32[256,128]{0,1:T(8,128)S(1)} %add.213), channel_id=1, source_target_pairs={{0,16},{2,18},{4,20},{6,22},{8,24},{10,26},{12,28},{14,30},{16,0},... | collective-permute-start | bytes 393224 | tf_op jit(solution)/shard_map/ppermute | solution.py:24
  98.7 10.5 %fusion = f32[512,1792]{1,0:T(8,128)S(1)} fusion(bf16[512,4096]{1,0:T(8,128)(2,1)S(1)} %bitcast.164, bf16[2,4096,1792]{2,1,0:T(8,128)(2,1)} %bitcast.144), kind=kOutput, calls=%fused_computation.2 | convolution fusion | flops 7516192768 | bytes 22544384 | tf_op jit(solution)/shard_map/dot_general | solution.py:125
  123.3 4.2 %select_add_fusion = f32[512,896]{1,0:T(8,128)} fusion(f32[512,896]{1,0:T(8,128)} %collective-permute-done.7, f32[512,1792]{1,0:T(8,128)} %copy-done.5, pred[]{:T(512)S(6)} %eq.18), kind=kLoop, calls=%fused_computation.18 | loop fusion | flops 917504 | bytes 7340033 | tf_op jit(solution)/shard_map/add | solution.py:134
  127.5 3.1 %select_add_fusion.1 = f32[512,896]{1,0:T(8,128)} fusion(f32[512,896]{1,0:T(8,128)} %collective-permute-done.5, f32[512,1792]{1,0:T(8,128)S(1)} %copy-done.4, pred[]{:T(512)S(6)} %eq.18), kind=kLoop, calls=%fused_computation.19 | loop fusion | flops 917504 | bytes 7340033 | tf_op jit(solution)/shard_map/add | solution.py:134
  135.9 5.4 %fusion.8 = f32[256,2048]{1,0:T(8,128)S(1)} fusion(bf16[1792,4096]{1,0:T(8,128)(2,1)} %param.10, bf16[256,896]{1,0:T(8,128)(2,1)S(1)} %collective-permute-done.8, bf16[128,896]{1,0:T(8,128)(2,1)S(1)} %fusion.39, bf16[128,896]{1,0:T(8,128)(2,1)S(1)} %fusion.41, pred[]{:T(512)S(6)} %eq.16), kind=kOutput, calls=%fused_computation.10 | convolution fusion | flops 1885011968 | bytes 10354689 | tf_op jit(solution)/shard_map/dot_general | solution.py:171
  143.2 2.1 %fusion.12 = f32[256,2048]{1,0:T(8,128)S(1)} fusion(bf16[1792,4096]{1,0:T(8,128)(2,1)S(1)} %bitcast.162, bf16[256,896]{1,0:T(8,128)(2,1)S(1)} %collective-permute-done.8, bf16[128,896]{1,0:T(8,128)(2,1)S(1)} %fusion.39, bf16[128,896]{1,0:T(8,128)(2,1)S(1)} %fusion.41, pred[]{:T(512)S(6)} %eq.16), kind=kOutput, calls=%fused_computation.14 | convolution fusion | flops 1885011968 | bytes 10354689 | tf_op jit(solution)/shard_map/dot_general | solution.py:171
  151.2 4.7 %collective-permute-done.11 = bf16[2,2,2,16,2048]{4,3,0,1,2:T(8,128)(2,1)S(1)} collective-permute-done((bf16[2,2,2,16,2048]{4,3,0,1,2:T(8,128)(2,1)S(1)}, bf16[2,2,2,16,2048]{4,3,0,1,2:T(8,128)(2,1)S(1)}, u32[]{:S(2)}, u32[]{:S(2)}) %collective-permute-start.11) | collective-permute-done | bytes 524320 | tf_op jit(solution)/shard_map/ppermute | solution.py:24
  157.6 2.6 %collective-permute-done.9 = bf16[2,2,2,16,2048]{4,3,0,1,2:T(8,128)(2,1)S(1)} collective-permute-done((bf16[2,2,2,16,2048]{4,3,0,1,2:T(8,128)(2,1)S(1)}, bf16[2,2,2,16,2048]{4,3,0,1,2:T(8,128)(2,1)S(1)}, u32[]{:S(2)}, u32[]{:S(2)}) %collective-permute-start.9) | collective-permute-done | bytes 524320 | tf_op jit(solution)/shard_map/ppermute | solution.py:24
  165.9 3.8 %collective-permute-done.10 = bf16[2,2,16,2048]{3,2,0,1:T(8,128)(2,1)S(1)} collective-permute-done((bf16[2,2,16,2048]{3,2,0,1:T(8,128)(2,1)S(1)}, bf16[2,2,16,2048]{3,2,0,1:T(8,128)(2,1)S(1)}, u32[]{:S(2)}, u32[]{:S(2)}) %collective-permute-start.10) | collective-permute-done | bytes 262176 | tf_op jit(solution)/shard_map/ppermute | solution.py:24
  169.8 6.6 %collective-permute-done.14 = bf16[2,2,2,16,2048]{4,3,0,1,2:T(8,128)(2,1)S(1)} collective-permute-done((bf16[2,2,2,16,2048]{4,3,0,1,2:T(8,128)(2,1)S(1)}, bf16[2,2,2,16,2048]{4,3,0,1,2:T(8,128)(2,1)S(1)}, u32[]{:S(2)}, u32[]{:S(2)}) %collective-permute-start.14) | collective-permute-done | bytes 524320 | tf_op jit(solution)/shard_map/ppermute | solution.py:24
  180.2 4.1 %collective-permute-done.18 = bf16[2,2,16,2048]{3,2,0,1:T(8,128)(2,1)S(1)} collective-permute-done((bf16[2,2,16,2048]{3,2,0,1:T(8,128)(2,1)S(1)}, bf16[2,2,16,2048]{3,2,0,1:T(8,128)(2,1)S(1)}, u32[]{:S(2)}, u32[]{:S(2)}) %collective-permute-start.18) | collective-permute-done | bytes 262176 | tf_op jit(solution)/shard_map/ppermute | solution.py:24
  185.5 3.4 %collective-permute-done.16 = bf16[2,16,4096]{2,1,0:T(8,128)(2,1)S(1)} collective-permute-done((bf16[2,16,4096]{2,1,0:T(8,128)(2,1)S(1)}, bf16[2,16,4096]{2,1,0:T(8,128)(2,1)S(1)}, u32[]{:S(2)}, u32[]{:S(2)}) %collective-permute-start.16) | collective-permute-done | bytes 262176 | tf_op jit(solution)/shard_map/ppermute | solution.py:24
  189.1 4.6 %collective-permute-done.20 = bf16[2,16,4096]{2,1,0:T(8,128)(2,1)S(1)} collective-permute-done((bf16[2,16,4096]{2,1,0:T(8,128)(2,1)S(1)}, bf16[2,16,4096]{2,1,0:T(8,128)(2,1)S(1)}, u32[]{:S(2)}, u32[]{:S(2)}) %collective-permute-start.20) | collective-permute-done | bytes 262176 | tf_op jit(solution)/shard_map/ppermute | solution.py:24
  193.8 3.9 %collective-permute-done.17 = bf16[16,4096]{1,0:T(8,128)(2,1)S(1)} collective-permute-done((bf16[16,4096]{1,0:T(8,128)(2,1)S(1)}, bf16[16,4096]{1,0:T(8,128)(2,1)S(1)}, u32[]{:S(2)}, u32[]{:S(2)}) %collective-permute-start.17) | collective-permute-done | bytes 131104 | tf_op jit(solution)/shard_map/ppermute | solution.py:24
  197.7 3.7 %collective-permute-done.21 = bf16[16,4096]{1,0:T(8,128)(2,1)S(1)} collective-permute-done((bf16[16,4096]{1,0:T(8,128)(2,1)S(1)}, bf16[16,4096]{1,0:T(8,128)(2,1)S(1)}, u32[]{:S(2)}, u32[]{:S(2)}) %collective-permute-start.21) | collective-permute-done | bytes 131104 | tf_op jit(solution)/shard_map/ppermute | solution.py:24
  (133 shorter events, 45.4 us)
Async XLA Ops:
  4.4 50.7 %all-to-all-start = ((bf16[32,32,896]{2,1,0:T(8,128)(2,1)}), bf16[32,32,896]{2,1,0:T(8,128)(2,1)}, u32[]{:S(2)}, u32[]{:S(2)}) async-start(bf16[32,32,896]{2,1,0:T(8,128)(2,1)} %copy.49), calls=%async_computation | async-start | bytes 3670016 | tf_op jit(solution)/shard_map/all_to_all | solution.py:90
  16.5 1.4 collective-permute-start
  18.0 11.1 %collective-permute-start.1 = (f32[256,128]{0,1:T(8,128)S(1)}, f32[256,128]{0,1:T(8,128)S(1)}, u32[]{:S(2)}, u32[]{:S(2)}) collective-permute-start(f32[256,128]{0,1:T(8,128)S(1)} %bitcast_add_fusion.10), channel_id=1, source_target_pairs={{0,2},{2,0},{4,6},{6,4},{8,10},{10,8},{12,14},{14,12},{16,18},{18,... | collective-permute-start | bytes 393224 | tf_op jit(solution)/shard_map/ppermute | solution.py:24
  29.1 23.3 %collective-permute-start.2 = (f32[256,128]{0,1:T(8,128)S(1)}, f32[256,128]{0,1:T(8,128)S(1)}, u32[]{:S(2)}, u32[]{:S(2)}) collective-permute-start(f32[256,128]{0,1:T(8,128)S(1)} %add.211), channel_id=1, source_target_pairs={{0,4},{2,6},{4,0},{6,2},{8,12},{10,14},{12,8},{14,10},{16,20},{18,... | collective-permute-start | bytes 393224 | tf_op jit(solution)/shard_map/ppermute | solution.py:24
  56.9 73.7 %all-to-all-start.1 = ((bf16[32,32,896]{2,1,0:T(8,128)(2,1)}), bf16[32,32,896]{2,1,0:T(8,128)(2,1)S(1)}, u32[]{:S(2)}, u32[]{:S(2)}) async-start(bf16[32,32,896]{2,1,0:T(8,128)(2,1)} %copy.50), calls=%async_computation.1 | async-start | bytes 3670016 | tf_op jit(solution)/shard_map/all_to_all | solution.py:90
  61.0 33.7 %collective-permute-start.3 = (f32[256,128]{0,1:T(8,128)S(1)}, f32[256,128]{0,1:T(8,128)S(1)}, u32[]{:S(2)}, u32[]{:S(2)}) collective-permute-start(f32[256,128]{0,1:T(8,128)S(1)} %add.212), channel_id=1, source_target_pairs={{0,8},{2,10},{4,12},{6,14},{8,0},{10,2},{12,4},{14,6},{16,24},{18,... | collective-permute-start | bytes 393224 | tf_op jit(solution)/shard_map/ppermute | solution.py:24
  94.7 15.1 %collective-permute-start.4 = (f32[256,128]{0,1:T(8,128)S(1)}, f32[256,128]{0,1:T(8,128)S(1)}, u32[]{:S(2)}, u32[]{:S(2)}) collective-permute-start(f32[256,128]{0,1:T(8,128)S(1)} %add.213), channel_id=1, source_target_pairs={{0,16},{2,18},{4,20},{6,22},{8,24},{10,26},{12,28},{14,30},{16,0},... | collective-permute-start | bytes 393224 | tf_op jit(solution)/shard_map/ppermute | solution.py:24
  111.7 11.6 %collective-permute-start.7 = (f32[512,896]{1,0:T(8,128)}, f32[512,896]{1,0:T(8,128)}, u32[]{:S(2)}, u32[]{:S(2)}) collective-permute-start(f32[512,896]{1,0:T(8,128)} %slice_select_fusion), channel_id=1, source_target_pairs={{0,1},{1,0},{2,3},{3,2},{4,5},{5,4},{6,7},{7,6},{8,9},{9,8},{10,11... | collective-permute-start | bytes 5505032 | tf_op jit(solution)/shard_map/ppermute | solution.py:24
  113.2 14.4 %collective-permute-start.5 = (f32[512,896]{1,0:T(8,128)}, f32[512,896]{1,0:T(8,128)}, u32[]{:S(2)}, u32[]{:S(2)}) collective-permute-start(f32[512,896]{1,0:T(8,128)} %slice_select_fusion.1), channel_id=1, source_target_pairs={{0,1},{1,0},{2,3},{3,2},{4,5},{5,4},{6,7},{7,6},{8,9},{9,8},{10,11... | collective-permute-start | bytes 5505032 | tf_op jit(solution)/shard_map/ppermute | solution.py:24
  113.8 9.3 %collective-permute-start.6 = (f32[256,128]{0,1:T(8,128)S(1)}, f32[256,128]{0,1:T(8,128)S(1)}, u32[]{:S(2)}, u32[]{:S(2)}) collective-permute-start(f32[256,128]{0,1:T(8,128)S(1)} %add.215), channel_id=1, source_target_pairs={{0,1},{1,0},{2,3},{3,2},{4,5},{5,4},{6,7},{7,6},{8,9},{9,8},{10,11... | collective-permute-start | bytes 393224 | tf_op jit(solution)/shard_map/ppermute | solution.py:24
  133.9 2.0 collective-permute-start.8
  135.7 11.0 %collective-permute-start.13 = (bf16[256,896]{1,0:T(8,128)(2,1)S(1)}, bf16[256,896]{1,0:T(8,128)(2,1)S(1)}, u32[]{:S(2)}, u32[]{:S(2)}) collective-permute-start(bf16[256,896]{1,0:T(8,128)(2,1)S(1)} %pad_maximum_fusion.1), channel_id=1, source_target_pairs={{0,1},{1,0},{2,3},{3,2},{4,5},{5,4},{6,7},{7,6},{8,9},{9,8},{10,11... | collective-permute-start | bytes 1376264 | tf_op jit(solution)/shard_map/ppermute | solution.py:24
  141.4 14.4 %collective-permute-start.11 = (bf16[2,2,2,16,2048]{4,3,0,1,2:T(8,128)(2,1)S(1)}, bf16[2,2,2,16,2048]{4,3,0,1,2:T(8,128)(2,1)S(1)}, u32[]{:S(2)}, u32[]{:S(2)}) collective-permute-start(bf16[2,2,2,16,2048]{4,3,0,1,2:T(8,128)(2,1)S(1)} %fusion.21), channel_id=1, source_target_pairs={{0,4},{2,6},{4,0},{6,2},{8,12},{10,14},{12,8},{14,10},{16,20},{18,... | collective-permute-start | bytes 1572872 | tf_op jit(solution)/shard_map/ppermute | solution.py:24
  145.4 14.8 %collective-permute-start.9 = (bf16[2,2,2,16,2048]{4,3,0,1,2:T(8,128)(2,1)S(1)}, bf16[2,2,2,16,2048]{4,3,0,1,2:T(8,128)(2,1)S(1)}, u32[]{:S(2)}, u32[]{:S(2)}) collective-permute-start(bf16[2,2,2,16,2048]{4,3,0,1,2:T(8,128)(2,1)S(1)} %fusion.20), channel_id=1, source_target_pairs={{0,2},{2,0},{4,6},{6,4},{8,10},{10,8},{12,14},{14,12},{16,18},{18,... | collective-permute-start | bytes 1572872 | tf_op jit(solution)/shard_map/ppermute | solution.py:24
  156.0 9.8 %collective-permute-start.12 = (bf16[2,2,16,2048]{3,2,0,1:T(8,128)(2,1)S(1)}, bf16[2,2,16,2048]{3,2,0,1:T(8,128)(2,1)S(1)}, u32[]{:S(2)}, u32[]{:S(2)}) collective-permute-start(bf16[2,2,16,2048]{3,2,0,1:T(8,128)(2,1)S(1)} %fusion.43), channel_id=1, source_target_pairs={{0,2},{2,0},{4,6},{6,4},{8,10},{10,8},{12,14},{14,12},{16,18},{18,... | collective-permute-start | bytes 786440 | tf_op jit(solution)/shard_map/ppermute | solution.py:24
  160.3 9.3 %collective-permute-start.10 = (bf16[2,2,16,2048]{3,2,0,1:T(8,128)(2,1)S(1)}, bf16[2,2,16,2048]{3,2,0,1:T(8,128)(2,1)S(1)}, u32[]{:S(2)}, u32[]{:S(2)}) collective-permute-start(bf16[2,2,16,2048]{3,2,0,1:T(8,128)(2,1)S(1)} %fusion.42), channel_id=1, source_target_pairs={{0,4},{2,6},{4,0},{6,2},{8,12},{10,14},{12,8},{14,10},{16,20},{18,... | collective-permute-start | bytes 786440 | tf_op jit(solution)/shard_map/ppermute | solution.py:24
  160.4 16.0 %collective-permute-start.14 = (bf16[2,2,2,16,2048]{4,3,0,1,2:T(8,128)(2,1)S(1)}, bf16[2,2,2,16,2048]{4,3,0,1,2:T(8,128)(2,1)S(1)}, u32[]{:S(2)}, u32[]{:S(2)}) collective-permute-start(bf16[2,2,2,16,2048]{4,3,0,1,2:T(8,128)(2,1)S(1)} %fusion.22), channel_id=1, source_target_pairs={{0,2},{2,0},{4,6},{6,4},{8,10},{10,8},{12,14},{14,12},{16,18},{18,... | collective-permute-start | bytes 1572872 | tf_op jit(solution)/shard_map/ppermute | solution.py:24
  161.8 16.9 %collective-permute-start.15 = (bf16[2,2,2,16,2048]{4,3,0,1,2:T(8,128)(2,1)S(1)}, bf16[2,2,2,16,2048]{4,3,0,1,2:T(8,128)(2,1)S(1)}, u32[]{:S(2)}, u32[]{:S(2)}) collective-permute-start(bf16[2,2,2,16,2048]{4,3,0,1,2:T(8,128)(2,1)S(1)} %fusion.23), channel_id=1, source_target_pairs={{0,4},{2,6},{4,0},{6,2},{8,12},{10,14},{12,8},{14,10},{16,20},{18,... | collective-permute-start | bytes 1572872 | tf_op jit(solution)/shard_map/ppermute | solution.py:24
  176.6 7.7 %collective-permute-start.18 = (bf16[2,2,16,2048]{3,2,0,1:T(8,128)(2,1)S(1)}, bf16[2,2,16,2048]{3,2,0,1:T(8,128)(2,1)S(1)}, u32[]{:S(2)}, u32[]{:S(2)}) collective-permute-start(bf16[2,2,16,2048]{3,2,0,1:T(8,128)(2,1)S(1)} %fusion.44), channel_id=1, source_target_pairs={{0,4},{2,6},{4,0},{6,2},{8,12},{10,14},{12,8},{14,10},{16,20},{18,... | collective-permute-start | bytes 786440 | tf_op jit(solution)/shard_map/ppermute | solution.py:24
  178.8 6.4 %collective-permute-start.19 = (bf16[2,2,16,2048]{3,2,0,1:T(8,128)(2,1)S(1)}, bf16[2,2,16,2048]{3,2,0,1:T(8,128)(2,1)S(1)}, u32[]{:S(2)}, u32[]{:S(2)}) collective-permute-start(bf16[2,2,16,2048]{3,2,0,1:T(8,128)(2,1)S(1)} %fusion.45), channel_id=1, source_target_pairs={{0,2},{2,0},{4,6},{6,4},{8,10},{10,8},{12,14},{14,12},{16,18},{18,... | collective-permute-start | bytes 786440 | tf_op jit(solution)/shard_map/ppermute | solution.py:24
  180.2 8.6 %collective-permute-start.16 = (bf16[2,16,4096]{2,1,0:T(8,128)(2,1)S(1)}, bf16[2,16,4096]{2,1,0:T(8,128)(2,1)S(1)}, u32[]{:S(2)}, u32[]{:S(2)}) collective-permute-start(bf16[2,16,4096]{2,1,0:T(8,128)(2,1)S(1)} %fusion.46), channel_id=1, source_target_pairs={{0,8},{2,10},{4,12},{6,14},{8,0},{10,2},{12,4},{14,6},{16,24},{18,... | collective-permute-start | bytes 786440 | tf_op jit(solution)/shard_map/ppermute | solution.py:24
  185.4 8.3 %collective-permute-start.20 = (bf16[2,16,4096]{2,1,0:T(8,128)(2,1)S(1)}, bf16[2,16,4096]{2,1,0:T(8,128)(2,1)S(1)}, u32[]{:S(2)}, u32[]{:S(2)}) collective-permute-start(bf16[2,16,4096]{2,1,0:T(8,128)(2,1)S(1)} %fusion.47), channel_id=1, source_target_pairs={{0,8},{2,10},{4,12},{6,14},{8,0},{10,2},{12,4},{14,6},{16,24},{18,... | collective-permute-start | bytes 786440 | tf_op jit(solution)/shard_map/ppermute | solution.py:24
  189.0 8.7 %collective-permute-start.17 = (bf16[16,4096]{1,0:T(8,128)(2,1)S(1)}, bf16[16,4096]{1,0:T(8,128)(2,1)S(1)}, u32[]{:S(2)}, u32[]{:S(2)}) collective-permute-start(bf16[16,4096]{1,0:T(8,128)(2,1)S(1)} %fusion.93), channel_id=1, source_target_pairs={{0,16},{2,18},{4,20},{6,22},{8,24},{10,26},{12,28},{14,30},{16,0},... | collective-permute-start | bytes 393224 | tf_op jit(solution)/shard_map/ppermute | solution.py:24
  193.7 7.8 %collective-permute-start.21 = (bf16[16,4096]{1,0:T(8,128)(2,1)S(1)}, bf16[16,4096]{1,0:T(8,128)(2,1)S(1)}, u32[]{:S(2)}, u32[]{:S(2)}) collective-permute-start(bf16[16,4096]{1,0:T(8,128)(2,1)S(1)} %fusion.94), channel_id=1, source_target_pairs={{0,16},{2,18},{4,20},{6,22},{8,24},{10,26},{12,28},{14,30},{16,0},... | collective-permute-start | bytes 393224 | tf_op jit(solution)/shard_map/ppermute | solution.py:24
  (16 other events, 184.6 us)

commit v4 on v2

--- a/solution.py
+++ b/solution.py
@@ -78,18 +78,16 @@
     rows_here = total_rows // pool_count
     slots = adapter_slot[block_adapter]
 
-    second = []
-    outgoing = []
-    for kind in range(kinds):
+    def columns_of(kind):
         columns = expand_store[0, kind].reshape(ranks_local, pool_count * tensor_count, units_here)
-        columns = columns.transpose(1, 0, 2)
-        if second:
-            columns = after(columns, second[-1])
-        outgoing.append(columns)
-        second.append(
-            lax.all_to_all(columns, ("pool", "tensor"), split_axis=0, concat_axis=0, tiled=True)
-        )
-    pages = [one.reshape(pool_count, rank, units_here) for one in second]
+        return columns.transpose(1, 0, 2)
+
+    def exchange_columns(columns):
+        got = lax.all_to_all(columns, ("pool", "tensor"), split_axis=0, concat_axis=0, tiled=True)
+        return got.reshape(pool_count, rank, units_here)
+
+    outgoing = [columns_of(kind) for kind in range(kinds)]
+    pages = [exchange_columns(outgoing[0])]
 
     first = jnp.einsum(
         "snd,kdc->snkc",
@@ -110,14 +108,17 @@
     middle = bits_of("pool") // 2
     shrunk = sum_over(shrunk, range(middle))
 
-    flat_tokens = tokens.reshape(steps * total_rows, width_local)
-
     weights = after(gate_up_weight, outgoing[0])
     weights = jnp.transpose(weights, (1, 0, 2))
-    weights, shrunk, flat_tokens, _ = lax.optimization_barrier(
-        (weights, shrunk, flat_tokens, second[0])
-    )
+    shrunk, weights, _ = lax.optimization_barrier((shrunk, weights, pages[0]))
     shrunk = sum_over(shrunk, range(middle, bits_of("pool")))
+    shrunk = gather(shrunk, "tensor", 0)
+    for kind in range(1, kinds):
+        outgoing[kind] = after(outgoing[kind], (shrunk, pages[-1]))
+        pages.append(exchange_columns(outgoing[kind]))
+
+    flat_tokens = tokens.reshape(steps * total_rows, width_local)
+    weights, flat_tokens, _ = lax.optimization_barrier((weights, flat_tokens, outgoing[-1]))
     products = [
         jnp.dot(flat_tokens, weights[kind], preferred_element_type=jnp.float32)
         for kind in range(kinds)
@@ -132,7 +133,6 @@
         else:
             main.append(scatter_sum(product, "tensor", 1))
 
-    shrunk = gather(shrunk, "tensor", 0)
     high = shrunk.astype(jnp.bfloat16)
     low = (shrunk - high.astype(jnp.float32)).astype(jnp.bfloat16)
 
@@ -179,7 +179,11 @@
     arrived = [None] * steps
 
     def prepare(step, stage):
-        for piece in range(2):
+        if stage == 2:
+            parts[step] = [jnp.concatenate(parts[step], axis=-1)]
+        kept[step] = [None] * len(parts[step])
+        sends[step] = [None] * len(parts[step])
+        for piece in range(len(parts[step])):
             left = sorted(orders[piece][stage:], reverse=True)
             bit = orders[piece][stage]
             kept[step][piece], sends[step][piece] = halve(
@@ -188,10 +192,11 @@
 
     def exchange_rows(step, stage):
         arrived[step] = [
-            swap(sends[step][piece], "pool", orders[piece][stage]) for piece in range(2)
+            swap(sends[step][piece], "pool", orders[piece][stage])
+            for piece in range(len(sends[step]))
         ]
         parts[step] = [
-            kept[step][piece] + arrived[step][piece].astype(jnp.float32) for piece in range(2)
+            mine + got.astype(jnp.float32) for mine, got in zip(kept[step], arrived[step])
         ]
 
     for stage in range(bits):
@@ -210,7 +215,7 @@
             (owners[:, None] == jnp.arange(NBLK)[None, :]) * block_live[step][None, :], axis=1
         )
         keep = (positions % BLK < live).astype(jnp.float32)
-        summed = jnp.concatenate(parts[step], axis=1)
+        summed = parts[step][0]
         results.append((summed * keep[:, None]).astype(jnp.bfloat16))
     return jnp.stack(results)
 

time: 202 us -> 194 us (0.960)
  starting transfers between devices: 41.4 us -> 35.7 us
    ppermute x26 -> x22, starting transfers between devices: 30 us -> 23.8 us  [swap(): return lax.ppermute(array, axis_name, bit_pairs(axis_name, bit))]
    ppermute x26 -> x22, waiting for transfers between devices: 61.4 us -> 58.6 us  [swap(): return lax.ppermute(array, axis_name, bit_pairs(axis_name, bit))]
  transfers between devices with their start and end apart: 28 -> 24, of which waited for: 19 -> 17; matrix products, arithmetic and copies ran while one was open for 38% -> 39% of each run, Pallas kernels for 0% -> 0%
where the time goes in v4:
time: 194 us; the launch traced here: 193 us
  waiting for transfers between devices  63 us (32%)
  matrix products  42.5 us (22%)
  starting transfers between devices  35.7 us (18%)
  local copies, waits for them, and re-layouts  31.6 us (16%)
  other arithmetic  12.5 us (6%)
  between operations  8.07 us (4%)
    ppermute x22, waiting for transfers between devices, swap(): return lax.ppermute(array, axis_name, bit_pairs(axis_name, bit))  58.6 us
    ppermute x22, starting transfers between devices, swap(): return lax.ppermute(array, axis_name, bit_pairs(axis_name, bit))  23.8 us
    dot_general x2, matrix products, shards(): jnp.dot(flat_tokens, weights[kind], preferred_element_type=jnp.float32)  23.7 us
    optimization_barrier x2, local copies, waits for them, and re-layouts, after(): return lax.optimization_barrier((array, arrived))[0]  22.2 us
    all_to_all x2, starting transfers between devices, exchange_columns(): lax.all_to_all(columns, ('pool', 'tensor'), split_axis=0, concat_axis=0,...  12 us
    dot_general x4, matrix products, shards(): jnp.dot(hidden, down_weight[:, piece * half:(piece + 1) * half], preferre...  11.8 us
    add x2, other arithmetic, shards(): main.append(jnp.where(core == 0, low_share, high_share) + got)  7.36 us
    all_to_all x2, waiting for transfers between devices, exchange_columns(): lax.all_to_all(columns, ('pool', 'tensor'), split_axis=0, concat_axis=0,...  4.37 us
  transfers between devices with their start and end apart: 24, of which 17 were waited for; matrix products, arithmetic and copies ran while one was open for 39% of the time, Pallas kernels for 0%

profile of v4, /device:TPU:0, one launch (start us, length us, event | category | flops | bytes accessed | tf_op | source)
XLA Modules:
  0.0 193.4 jit_solution(3807895547519778052)
XLA Ops:
  0.0 2.4 %fusion.128 = (bf16[1,1,32,28672]{3,2,1,0:T(8,128)(2,1)S(1)}, bf16[1,1,32,28672]{3,2,1,0:T(8,128)(2,1)S(1)}) fusion(bf16[1,2,32,28672]{3,2,1,0:T(8,128)(2,1)} %param.12), kind=kLoop, calls=%fused_computation.203 | loop fusion | bytes 7340032 | tf_op jit(solution)/shard_map/slice | solution.py:82
  4.4 7.4 %all-to-all-start = ((bf16[32,32,896]{2,1,0:T(8,128)(2,1)}), bf16[32,32,896]{2,1,0:T(8,128)(2,1)}, u32[]{:S(2)}, u32[]{:S(2)}) async-start(bf16[32,32,896]{2,1,0:T(8,128)(2,1)} %copy.49), calls=%async_computation | async-start | bytes 3670016 | tf_op jit(solution)/shard_map/all_to_all | solution.py:86
  12.8 3.7 %fusion.16 = f32[2,256,2,64]{1,3,2,0:T(8,128)S(1)} fusion(bf16[2,256,4096]{2,1,0:T(8,128)(2,1)} %param.8, bf16[1,2,4096,64]{2,3,1,0:T(8,128)(2,1)S(1)} %copy-done, f32[2,256]{1,0:T(2,128)S(1)} %bitcast.160), kind=kOutput, calls=%fused_computation.30 | convolution fusion | flops 536936448 | bytes 5507072 | tf_op jit(solution)/shard_map/snd,kdc->snkc/dot_general | solution.py:92
  19.7 9.3 %collective-permute-done.1 = f32[256,128]{0,1:T(8,128)S(1)} collective-permute-done((f32[256,128]{0,1:T(8,128)S(1)}, f32[256,128]{0,1:T(8,128)S(1)}, u32[]{:S(2)}, u32[]{:S(2)}) %collective-permute-start.1) | collective-permute-done | bytes 131104 | tf_op jit(solution)/shard_map/ppermute | solution.py:24
  30.3 20.4 %copy.85 = bf16[4096,2,1792]{2,0,1:T(8,128)(2,1)} copy(bf16[4096,2,1792]{2,1,0:T(2,128)(2,1)} %param.9) | data formatting | bytes 58720256 | tf_op jit(solution)/shard_map/optimization_barrier | solution.py:55
  50.7 4.4 %all-to-all-done = bf16[32,32,896]{2,1,0:T(8,128)(2,1)} async-done(((bf16[32,32,896]{2,1,0:T(8,128)(2,1)}), bf16[32,32,896]{2,1,0:T(8,128)(2,1)}, u32[]{:S(2)}, u32[]{:S(2)}) %all-to-all-start) | async-done | bytes 1835040 | tf_op jit(solution)/shard_map/all_to_all | solution.py:86
  55.1 5.0 %collective-permute-done.3 = f32[256,128]{0,1:T(8,128)S(1)} collective-permute-done((f32[256,128]{0,1:T(8,128)S(1)}, f32[256,128]{0,1:T(8,128)S(1)}, u32[]{:S(2)}, u32[]{:S(2)}) %collective-permute-start.3) | collective-permute-done | bytes 131104 | tf_op jit(solution)/shard_map/ppermute | solution.py:24
  61.8 6.6 %collective-permute-done.4 = f32[256,128]{0,1:T(8,128)S(1)} collective-permute-done((f32[256,128]{0,1:T(8,128)S(1)}, f32[256,128]{0,1:T(8,128)S(1)}, u32[]{:S(2)}, u32[]{:S(2)}) %collective-permute-start.4) | collective-permute-done | bytes 131104 | tf_op jit(solution)/shard_map/ppermute | solution.py:24
  71.7 4.6 %all-to-all-start.1 = ((bf16[32,32,896]{2,1,0:T(8,128)(2,1)}), bf16[32,32,896]{2,1,0:T(8,128)(2,1)S(1)}, u32[]{:S(2)}, u32[]{:S(2)}) async-start(bf16[32,32,896]{2,1,0:T(8,128)(2,1)} %copy.50), calls=%async_computation.1 | async-start | bytes 3670016 | tf_op jit(solution)/shard_map/all_to_all | solution.py:86
  76.3 11.8 %fusion = f32[512,1792]{1,0:T(8,128)S(1)} fusion(bf16[512,4096]{1,0:T(8,128)(2,1)} %bitcast.163, bf16[2,4096,1792]{2,1,0:T(8,128)(2,1)} %bitcast.143), kind=kOutput, calls=%fused_computation.2 | convolution fusion | flops 7516192768 | bytes 22544384 | tf_op jit(solution)/shard_map/dot_general | solution.py:123
  88.1 11.9 %fusion.2 = f32[512,1792]{1,0:T(8,128)S(1)} fusion(bf16[512,4096]{1,0:T(8,128)(2,1)S(1)} %bitcast.164, bf16[2,4096,1792]{2,1,0:T(8,128)(2,1)} %bitcast.144), kind=kOutput, calls=%fused_computation.4 | convolution fusion | flops 7516192768 | bytes 22544384 | tf_op jit(solution)/shard_map/dot_general | solution.py:123
  113.6 4.2 %select_add_fusion = f32[512,896]{1,0:T(8,128)} fusion(f32[512,896]{1,0:T(8,128)} %collective-permute-done.7, f32[512,1792]{1,0:T(8,128)} %copy-done.5, pred[]{:T(512)S(6)} %eq.18), kind=kLoop, calls=%fused_computation.18 | loop fusion | flops 917504 | bytes 7340033 | tf_op jit(solution)/shard_map/add | solution.py:132
  117.8 3.1 %select_add_fusion.1 = f32[512,896]{1,0:T(8,128)} fusion(f32[512,896]{1,0:T(8,128)} %collective-permute-done.6, f32[512,1792]{1,0:T(8,128)S(1)} %copy-done.4, pred[]{:T(512)S(6)} %eq.18), kind=kLoop, calls=%fused_computation.19 | loop fusion | flops 917504 | bytes 7340033 | tf_op jit(solution)/shard_map/add | solution.py:132
  126.1 5.5 %fusion.8 = f32[256,2048]{1,0:T(8,128)S(1)} fusion(bf16[1792,4096]{1,0:T(8,128)(2,1)} %param.10, bf16[256,896]{1,0:T(8,128)(2,1)S(1)} %collective-permute-done.8, bf16[128,896]{1,0:T(8,128)(2,1)S(1)} %fusion.39, bf16[128,896]{1,0:T(8,128)(2,1)S(1)} %fusion.41, pred[]{:T(512)S(6)} %eq.16), kind=kOutput, calls=%fused_computation.10 | convolution fusion | flops 1885011968 | bytes 10354689 | tf_op jit(solution)/shard_map/dot_general | solution.py:168
  133.4 2.1 %fusion.12 = f32[256,2048]{1,0:T(8,128)S(1)} fusion(bf16[1792,4096]{1,0:T(8,128)(2,1)S(1)} %bitcast.162, bf16[256,896]{1,0:T(8,128)(2,1)S(1)} %collective-permute-done.8, bf16[128,896]{1,0:T(8,128)(2,1)S(1)} %fusion.39, bf16[128,896]{1,0:T(8,128)(2,1)S(1)} %fusion.41, pred[]{:T(512)S(6)} %eq.16), kind=kOutput, calls=%fused_computation.14 | convolution fusion | flops 1885011968 | bytes 10354689 | tf_op jit(solution)/shard_map/dot_general | solution.py:168
  139.2 2.1 %fusion.10 = f32[256,2048]{1,0:T(8,128)S(1)} fusion(bf16[1792,4096]{1,0:T(8,128)(2,1)S(1)} %bitcast.162, bf16[256,896]{1,0:T(8,128)(2,1)S(1)} %collective-permute-done.13, bf16[128,896]{1,0:T(8,128)(2,1)S(1)} %fusion.35, bf16[128,896]{1,0:T(8,128)(2,1)S(1)} %fusion.37, pred[]{:T(512)S(6)} %eq.16), kind=kOutput, calls=%fused_computation.12 | convolution fusion | flops 1885011968 | bytes 10354689 | tf_op jit(solution)/shard_map/dot_general | solution.py:168
  141.5 4.4 %collective-permute-done.11 = bf16[2,2,2,16,2048]{4,3,0,1,2:T(8,128)(2,1)S(1)} collective-permute-done((bf16[2,2,2,16,2048]{4,3,0,1,2:T(8,128)(2,1)S(1)}, bf16[2,2,2,16,2048]{4,3,0,1,2:T(8,128)(2,1)S(1)}, u32[]{:S(2)}, u32[]{:S(2)}) %collective-permute-start.11) | collective-permute-done | bytes 524320 | tf_op jit(solution)/shard_map/ppermute | solution.py:24
  147.8 2.6 %collective-permute-done.9 = bf16[2,2,2,16,2048]{4,3,0,1,2:T(8,128)(2,1)S(1)} collective-permute-done((bf16[2,2,2,16,2048]{4,3,0,1,2:T(8,128)(2,1)S(1)}, bf16[2,2,2,16,2048]{4,3,0,1,2:T(8,128)(2,1)S(1)}, u32[]{:S(2)}, u32[]{:S(2)}) %collective-permute-start.9) | collective-permute-done | bytes 524320 | tf_op jit(solution)/shard_map/ppermute | solution.py:24
  156.1 3.8 %collective-permute-done.10 = bf16[2,2,16,2048]{3,2,0,1:T(8,128)(2,1)S(1)} collective-permute-done((bf16[2,2,16,2048]{3,2,0,1:T(8,128)(2,1)S(1)}, bf16[2,2,16,2048]{3,2,0,1:T(8,128)(2,1)S(1)}, u32[]{:S(2)}, u32[]{:S(2)}) %collective-permute-start.10) | collective-permute-done | bytes 262176 | tf_op jit(solution)/shard_map/ppermute | solution.py:24
  160.0 6.5 %collective-permute-done.14 = bf16[2,2,2,16,2048]{4,3,0,1,2:T(8,128)(2,1)S(1)} collective-permute-done((bf16[2,2,2,16,2048]{4,3,0,1,2:T(8,128)(2,1)S(1)}, bf16[2,2,2,16,2048]{4,3,0,1,2:T(8,128)(2,1)S(1)}, u32[]{:S(2)}, u32[]{:S(2)}) %collective-permute-start.14) | collective-permute-done | bytes 524320 | tf_op jit(solution)/shard_map/ppermute | solution.py:24
  171.8 2.5 %collective-permute-done.18 = bf16[2,2,16,2048]{3,2,0,1:T(8,128)(2,1)S(1)} collective-permute-done((bf16[2,2,16,2048]{3,2,0,1:T(8,128)(2,1)S(1)}, bf16[2,2,16,2048]{3,2,0,1:T(8,128)(2,1)S(1)}, u32[]{:S(2)}, u32[]{:S(2)}) %collective-permute-start.18) | collective-permute-done | bytes 262176 | tf_op jit(solution)/shard_map/ppermute | solution.py:24
  177.9 2.9 %collective-permute-start.17 = (bf16[16,4096]{1,0:T(8,128)(2,1)S(1)}, bf16[16,4096]{1,0:T(8,128)(2,1)S(1)}, u32[]{:S(2)}, u32[]{:S(2)}) collective-permute-start(bf16[16,4096]{1,0:T(8,128)(2,1)S(1)} %fusion.92), channel_id=1, source_target_pairs={{0,16},{2,18},{4,20},{6,22},{8,24},{10,26},{12,28},{14,30},{16,0},... | collective-permute-start | bytes 393224 | tf_op jit(solution)/shard_map/ppermute | solution.py:24
  180.8 4.3 %collective-permute-done.20 = bf16[2,16,4096]{2,1,0:T(8,128)(2,1)S(1)} collective-permute-done((bf16[2,16,4096]{2,1,0:T(8,128)(2,1)S(1)}, bf16[2,16,4096]{2,1,0:T(8,128)(2,1)S(1)}, u32[]{:S(2)}, u32[]{:S(2)}) %collective-permute-start.20) | collective-permute-done | bytes 262176 | tf_op jit(solution)/shard_map/ppermute | solution.py:24
  186.4 6.2 %collective-permute-done.21 = bf16[16,4096]{1,0:T(8,128)(2,1)S(1)} collective-permute-done((bf16[16,4096]{1,0:T(8,128)(2,1)S(1)}, bf16[16,4096]{1,0:T(8,128)(2,1)S(1)}, u32[]{:S(2)}, u32[]{:S(2)}) %collective-permute-start.21) | collective-permute-done | bytes 131104 | tf_op jit(solution)/shard_map/ppermute | solution.py:24
  (130 shorter events, 47.7 us)
Async XLA Ops:
  4.4 50.7 %all-to-all-start = ((bf16[32,32,896]{2,1,0:T(8,128)(2,1)}), bf16[32,32,896]{2,1,0:T(8,128)(2,1)}, u32[]{:S(2)}, u32[]{:S(2)}) async-start(bf16[32,32,896]{2,1,0:T(8,128)(2,1)} %copy.49), calls=%async_computation | async-start | bytes 3670016 | tf_op jit(solution)/shard_map/all_to_all | solution.py:86
  16.5 1.4 collective-permute-start
  18.0 11.1 %collective-permute-start.1 = (f32[256,128]{0,1:T(8,128)S(1)}, f32[256,128]{0,1:T(8,128)S(1)}, u32[]{:S(2)}, u32[]{:S(2)}) collective-permute-start(f32[256,128]{0,1:T(8,128)S(1)} %bitcast_add_fusion.10), channel_id=1, source_target_pairs={{0,2},{2,0},{4,6},{6,4},{8,10},{10,8},{12,14},{14,12},{16,18},{18,... | collective-permute-start | bytes 393224 | tf_op jit(solution)/shard_map/ppermute | solution.py:24
  29.1 21.6 %collective-permute-start.2 = (f32[256,128]{0,1:T(8,128)S(1)}, f32[256,128]{0,1:T(8,128)S(1)}, u32[]{:S(2)}, u32[]{:S(2)}) collective-permute-start(f32[256,128]{0,1:T(8,128)S(1)} %add.211), channel_id=1, source_target_pairs={{0,4},{2,6},{4,0},{6,2},{8,12},{10,14},{12,8},{14,10},{16,20},{18,... | collective-permute-start | bytes 393224 | tf_op jit(solution)/shard_map/ppermute | solution.py:24
  55.1 5.0 %collective-permute-start.3 = (f32[256,128]{0,1:T(8,128)S(1)}, f32[256,128]{0,1:T(8,128)S(1)}, u32[]{:S(2)}, u32[]{:S(2)}) collective-permute-start(f32[256,128]{0,1:T(8,128)S(1)} %add.212), channel_id=1, source_target_pairs={{0,8},{2,10},{4,12},{6,14},{8,0},{10,2},{12,4},{14,6},{16,24},{18,... | collective-permute-start | bytes 393224 | tf_op jit(solution)/shard_map/ppermute | solution.py:24
  60.1 8.3 %collective-permute-start.4 = (f32[256,128]{0,1:T(8,128)S(1)}, f32[256,128]{0,1:T(8,128)S(1)}, u32[]{:S(2)}, u32[]{:S(2)}) collective-permute-start(f32[256,128]{0,1:T(8,128)S(1)} %add.213), channel_id=1, source_target_pairs={{0,16},{2,18},{4,20},{6,22},{8,24},{10,26},{12,28},{14,30},{16,0},... | collective-permute-start | bytes 393224 | tf_op jit(solution)/shard_map/ppermute | solution.py:24
  68.4 1.4 collective-permute-start.5
  71.7 49.2 %all-to-all-start.1 = ((bf16[32,32,896]{2,1,0:T(8,128)(2,1)}), bf16[32,32,896]{2,1,0:T(8,128)(2,1)S(1)}, u32[]{:S(2)}, u32[]{:S(2)}) async-start(bf16[32,32,896]{2,1,0:T(8,128)(2,1)} %copy.50), calls=%async_computation.1 | async-start | bytes 3670016 | tf_op jit(solution)/shard_map/all_to_all | solution.py:86
  101.6 12.0 %collective-permute-start.7 = (f32[512,896]{1,0:T(8,128)}, f32[512,896]{1,0:T(8,128)}, u32[]{:S(2)}, u32[]{:S(2)}) collective-permute-start(f32[512,896]{1,0:T(8,128)} %slice_select_fusion), channel_id=1, source_target_pairs={{0,1},{1,0},{2,3},{3,2},{4,5},{5,4},{6,7},{7,6},{8,9},{9,8},{10,11... | collective-permute-start | bytes 5505032 | tf_op jit(solution)/shard_map/ppermute | solution.py:24
  103.9 13.9 %collective-permute-start.6 = (f32[512,896]{1,0:T(8,128)}, f32[512,896]{1,0:T(8,128)}, u32[]{:S(2)}, u32[]{:S(2)}) collective-permute-start(f32[512,896]{1,0:T(8,128)} %slice_select_fusion.1), channel_id=1, source_target_pairs={{0,1},{1,0},{2,3},{3,2},{4,5},{5,4},{6,7},{7,6},{8,9},{9,8},{10,11... | collective-permute-start | bytes 5505032 | tf_op jit(solution)/shard_map/ppermute | solution.py:24
  124.2 1.9 collective-permute-start.8
  125.8 11.3 %collective-permute-start.13 = (bf16[256,896]{1,0:T(8,128)(2,1)S(1)}, bf16[256,896]{1,0:T(8,128)(2,1)S(1)}, u32[]{:S(2)}, u32[]{:S(2)}) collective-permute-start(bf16[256,896]{1,0:T(8,128)(2,1)S(1)} %pad_maximum_fusion.1), channel_id=1, source_target_pairs={{0,1},{1,0},{2,3},{3,2},{4,5},{5,4},{6,7},{7,6},{8,9},{9,8},{10,11... | collective-permute-start | bytes 1376264 | tf_op jit(solution)/shard_map/ppermute | solution.py:24
  131.7 14.2 %collective-permute-start.11 = (bf16[2,2,2,16,2048]{4,3,0,1,2:T(8,128)(2,1)S(1)}, bf16[2,2,2,16,2048]{4,3,0,1,2:T(8,128)(2,1)S(1)}, u32[]{:S(2)}, u32[]{:S(2)}) collective-permute-start(bf16[2,2,2,16,2048]{4,3,0,1,2:T(8,128)(2,1)S(1)} %fusion.21), channel_id=1, source_target_pairs={{0,4},{2,6},{4,0},{6,2},{8,12},{10,14},{12,8},{14,10},{16,20},{18,... | collective-permute-start | bytes 1572872 | tf_op jit(solution)/shard_map/ppermute | solution.py:24
  135.6 14.8 %collective-permute-start.9 = (bf16[2,2,2,16,2048]{4,3,0,1,2:T(8,128)(2,1)S(1)}, bf16[2,2,2,16,2048]{4,3,0,1,2:T(8,128)(2,1)S(1)}, u32[]{:S(2)}, u32[]{:S(2)}) collective-permute-start(bf16[2,2,2,16,2048]{4,3,0,1,2:T(8,128)(2,1)S(1)} %fusion.20), channel_id=1, source_target_pairs={{0,2},{2,0},{4,6},{6,4},{8,10},{10,8},{12,14},{14,12},{16,18},{18,... | collective-permute-start | bytes 1572872 | tf_op jit(solution)/shard_map/ppermute | solution.py:24
  146.0 10.0 %collective-permute-start.12 = (bf16[2,2,16,2048]{3,2,0,1:T(8,128)(2,1)S(1)}, bf16[2,2,16,2048]{3,2,0,1:T(8,128)(2,1)S(1)}, u32[]{:S(2)}, u32[]{:S(2)}) collective-permute-start(bf16[2,2,16,2048]{3,2,0,1:T(8,128)(2,1)S(1)} %fusion.43), channel_id=1, source_target_pairs={{0,2},{2,0},{4,6},{6,4},{8,10},{10,8},{12,14},{14,12},{16,18},{18,... | collective-permute-start | bytes 786440 | tf_op jit(solution)/shard_map/ppermute | solution.py:24
  150.6 9.3 %collective-permute-start.10 = (bf16[2,2,16,2048]{3,2,0,1:T(8,128)(2,1)S(1)}, bf16[2,2,16,2048]{3,2,0,1:T(8,128)(2,1)S(1)}, u32[]{:S(2)}, u32[]{:S(2)}) collective-permute-start(bf16[2,2,16,2048]{3,2,0,1:T(8,128)(2,1)S(1)} %fusion.42), channel_id=1, source_target_pairs={{0,4},{2,6},{4,0},{6,2},{8,12},{10,14},{12,8},{14,10},{16,20},{18,... | collective-permute-start | bytes 786440 | tf_op jit(solution)/shard_map/ppermute | solution.py:24
  150.6 15.8 %collective-permute-start.14 = (bf16[2,2,2,16,2048]{4,3,0,1,2:T(8,128)(2,1)S(1)}, bf16[2,2,2,16,2048]{4,3,0,1,2:T(8,128)(2,1)S(1)}, u32[]{:S(2)}, u32[]{:S(2)}) collective-permute-start(bf16[2,2,2,16,2048]{4,3,0,1,2:T(8,128)(2,1)S(1)} %fusion.22), channel_id=1, source_target_pairs={{0,2},{2,0},{4,6},{6,4},{8,10},{10,8},{12,14},{14,12},{16,18},{18,... | collective-permute-start | bytes 1572872 | tf_op jit(solution)/shard_map/ppermute | solution.py:24
  152.2 16.5 %collective-permute-start.15 = (bf16[2,2,2,16,2048]{4,3,0,1,2:T(8,128)(2,1)S(1)}, bf16[2,2,2,16,2048]{4,3,0,1,2:T(8,128)(2,1)S(1)}, u32[]{:S(2)}, u32[]{:S(2)}) collective-permute-start(bf16[2,2,2,16,2048]{4,3,0,1,2:T(8,128)(2,1)S(1)} %fusion.23), channel_id=1, source_target_pairs={{0,4},{2,6},{4,0},{6,2},{8,12},{10,14},{12,8},{14,10},{16,20},{18,... | collective-permute-start | bytes 1572872 | tf_op jit(solution)/shard_map/ppermute | solution.py:24
  166.7 7.6 %collective-permute-start.18 = (bf16[2,2,16,2048]{3,2,0,1:T(8,128)(2,1)S(1)}, bf16[2,2,16,2048]{3,2,0,1:T(8,128)(2,1)S(1)}, u32[]{:S(2)}, u32[]{:S(2)}) collective-permute-start(bf16[2,2,16,2048]{3,2,0,1:T(8,128)(2,1)S(1)} %fusion.44), channel_id=1, source_target_pairs={{0,4},{2,6},{4,0},{6,2},{8,12},{10,14},{12,8},{14,10},{16,20},{18,... | collective-permute-start | bytes 786440 | tf_op jit(solution)/shard_map/ppermute | solution.py:24
  168.8 6.4 %collective-permute-start.19 = (bf16[2,2,16,2048]{3,2,0,1:T(8,128)(2,1)S(1)}, bf16[2,2,16,2048]{3,2,0,1:T(8,128)(2,1)S(1)}, u32[]{:S(2)}, u32[]{:S(2)}) collective-permute-start(bf16[2,2,16,2048]{3,2,0,1:T(8,128)(2,1)S(1)} %fusion.45), channel_id=1, source_target_pairs={{0,2},{2,0},{4,6},{6,4},{8,10},{10,8},{12,14},{14,12},{16,18},{18,... | collective-permute-start | bytes 786440 | tf_op jit(solution)/shard_map/ppermute | solution.py:24
  170.3 7.5 %collective-permute-start.16 = (bf16[2,16,4096]{2,1,0:T(8,128)(2,1)S(1)}, bf16[2,16,4096]{2,1,0:T(8,128)(2,1)S(1)}, u32[]{:S(2)}, u32[]{:S(2)}) collective-permute-start(bf16[2,16,4096]{2,1,0:T(8,128)(2,1)S(1)} %fusion.46), channel_id=1, source_target_pairs={{0,8},{2,10},{4,12},{6,14},{8,0},{10,2},{12,4},{14,6},{16,24},{18,... | collective-permute-start | bytes 786440 | tf_op jit(solution)/shard_map/ppermute | solution.py:24
  175.3 9.8 %collective-permute-start.20 = (bf16[2,16,4096]{2,1,0:T(8,128)(2,1)S(1)}, bf16[2,16,4096]{2,1,0:T(8,128)(2,1)S(1)}, u32[]{:S(2)}, u32[]{:S(2)}) collective-permute-start(bf16[2,16,4096]{2,1,0:T(8,128)(2,1)S(1)} %fusion.47), channel_id=1, source_target_pairs={{0,8},{2,10},{4,12},{6,14},{8,0},{10,2},{12,4},{14,6},{16,24},{18,... | collective-permute-start | bytes 786440 | tf_op jit(solution)/shard_map/ppermute | solution.py:24
  177.9 8.3 %collective-permute-start.17 = (bf16[16,4096]{1,0:T(8,128)(2,1)S(1)}, bf16[16,4096]{1,0:T(8,128)(2,1)S(1)}, u32[]{:S(2)}, u32[]{:S(2)}) collective-permute-start(bf16[16,4096]{1,0:T(8,128)(2,1)S(1)} %fusion.92), channel_id=1, source_target_pairs={{0,16},{2,18},{4,20},{6,22},{8,24},{10,26},{12,28},{14,30},{16,0},... | collective-permute-start | bytes 393224 | tf_op jit(solution)/shard_map/ppermute | solution.py:24
  185.2 7.4 %collective-permute-start.21 = (bf16[16,4096]{1,0:T(8,128)(2,1)S(1)}, bf16[16,4096]{1,0:T(8,128)(2,1)S(1)}, u32[]{:S(2)}, u32[]{:S(2)}) collective-permute-start(bf16[16,4096]{1,0:T(8,128)(2,1)S(1)} %fusion.93), channel_id=1, source_target_pairs={{0,16},{2,18},{4,20},{6,22},{8,24},{10,26},{12,28},{14,30},{16,0},... | collective-permute-start | bytes 393224 | tf_op jit(solution)/shard_map/ppermute | solution.py:24
  (15 other events, 121.2 us)

commit v5 on v4

--- a/solution.py
+++ b/solution.py
@@ -110,7 +110,10 @@
 
     weights = after(gate_up_weight, outgoing[0])
     weights = jnp.transpose(weights, (1, 0, 2))
-    shrunk, weights, _ = lax.optimization_barrier((shrunk, weights, pages[0]))
+    block_slots = [[slots[step, block] for block in range(NBLK)] for step in range(steps)]
+    shrunk, weights, block_slots, _ = lax.optimization_barrier(
+        (shrunk, weights, block_slots, pages[0])
+    )
     shrunk = sum_over(shrunk, range(middle, bits_of("pool")))
     shrunk = gather(shrunk, "tensor", 0)
     for kind in range(1, kinds):
@@ -129,9 +132,16 @@
         if tensor_count == 2:
             low_share, high_share = product[:, :units_here], product[:, units_here:]
             got = swap(jnp.where(core == 0, high_share, low_share), "tensor", 0)
-            main.append(jnp.where(core == 0, low_share, high_share) + got)
+            step_rows = [slice(s * total_rows, (s + 1) * total_rows) for s in range(steps)]
+            main.append(
+                [
+                    jnp.where(core == 0, low_share[rows], high_share[rows]) + got[rows]
+                    for rows in step_rows
+                ]
+            )
         else:
-            main.append(scatter_sum(product, "tensor", 1))
+            whole = scatter_sum(product, "tensor", 1)
+            main.append([whole[s * total_rows : (s + 1) * total_rows] for s in range(steps)])
 
     high = shrunk.astype(jnp.bfloat16)
     low = (shrunk - high.astype(jnp.float32)).astype(jnp.bfloat16)
@@ -146,12 +156,12 @@
         hidden_blocks = []
         for block in range(NBLK):
             page = [
-                lax.dynamic_index_in_dim(one, slots[step, block], 0, keepdims=False)
+                lax.dynamic_index_in_dim(one, block_slots[step][block], 0, keepdims=False)
                 for one in pages
             ]
             rows = slice(step * total_rows + block * BLK, step * total_rows + (block + 1) * BLK)
             gate, up = [
-                main[kind][rows]
+                main[kind][step][block * BLK : (block + 1) * BLK]
                 + jnp.dot(
                     jnp.concatenate(
                         [part[rows, kind * rank : (kind + 1) * rank] for part in (high, low)], axis=1

time: 194 us -> 194 us (level)
  transfers between devices with their start and end apart: 24 -> 24, of which waited for: 17 -> 16; matrix products, arithmetic and copies ran while one was open for 39% -> 39% of each run, Pallas kernels for 0% -> 0%
where the time goes in v5:
time: 194 us
  waiting for transfers between devices  63.1 us (33%)
  matrix products  41.5 us (21%)
  starting transfers between devices  35.6 us (18%)
  local copies, waits for them, and re-layouts  32.7 us (17%)
  other arithmetic  12.6 us (6%)
  between operations  8.34 us (4%)
    ppermute x22, waiting for transfers between devices, swap(): return lax.ppermute(array, axis_name, bit_pairs(axis_name, bit))  59.4 us
    ppermute x22, starting transfers between devices, swap(): return lax.ppermute(array, axis_name, bit_pairs(axis_name, bit))  23.8 us
    dot_general x2, matrix products, shards(): jnp.dot(flat_tokens, weights[kind], preferred_element_type=jnp.float32)  23.7 us
    optimization_barrier x2, local copies, waits for them, and re-layouts, after(): return lax.optimization_barrier((array, arrived))[0]  22.2 us
    all_to_all x2, starting transfers between devices, exchange_columns(): lax.all_to_all(columns, ('pool', 'tensor'), split_axis=0, concat_axis=0,...  11.9 us
    dot_general x4, matrix products, shards(): jnp.dot(hidden, down_weight[:, piece * half:(piece + 1) * half], preferre...  11.8 us
    add x2, other arithmetic, shards(): jnp.where(core == 0, low_share[rows], high_share[rows]) + got[rows]  6.99 us
  transfers between devices with their start and end apart: 24, of which 16 were waited for; matrix products, arithmetic and copies ran while one was open for 39% of the time, Pallas kernels for 0%

profile of v5, /device:TPU:0, one launch (start us, length us, event | category | flops | bytes accessed | tf_op | source)
XLA Modules:
  0.0 193.9 jit_solution(13652401257237860720)
XLA Ops:
  0.0 2.4 %fusion.128 = (bf16[1,1,32,28672]{3,2,1,0:T(8,128)(2,1)S(1)}, bf16[1,1,32,28672]{3,2,1,0:T(8,128)(2,1)S(1)}) fusion(bf16[1,2,32,28672]{3,2,1,0:T(8,128)(2,1)} %param.12), kind=kLoop, calls=%fused_computation.205 | loop fusion | bytes 7340032 | tf_op jit(solution)/shard_map/slice | solution.py:82
  4.4 7.4 %all-to-all-start = ((bf16[32,32,896]{2,1,0:T(8,128)(2,1)}), bf16[32,32,896]{2,1,0:T(8,128)(2,1)}, u32[]{:S(2)}, u32[]{:S(2)}) async-start(bf16[32,32,896]{2,1,0:T(8,128)(2,1)} %copy.49), calls=%async_computation | async-start | bytes 3670016 | tf_op jit(solution)/shard_map/all_to_all | solution.py:86
  12.8 3.7 %fusion.16 = f32[2,256,2,64]{1,3,2,0:T(8,128)S(1)} fusion(bf16[2,256,4096]{2,1,0:T(8,128)(2,1)} %param.8, bf16[1,2,4096,64]{2,3,1,0:T(8,128)(2,1)S(1)} %copy-done, f32[2,256]{1,0:T(2,128)S(1)} %bitcast.160), kind=kOutput, calls=%fused_computation.28 | convolution fusion | flops 536936448 | bytes 5507072 | tf_op jit(solution)/shard_map/snd,kdc->snkc/dot_general | solution.py:92
  19.7 9.3 %collective-permute-done.1 = f32[256,128]{0,1:T(8,128)S(1)} collective-permute-done((f32[256,128]{0,1:T(8,128)S(1)}, f32[256,128]{0,1:T(8,128)S(1)}, u32[]{:S(2)}, u32[]{:S(2)}) %collective-permute-start.1) | collective-permute-done | bytes 131104 | tf_op jit(solution)/shard_map/ppermute | solution.py:24
  30.3 20.4 %copy.85 = bf16[4096,2,1792]{2,0,1:T(8,128)(2,1)} copy(bf16[4096,2,1792]{2,1,0:T(2,128)(2,1)} %param.9) | data formatting | bytes 58720256 | tf_op jit(solution)/shard_map/optimization_barrier | solution.py:55
  51.4 3.7 %all-to-all-done = bf16[32,32,896]{2,1,0:T(8,128)(2,1)} async-done(((bf16[32,32,896]{2,1,0:T(8,128)(2,1)}), bf16[32,32,896]{2,1,0:T(8,128)(2,1)}, u32[]{:S(2)}, u32[]{:S(2)}) %all-to-all-start) | async-done | bytes 1835040 | tf_op jit(solution)/shard_map/all_to_all | solution.py:86
  55.1 5.0 %collective-permute-done.3 = f32[256,128]{0,1:T(8,128)S(1)} collective-permute-done((f32[256,128]{0,1:T(8,128)S(1)}, f32[256,128]{0,1:T(8,128)S(1)}, u32[]{:S(2)}, u32[]{:S(2)}) %collective-permute-start.3) | collective-permute-done | bytes 131104 | tf_op jit(solution)/shard_map/ppermute | solution.py:24
  61.9 6.6 %collective-permute-done.4 = f32[256,128]{0,1:T(8,128)S(1)} collective-permute-done((f32[256,128]{0,1:T(8,128)S(1)}, f32[256,128]{0,1:T(8,128)S(1)}, u32[]{:S(2)}, u32[]{:S(2)}) %collective-permute-start.4) | collective-permute-done | bytes 131104 | tf_op jit(solution)/shard_map/ppermute | solution.py:24
  71.8 4.5 %all-to-all-start.1 = ((bf16[32,32,896]{2,1,0:T(8,128)(2,1)}), bf16[32,32,896]{2,1,0:T(8,128)(2,1)S(1)}, u32[]{:S(2)}, u32[]{:S(2)}) async-start(bf16[32,32,896]{2,1,0:T(8,128)(2,1)} %copy.50), calls=%async_computation.1 | async-start | bytes 3670016 | tf_op jit(solution)/shard_map/all_to_all | solution.py:86
  76.3 11.8 %fusion = f32[512,1792]{1,0:T(8,128)S(1)} fusion(bf16[512,4096]{1,0:T(8,128)(2,1)} %bitcast.163, bf16[2,4096,1792]{2,1,0:T(8,128)(2,1)} %bitcast.143), kind=kOutput, calls=%fused_computation.2 | convolution fusion | flops 7516192768 | bytes 22544384 | tf_op jit(solution)/shard_map/dot_general | solution.py:126
  88.1 11.9 %fusion.2 = f32[512,1792]{1,0:T(8,128)S(1)} fusion(bf16[512,4096]{1,0:T(8,128)(2,1)S(1)} %bitcast.164, bf16[2,4096,1792]{2,1,0:T(8,128)(2,1)} %bitcast.144), kind=kOutput, calls=%fused_computation.4 | convolution fusion | flops 7516192768 | bytes 22544384 | tf_op jit(solution)/shard_map/dot_general | solution.py:126
  114.5 3.9 %slice_add_fusion.3 = (f32[256,896]{1,0:T(8,128)}, f32[256,896]{1,0:T(8,128)S(1)}) fusion(f32[512,896]{1,0:T(8,128)} %collective-permute-done.6, f32[512,1792]{1,0:T(8,128)} %copy-done.5, pred[]{:T(512)S(6)} %eq.17), kind=kLoop, calls=%fused_computation.41 | loop fusion | flops 917504 | bytes 7340033 | tf_op jit(solution)/shard_map/add | solution.py:138
  118.4 3.1 %slice_add_fusion.2 = (f32[256,896]{1,0:T(8,128)}, f32[256,896]{1,0:T(8,128)}) fusion(f32[512,896]{1,0:T(8,128)} %collective-permute-done.7, f32[512,1792]{1,0:T(8,128)S(1)} %copy-done.4, pred[]{:T(512)S(6)} %eq.17), kind=kLoop, calls=%fused_computation.40 | loop fusion | flops 917504 | bytes 7340033 | tf_op jit(solution)/shard_map/add | solution.py:138
  125.8 5.5 %fusion.8 = f32[256,2048]{1,0:T(8,128)S(1)} fusion(bf16[1792,4096]{1,0:T(8,128)(2,1)} %param.10, bf16[256,896]{1,0:T(8,128)(2,1)S(1)} %collective-permute-done.8, bf16[128,896]{1,0:T(8,128)(2,1)S(1)} %fusion.39, bf16[128,896]{1,0:T(8,128)(2,1)S(1)} %fusion.41, pred[]{:T(512)S(6)} %eq.16), kind=kOutput, calls=%fused_computation.10 | convolution fusion | flops 1885011968 | bytes 10354689 | tf_op jit(solution)/shard_map/dot_general | solution.py:178
  133.1 2.1 %fusion.12 = f32[256,2048]{1,0:T(8,128)S(1)} fusion(bf16[1792,4096]{1,0:T(8,128)(2,1)S(1)} %bitcast.162, bf16[256,896]{1,0:T(8,128)(2,1)S(1)} %collective-permute-done.8, bf16[128,896]{1,0:T(8,128)(2,1)S(1)} %fusion.39, bf16[128,896]{1,0:T(8,128)(2,1)S(1)} %fusion.41, pred[]{:T(512)S(6)} %eq.16), kind=kOutput, calls=%fused_computation.14 | convolution fusion | flops 1885011968 | bytes 10354689 | tf_op jit(solution)/shard_map/dot_general | solution.py:178
  138.9 2.1 %fusion.10 = f32[256,2048]{1,0:T(8,128)S(1)} fusion(bf16[1792,4096]{1,0:T(8,128)(2,1)S(1)} %bitcast.162, bf16[256,896]{1,0:T(8,128)(2,1)S(1)} %collective-permute-done.13, bf16[128,896]{1,0:T(8,128)(2,1)S(1)} %fusion.35, bf16[128,896]{1,0:T(8,128)(2,1)S(1)} %fusion.37, pred[]{:T(512)S(6)} %eq.16), kind=kOutput, calls=%fused_computation.12 | convolution fusion | flops 1885011968 | bytes 10354689 | tf_op jit(solution)/shard_map/dot_general | solution.py:178
  141.2 4.4 %collective-permute-done.11 = bf16[2,2,2,16,2048]{4,3,0,1,2:T(8,128)(2,1)S(1)} collective-permute-done((bf16[2,2,2,16,2048]{4,3,0,1,2:T(8,128)(2,1)S(1)}, bf16[2,2,2,16,2048]{4,3,0,1,2:T(8,128)(2,1)S(1)}, u32[]{:S(2)}, u32[]{:S(2)}) %collective-permute-start.11) | collective-permute-done | bytes 524320 | tf_op jit(solution)/shard_map/ppermute | solution.py:24
  147.6 2.5 %collective-permute-done.9 = bf16[2,2,2,16,2048]{4,3,0,1,2:T(8,128)(2,1)S(1)} collective-permute-done((bf16[2,2,2,16,2048]{4,3,0,1,2:T(8,128)(2,1)S(1)}, bf16[2,2,2,16,2048]{4,3,0,1,2:T(8,128)(2,1)S(1)}, u32[]{:S(2)}, u32[]{:S(2)}) %collective-permute-start.9) | collective-permute-done | bytes 524320 | tf_op jit(solution)/shard_map/ppermute | solution.py:24
  155.8 3.8 %collective-permute-done.10 = bf16[2,2,16,2048]{3,2,0,1:T(8,128)(2,1)S(1)} collective-permute-done((bf16[2,2,16,2048]{3,2,0,1:T(8,128)(2,1)S(1)}, bf16[2,2,16,2048]{3,2,0,1:T(8,128)(2,1)S(1)}, u32[]{:S(2)}, u32[]{:S(2)}) %collective-permute-start.10) | collective-permute-done | bytes 262176 | tf_op jit(solution)/shard_map/ppermute | solution.py:24
  159.7 8.7 %collective-permute-done.15 = bf16[2,2,2,16,2048]{4,3,0,1,2:T(8,128)(2,1)S(1)} collective-permute-done((bf16[2,2,2,16,2048]{4,3,0,1,2:T(8,128)(2,1)S(1)}, bf16[2,2,2,16,2048]{4,3,0,1,2:T(8,128)(2,1)S(1)}, u32[]{:S(2)}, u32[]{:S(2)}) %collective-permute-start.15) | collective-permute-done | bytes 524320 | tf_op jit(solution)/shard_map/ppermute | solution.py:24
  172.4 2.7 %collective-permute-done.19 = bf16[2,2,16,2048]{3,2,0,1:T(8,128)(2,1)S(1)} collective-permute-done((bf16[2,2,16,2048]{3,2,0,1:T(8,128)(2,1)S(1)}, bf16[2,2,16,2048]{3,2,0,1:T(8,128)(2,1)S(1)}, u32[]{:S(2)}, u32[]{:S(2)}) %collective-permute-start.19) | collective-permute-done | bytes 262176 | tf_op jit(solution)/shard_map/ppermute | solution.py:24
  181.3 2.9 %collective-permute-done.20 = bf16[2,16,4096]{2,1,0:T(8,128)(2,1)S(1)} collective-permute-done((bf16[2,16,4096]{2,1,0:T(8,128)(2,1)S(1)}, bf16[2,16,4096]{2,1,0:T(8,128)(2,1)S(1)}, u32[]{:S(2)}, u32[]{:S(2)}) %collective-permute-start.20) | collective-permute-done | bytes 262176 | tf_op jit(solution)/shard_map/ppermute | solution.py:24
  184.4 2.4 %collective-permute-start.21 = (bf16[16,4096]{1,0:T(8,128)(2,1)S(1)}, bf16[16,4096]{1,0:T(8,128)(2,1)S(1)}, u32[]{:S(2)}, u32[]{:S(2)}) collective-permute-start(bf16[16,4096]{1,0:T(8,128)(2,1)S(1)} %fusion.93), channel_id=1, source_target_pairs={{0,16},{2,18},{4,20},{6,22},{8,24},{10,26},{12,28},{14,30},{16,0},... | collective-permute-start | bytes 393224 | tf_op jit(solution)/shard_map/ppermute | solution.py:24
  186.9 6.2 %collective-permute-done.21 = bf16[16,4096]{1,0:T(8,128)(2,1)S(1)} collective-permute-done((bf16[16,4096]{1,0:T(8,128)(2,1)S(1)}, bf16[16,4096]{1,0:T(8,128)(2,1)S(1)}, u32[]{:S(2)}, u32[]{:S(2)}) %collective-permute-start.21) | collective-permute-done | bytes 131104 | tf_op jit(solution)/shard_map/ppermute | solution.py:24
  (140 shorter events, 48.5 us)
Async XLA Ops:
  4.4 50.7 %all-to-all-start = ((bf16[32,32,896]{2,1,0:T(8,128)(2,1)}), bf16[32,32,896]{2,1,0:T(8,128)(2,1)}, u32[]{:S(2)}, u32[]{:S(2)}) async-start(bf16[32,32,896]{2,1,0:T(8,128)(2,1)} %copy.49), calls=%async_computation | async-start | bytes 3670016 | tf_op jit(solution)/shard_map/all_to_all | solution.py:86
  16.5 1.4 collective-permute-start
  18.0 11.1 %collective-permute-start.1 = (f32[256,128]{0,1:T(8,128)S(1)}, f32[256,128]{0,1:T(8,128)S(1)}, u32[]{:S(2)}, u32[]{:S(2)}) collective-permute-start(f32[256,128]{0,1:T(8,128)S(1)} %bitcast_add_fusion.10), channel_id=1, source_target_pairs={{0,2},{2,0},{4,6},{6,4},{8,10},{10,8},{12,14},{14,12},{16,18},{18,... | collective-permute-start | bytes 393224 | tf_op jit(solution)/shard_map/ppermute | solution.py:24
  29.1 22.3 %collective-permute-start.2 = (f32[256,128]{0,1:T(8,128)S(1)}, f32[256,128]{0,1:T(8,128)S(1)}, u32[]{:S(2)}, u32[]{:S(2)}) collective-permute-start(f32[256,128]{0,1:T(8,128)S(1)} %add.217), channel_id=1, source_target_pairs={{0,4},{2,6},{4,0},{6,2},{8,12},{10,14},{12,8},{14,10},{16,20},{18,... | collective-permute-start | bytes 393224 | tf_op jit(solution)/shard_map/ppermute | solution.py:24
  55.1 5.0 %collective-permute-start.3 = (f32[256,128]{0,1:T(8,128)S(1)}, f32[256,128]{0,1:T(8,128)S(1)}, u32[]{:S(2)}, u32[]{:S(2)}) collective-permute-start(f32[256,128]{0,1:T(8,128)S(1)} %add.218), channel_id=1, source_target_pairs={{0,8},{2,10},{4,12},{6,14},{8,0},{10,2},{12,4},{14,6},{16,24},{18,... | collective-permute-start | bytes 393224 | tf_op jit(solution)/shard_map/ppermute | solution.py:24
  60.1 8.3 %collective-permute-start.4 = (f32[256,128]{0,1:T(8,128)S(1)}, f32[256,128]{0,1:T(8,128)S(1)}, u32[]{:S(2)}, u32[]{:S(2)}) collective-permute-start(f32[256,128]{0,1:T(8,128)S(1)} %add.219), channel_id=1, source_target_pairs={{0,16},{2,18},{4,20},{6,22},{8,24},{10,26},{12,28},{14,30},{16,0},... | collective-permute-start | bytes 393224 | tf_op jit(solution)/shard_map/ppermute | solution.py:24
  68.5 1.4 collective-permute-start.5
  71.8 49.7 %all-to-all-start.1 = ((bf16[32,32,896]{2,1,0:T(8,128)(2,1)}), bf16[32,32,896]{2,1,0:T(8,128)(2,1)S(1)}, u32[]{:S(2)}, u32[]{:S(2)}) async-start(bf16[32,32,896]{2,1,0:T(8,128)(2,1)} %copy.50), calls=%async_computation.1 | async-start | bytes 3670016 | tf_op jit(solution)/shard_map/all_to_all | solution.py:86
  102.3 12.2 %collective-permute-start.6 = (f32[512,896]{1,0:T(8,128)}, f32[512,896]{1,0:T(8,128)}, u32[]{:S(2)}, u32[]{:S(2)}) collective-permute-start(f32[512,896]{1,0:T(8,128)} %slice_select_fusion.1), channel_id=1, source_target_pairs={{0,1},{1,0},{2,3},{3,2},{4,5},{5,4},{6,7},{7,6},{8,9},{9,8},{10,11... | collective-permute-start | bytes 5505032 | tf_op jit(solution)/shard_map/ppermute | solution.py:24
  104.0 14.4 %collective-permute-start.7 = (f32[512,896]{1,0:T(8,128)}, f32[512,896]{1,0:T(8,128)}, u32[]{:S(2)}, u32[]{:S(2)}) collective-permute-start(f32[512,896]{1,0:T(8,128)} %slice_select_fusion), channel_id=1, source_target_pairs={{0,1},{1,0},{2,3},{3,2},{4,5},{5,4},{6,7},{7,6},{8,9},{9,8},{10,11... | collective-permute-start | bytes 5505032 | tf_op jit(solution)/shard_map/ppermute | solution.py:24
  123.7 2.1 %collective-permute-start.8 = (bf16[256,896]{1,0:T(8,128)(2,1)S(1)}, bf16[256,896]{1,0:T(8,128)(2,1)S(1)}, u32[]{:S(2)}, u32[]{:S(2)}) collective-permute-start(bf16[256,896]{1,0:T(8,128)(2,1)S(1)} %pad_maximum_fusion), channel_id=1, source_target_pairs={{0,1},{1,0},{2,3},{3,2},{4,5},{5,4},{6,7},{7,6},{8,9},{9,8},{10,11... | collective-permute-start | bytes 1376264 | tf_op jit(solution)/shard_map/ppermute | solution.py:24
  125.5 11.3 %collective-permute-start.13 = (bf16[256,896]{1,0:T(8,128)(2,1)S(1)}, bf16[256,896]{1,0:T(8,128)(2,1)S(1)}, u32[]{:S(2)}, u32[]{:S(2)}) collective-permute-start(bf16[256,896]{1,0:T(8,128)(2,1)S(1)} %pad_maximum_fusion.1), channel_id=1, source_target_pairs={{0,1},{1,0},{2,3},{3,2},{4,5},{5,4},{6,7},{7,6},{8,9},{9,8},{10,11... | collective-permute-start | bytes 1376264 | tf_op jit(solution)/shard_map/ppermute | solution.py:24
  131.4 14.3 %collective-permute-start.11 = (bf16[2,2,2,16,2048]{4,3,0,1,2:T(8,128)(2,1)S(1)}, bf16[2,2,2,16,2048]{4,3,0,1,2:T(8,128)(2,1)S(1)}, u32[]{:S(2)}, u32[]{:S(2)}) collective-permute-start(bf16[2,2,2,16,2048]{4,3,0,1,2:T(8,128)(2,1)S(1)} %fusion.21), channel_id=1, source_target_pairs={{0,4},{2,6},{4,0},{6,2},{8,12},{10,14},{12,8},{14,10},{16,20},{18,... | collective-permute-start | bytes 1572872 | tf_op jit(solution)/shard_map/ppermute | solution.py:24
  135.3 14.8 %collective-permute-start.9 = (bf16[2,2,2,16,2048]{4,3,0,1,2:T(8,128)(2,1)S(1)}, bf16[2,2,2,16,2048]{4,3,0,1,2:T(8,128)(2,1)S(1)}, u32[]{:S(2)}, u32[]{:S(2)}) collective-permute-start(bf16[2,2,2,16,2048]{4,3,0,1,2:T(8,128)(2,1)S(1)} %fusion.20), channel_id=1, source_target_pairs={{0,2},{2,0},{4,6},{6,4},{8,10},{10,8},{12,14},{14,12},{16,18},{18,... | collective-permute-start | bytes 1572872 | tf_op jit(solution)/shard_map/ppermute | solution.py:24
  145.8 9.9 %collective-permute-start.12 = (bf16[2,2,16,2048]{3,2,0,1:T(8,128)(2,1)S(1)}, bf16[2,2,16,2048]{3,2,0,1:T(8,128)(2,1)S(1)}, u32[]{:S(2)}, u32[]{:S(2)}) collective-permute-start(bf16[2,2,16,2048]{3,2,0,1:T(8,128)(2,1)S(1)} %fusion.43), channel_id=1, source_target_pairs={{0,2},{2,0},{4,6},{6,4},{8,10},{10,8},{12,14},{14,12},{16,18},{18,... | collective-permute-start | bytes 786440 | tf_op jit(solution)/shard_map/ppermute | solution.py:24
  150.3 9.3 %collective-permute-start.10 = (bf16[2,2,16,2048]{3,2,0,1:T(8,128)(2,1)S(1)}, bf16[2,2,16,2048]{3,2,0,1:T(8,128)(2,1)S(1)}, u32[]{:S(2)}, u32[]{:S(2)}) collective-permute-start(bf16[2,2,16,2048]{3,2,0,1:T(8,128)(2,1)S(1)} %fusion.42), channel_id=1, source_target_pairs={{0,4},{2,6},{4,0},{6,2},{8,12},{10,14},{12,8},{14,10},{16,20},{18,... | collective-permute-start | bytes 786440 | tf_op jit(solution)/shard_map/ppermute | solution.py:24
  150.4 18.1 %collective-permute-start.15 = (bf16[2,2,2,16,2048]{4,3,0,1,2:T(8,128)(2,1)S(1)}, bf16[2,2,2,16,2048]{4,3,0,1,2:T(8,128)(2,1)S(1)}, u32[]{:S(2)}, u32[]{:S(2)}) collective-permute-start(bf16[2,2,2,16,2048]{4,3,0,1,2:T(8,128)(2,1)S(1)} %fusion.23), channel_id=1, source_target_pairs={{0,4},{2,6},{4,0},{6,2},{8,12},{10,14},{12,8},{14,10},{16,20},{18,... | collective-permute-start | bytes 1572872 | tf_op jit(solution)/shard_map/ppermute | solution.py:24
  152.4 17.8 %collective-permute-start.14 = (bf16[2,2,2,16,2048]{4,3,0,1,2:T(8,128)(2,1)S(1)}, bf16[2,2,2,16,2048]{4,3,0,1,2:T(8,128)(2,1)S(1)}, u32[]{:S(2)}, u32[]{:S(2)}) collective-permute-start(bf16[2,2,2,16,2048]{4,3,0,1,2:T(8,128)(2,1)S(1)} %fusion.22), channel_id=1, source_target_pairs={{0,2},{2,0},{4,6},{6,4},{8,10},{10,8},{12,14},{14,12},{16,18},{18,... | collective-permute-start | bytes 1572872 | tf_op jit(solution)/shard_map/ppermute | solution.py:24
  168.6 6.4 %collective-permute-start.19 = (bf16[2,2,16,2048]{3,2,0,1:T(8,128)(2,1)S(1)}, bf16[2,2,16,2048]{3,2,0,1:T(8,128)(2,1)S(1)}, u32[]{:S(2)}, u32[]{:S(2)}) collective-permute-start(bf16[2,2,16,2048]{3,2,0,1:T(8,128)(2,1)S(1)} %fusion.45), channel_id=1, source_target_pairs={{0,2},{2,0},{4,6},{6,4},{8,10},{10,8},{12,14},{14,12},{16,18},{18,... | collective-permute-start | bytes 786440 | tf_op jit(solution)/shard_map/ppermute | solution.py:24
  170.3 6.4 %collective-permute-start.18 = (bf16[2,2,16,2048]{3,2,0,1:T(8,128)(2,1)S(1)}, bf16[2,2,16,2048]{3,2,0,1:T(8,128)(2,1)S(1)}, u32[]{:S(2)}, u32[]{:S(2)}) collective-permute-start(bf16[2,2,16,2048]{3,2,0,1:T(8,128)(2,1)S(1)} %fusion.44), channel_id=1, source_target_pairs={{0,4},{2,6},{4,0},{6,2},{8,12},{10,14},{12,8},{14,10},{16,20},{18,... | collective-permute-start | bytes 786440 | tf_op jit(solution)/shard_map/ppermute | solution.py:24
  170.9 8.9 %collective-permute-start.16 = (bf16[2,16,4096]{2,1,0:T(8,128)(2,1)S(1)}, bf16[2,16,4096]{2,1,0:T(8,128)(2,1)S(1)}, u32[]{:S(2)}, u32[]{:S(2)}) collective-permute-start(bf16[2,16,4096]{2,1,0:T(8,128)(2,1)S(1)} %fusion.46), channel_id=1, source_target_pairs={{0,8},{2,10},{4,12},{6,14},{8,0},{10,2},{12,4},{14,6},{16,24},{18,... | collective-permute-start | bytes 786440 | tf_op jit(solution)/shard_map/ppermute | solution.py:24
  176.9 7.4 %collective-permute-start.20 = (bf16[2,16,4096]{2,1,0:T(8,128)(2,1)S(1)}, bf16[2,16,4096]{2,1,0:T(8,128)(2,1)S(1)}, u32[]{:S(2)}, u32[]{:S(2)}) collective-permute-start(bf16[2,16,4096]{2,1,0:T(8,128)(2,1)S(1)} %fusion.47), channel_id=1, source_target_pairs={{0,8},{2,10},{4,12},{6,14},{8,0},{10,2},{12,4},{14,6},{16,24},{18,... | collective-permute-start | bytes 786440 | tf_op jit(solution)/shard_map/ppermute | solution.py:24
  179.9 6.9 %collective-permute-start.17 = (bf16[16,4096]{1,0:T(8,128)(2,1)S(1)}, bf16[16,4096]{1,0:T(8,128)(2,1)S(1)}, u32[]{:S(2)}, u32[]{:S(2)}) collective-permute-start(bf16[16,4096]{1,0:T(8,128)(2,1)S(1)} %fusion.92), channel_id=1, source_target_pairs={{0,16},{2,18},{4,20},{6,22},{8,24},{10,26},{12,28},{14,30},{16,0},... | collective-permute-start | bytes 393224 | tf_op jit(solution)/shard_map/ppermute | solution.py:24
  184.4 8.7 %collective-permute-start.21 = (bf16[16,4096]{1,0:T(8,128)(2,1)S(1)}, bf16[16,4096]{1,0:T(8,128)(2,1)S(1)}, u32[]{:S(2)}, u32[]{:S(2)}) collective-permute-start(bf16[16,4096]{1,0:T(8,128)(2,1)S(1)} %fusion.93), channel_id=1, source_target_pairs={{0,16},{2,18},{4,20},{6,22},{8,24},{10,26},{12,28},{14,30},{16,0},... | collective-permute-start | bytes 393224 | tf_op jit(solution)/shard_map/ppermute | solution.py:24
  (20 other events, 142.3 us)

commit v6 on v5

--- a/solution.py
+++ b/solution.py
@@ -12,7 +12,7 @@
 
 
 def halve(array, axis_name, bit, axis, wire=None):
-    mine = (lax.axis_index(axis_name) >> bit) & 1
+    mine = ((lax.axis_index(axis_name) >> bit) & 1).astype(jnp.uint32)
     keep = lax.dynamic_index_in_dim(array, mine, axis, keepdims=False)
     send = lax.dynamic_index_in_dim(array, 1 - mine, axis, keepdims=False)
     if wire is not None:
@@ -110,7 +110,8 @@
 
     weights = after(gate_up_weight, outgoing[0])
     weights = jnp.transpose(weights, (1, 0, 2))
-    block_slots = [[slots[step, block] for block in range(NBLK)] for step in range(steps)]
+    places = slots.astype(jnp.uint32)
+    block_slots = [[places[step, block] for block in range(NBLK)] for step in range(steps)]
     shrunk, weights, block_slots, _ = lax.optimization_barrier(
         (shrunk, weights, block_slots, pages[0])
     )

time: 194 us -> 193 us (level)
  waiting for transfers between devices: 63.1 us -> 72.4 us
  between operations: 8.34 us -> 0.61 us
  starting transfers between devices: 35.6 us -> 28.5 us
  local copies, waits for them, and re-layouts: 32.7 us -> 37.5 us
    ppermute x22, starting transfers between devices: 23.8 us -> 16.6 us  [swap(): return lax.ppermute(array, axis_name, bit_pairs(axis_name, bit))]
    ppermute x22, waiting for transfers between devices: 59.4 us -> 65.6 us  [swap(): return lax.ppermute(array, axis_name, bit_pairs(axis_name, bit))]
    squeeze x2, local copies, waits for them, and re-layouts: 1.16 us -> 6.5 us  [shards(): lax.dynamic_index_in_dim(one, block_slots[step][block], 0, keepdims=False)]
    all_to_all x2, waiting for transfers between devices: 3.71 us -> 6.75 us  [exchange_columns(): lax.all_to_all(columns, ('pool', 'tensor'), split_axis=0, concat_axis=0,...]
  transfers between devices with their start and end apart: 24 -> 24, of which waited for: 16 -> 18; matrix products, arithmetic and copies ran while one was open for 39% -> 41% of each run, Pallas kernels for 0% -> 0%
where the time goes in v6:
time: 193 us
  waiting for transfers between devices  72.4 us (38%)
  matrix products  41.4 us (21%)
  local copies, waits for them, and re-layouts  37.5 us (19%)
  starting transfers between devices  28.5 us (15%)
  other arithmetic  12.6 us (7%)
    ppermute x22, waiting for transfers between devices, swap(): return lax.ppermute(array, axis_name, bit_pairs(axis_name, bit))  65.6 us
    dot_general x2, matrix products, shards(): jnp.dot(flat_tokens, weights[kind], preferred_element_type=jnp.float32)  23.7 us
    optimization_barrier x2, local copies, waits for them, and re-layouts, after(): return lax.optimization_barrier((array, arrived))[0]  22.2 us
    ppermute x22, starting transfers between devices, swap(): return lax.ppermute(array, axis_name, bit_pairs(axis_name, bit))  16.6 us
    all_to_all x2, starting transfers between devices, exchange_columns(): lax.all_to_all(columns, ('pool', 'tensor'), split_axis=0, concat_axis=0,...  11.9 us
    dot_general x4, matrix products, shards(): jnp.dot(hidden, down_weight[:, piece * half:(piece + 1) * half], preferre...  11.7 us
    add x2, other arithmetic, shards(): jnp.where(core == 0, low_share[rows], high_share[rows]) + got[rows]  6.99 us
    all_to_all x2, waiting for transfers between devices, exchange_columns(): lax.all_to_all(columns, ('pool', 'tensor'), split_axis=0, concat_axis=0,...  6.75 us
  transfers between devices with their start and end apart: 24, of which 18 were waited for; matrix products, arithmetic and copies ran while one was open for 41% of the time, Pallas kernels for 0%

profile of v6, /device:TPU:0, one launch (start us, length us, event | category | flops | bytes accessed | tf_op | source)
XLA Modules:
  0.0 193.0 jit_solution(14125556042275966979)
XLA Ops:
  0.0 2.4 %fusion.128 = (bf16[1,1,32,28672]{3,2,1,0:T(8,128)(2,1)S(1)}, bf16[1,1,32,28672]{3,2,1,0:T(8,128)(2,1)S(1)}) fusion(bf16[1,2,32,28672]{3,2,1,0:T(8,128)(2,1)} %param.12), kind=kLoop, calls=%fused_computation.205 | loop fusion | bytes 7340032 | tf_op jit(solution)/shard_map/slice | solution.py:82
  4.4 7.4 %all-to-all-start = ((bf16[32,32,896]{2,1,0:T(8,128)(2,1)}), bf16[32,32,896]{2,1,0:T(8,128)(2,1)}, u32[]{:S(2)}, u32[]{:S(2)}) async-start(bf16[32,32,896]{2,1,0:T(8,128)(2,1)} %copy.49), calls=%async_computation | async-start | bytes 3670016 | tf_op jit(solution)/shard_map/all_to_all | solution.py:86
  12.8 3.7 %fusion.16 = f32[2,256,2,64]{1,3,2,0:T(8,128)S(1)} fusion(bf16[2,256,4096]{2,1,0:T(8,128)(2,1)} %param.8, bf16[1,2,4096,64]{2,3,1,0:T(8,128)(2,1)S(1)} %copy-done, f32[2,256]{1,0:T(2,128)S(1)} %bitcast.160), kind=kOutput, calls=%fused_computation.28 | convolution fusion | flops 536936448 | bytes 5507072 | tf_op jit(solution)/shard_map/snd,kdc->snkc/dot_general | solution.py:92
  19.7 9.3 %collective-permute-done.1 = f32[256,128]{0,1:T(8,128)S(1)} collective-permute-done((f32[256,128]{0,1:T(8,128)S(1)}, f32[256,128]{0,1:T(8,128)S(1)}, u32[]{:S(2)}, u32[]{:S(2)}) %collective-permute-start.1) | collective-permute-done | bytes 131104 | tf_op jit(solution)/shard_map/ppermute | solution.py:24
  30.4 20.4 %copy.85 = bf16[4096,2,1792]{2,0,1:T(8,128)(2,1)} copy(bf16[4096,2,1792]{2,1,0:T(2,128)(2,1)} %param.9) | data formatting | bytes 58720256 | tf_op jit(solution)/shard_map/optimization_barrier | solution.py:55
  51.5 3.6 %all-to-all-done = bf16[32,32,896]{2,1,0:T(8,128)(2,1)} async-done(((bf16[32,32,896]{2,1,0:T(8,128)(2,1)}), bf16[32,32,896]{2,1,0:T(8,128)(2,1)}, u32[]{:S(2)}, u32[]{:S(2)}) %all-to-all-start) | async-done | bytes 1835040 | tf_op jit(solution)/shard_map/all_to_all | solution.py:86
  55.1 5.0 %collective-permute-done.3 = f32[256,128]{0,1:T(8,128)S(1)} collective-permute-done((f32[256,128]{0,1:T(8,128)S(1)}, f32[256,128]{0,1:T(8,128)S(1)}, u32[]{:S(2)}, u32[]{:S(2)}) %collective-permute-start.3) | collective-permute-done | bytes 131104 | tf_op jit(solution)/shard_map/ppermute | solution.py:24
  61.9 6.5 %collective-permute-done.4 = f32[256,128]{0,1:T(8,128)S(1)} collective-permute-done((f32[256,128]{0,1:T(8,128)S(1)}, f32[256,128]{0,1:T(8,128)S(1)}, u32[]{:S(2)}, u32[]{:S(2)}) %collective-permute-start.4) | collective-permute-done | bytes 131104 | tf_op jit(solution)/shard_map/ppermute | solution.py:24
  71.8 4.5 %all-to-all-start.1 = ((bf16[32,32,896]{2,1,0:T(8,128)(2,1)}), bf16[32,32,896]{2,1,0:T(8,128)(2,1)S(1)}, u32[]{:S(2)}, u32[]{:S(2)}) async-start(bf16[32,32,896]{2,1,0:T(8,128)(2,1)} %copy.50), calls=%async_computation.1 | async-start | bytes 3670016 | tf_op jit(solution)/shard_map/all_to_all | solution.py:86
  76.3 11.8 %fusion = f32[512,1792]{1,0:T(8,128)S(1)} fusion(bf16[512,4096]{1,0:T(8,128)(2,1)} %bitcast.163, bf16[2,4096,1792]{2,1,0:T(8,128)(2,1)} %bitcast.143), kind=kOutput, calls=%fused_computation.2 | convolution fusion | flops 7516192768 | bytes 22544384 | tf_op jit(solution)/shard_map/dot_general | solution.py:127
  88.1 11.9 %fusion.2 = f32[512,1792]{1,0:T(8,128)S(1)} fusion(bf16[512,4096]{1,0:T(8,128)(2,1)S(1)} %bitcast.164, bf16[2,4096,1792]{2,1,0:T(8,128)(2,1)} %bitcast.144), kind=kOutput, calls=%fused_computation.4 | convolution fusion | flops 7516192768 | bytes 22544384 | tf_op jit(solution)/shard_map/dot_general | solution.py:127
  105.0 3.7 %dynamic-slice_bitcast_fusion.8 = (bf16[64,896]{1,0:T(8,128)(2,1)S(1)}, bf16[64,896]{1,0:T(8,128)(2,1)S(1)}, bf16[64,896]{1,0:T(8,128)(2,1)S(1)}, bf16[64,896]{1,0:T(8,128)(2,1)S(1)}) fusion(bf16[16,64,896]{2,1,0:T(8,128)(2,1)} %bitcast.13, u32[]{:T(128)} %bitcast.9, u32[]{:T(128)} %bitcast.12, u32[]{:T(128)} %bitcast.11, u32[]{:T(128)} %bitcast.10), kind=kLoop, calls=%fused_computation.146 | loop fusion | bytes 917520 | tf_op jit(solution)/shard_map/jit(dynamic_index_in_dim)/squeeze | solution.py:160
  109.4 3.9 %slice_add_fusion.3 = (f32[256,896]{1,0:T(8,128)}, f32[256,896]{1,0:T(8,128)S(1)}) fusion(f32[512,896]{1,0:T(8,128)} %collective-permute-done.6, f32[512,1792]{1,0:T(8,128)} %copy-done.5, pred[]{:T(512)S(6)} %eq.17), kind=kLoop, calls=%fused_computation.41 | loop fusion | flops 917504 | bytes 7340033 | tf_op jit(solution)/shard_map/add | solution.py:139
  113.3 3.1 %slice_add_fusion.2 = (f32[256,896]{1,0:T(8,128)}, f32[256,896]{1,0:T(8,128)}) fusion(f32[512,896]{1,0:T(8,128)} %collective-permute-done.7, f32[512,1792]{1,0:T(8,128)S(1)} %copy-done.4, pred[]{:T(512)S(6)} %eq.17), kind=kLoop, calls=%fused_computation.40 | loop fusion | flops 917504 | bytes 7340033 | tf_op jit(solution)/shard_map/add | solution.py:139
  116.4 3.1 %all-to-all-done.1 = bf16[32,32,896]{2,1,0:T(8,128)(2,1)S(1)} async-done(((bf16[32,32,896]{2,1,0:T(8,128)(2,1)}), bf16[32,32,896]{2,1,0:T(8,128)(2,1)S(1)}, u32[]{:S(2)}, u32[]{:S(2)}) %all-to-all-start.1) | async-done | bytes 1835040 | tf_op jit(solution)/shard_map/all_to_all | solution.py:86
  119.5 2.8 %dynamic-slice_bitcast_fusion.7 = (bf16[64,896]{1,0:T(8,128)(2,1)S(1)}, bf16[64,896]{1,0:T(8,128)(2,1)S(1)}, bf16[64,896]{1,0:T(8,128)(2,1)S(1)}, bf16[64,896]{1,0:T(8,128)(2,1)S(1)}) fusion(bf16[16,64,896]{2,1,0:T(8,128)(2,1)S(1)} %bitcast.149, u32[]{:T(128)} %bitcast.9, u32[]{:T(128)} %bitcast.12, u32[]{:T(128)} %bitcast.11, u32[]{:T(128)} %bitcast.10), kind=kLoop, calls=%fused_computation.145 | loop fusion | bytes 917520 | tf_op jit(solution)/shard_map/jit(dynamic_index_in_dim)/squeeze | solution.py:160
  125.5 5.4 %fusion.8 = f32[256,2048]{1,0:T(8,128)S(1)} fusion(bf16[1792,4096]{1,0:T(8,128)(2,1)} %param.10, bf16[256,896]{1,0:T(8,128)(2,1)S(1)} %collective-permute-done.8, bf16[128,896]{1,0:T(8,128)(2,1)S(1)} %fusion.39, bf16[128,896]{1,0:T(8,128)(2,1)S(1)} %fusion.41, pred[]{:T(512)S(6)} %eq.16), kind=kOutput, calls=%fused_computation.10 | convolution fusion | flops 1885011968 | bytes 10354689 | tf_op jit(solution)/shard_map/dot_general | solution.py:179
  140.6 4.8 %collective-permute-done.11 = bf16[2,2,2,16,2048]{4,3,0,1,2:T(8,128)(2,1)S(1)} collective-permute-done((bf16[2,2,2,16,2048]{4,3,0,1,2:T(8,128)(2,1)S(1)}, bf16[2,2,2,16,2048]{4,3,0,1,2:T(8,128)(2,1)S(1)}, u32[]{:S(2)}, u32[]{:S(2)}) %collective-permute-start.11) | collective-permute-done | bytes 524320 | tf_op jit(solution)/shard_map/ppermute | solution.py:24
  155.1 3.8 %collective-permute-done.10 = bf16[2,2,16,2048]{3,2,0,1:T(8,128)(2,1)S(1)} collective-permute-done((bf16[2,2,16,2048]{3,2,0,1:T(8,128)(2,1)S(1)}, bf16[2,2,16,2048]{3,2,0,1:T(8,128)(2,1)S(1)}, u32[]{:S(2)}, u32[]{:S(2)}) %collective-permute-start.10) | collective-permute-done | bytes 262176 | tf_op jit(solution)/shard_map/ppermute | solution.py:24
  159.0 9.0 %collective-permute-done.15 = bf16[2,2,2,16,2048]{4,3,0,1,2:T(8,128)(2,1)S(1)} collective-permute-done((bf16[2,2,2,16,2048]{4,3,0,1,2:T(8,128)(2,1)S(1)}, bf16[2,2,2,16,2048]{4,3,0,1,2:T(8,128)(2,1)S(1)}, u32[]{:S(2)}, u32[]{:S(2)}) %collective-permute-start.15) | collective-permute-done | bytes 524320 | tf_op jit(solution)/shard_map/ppermute | solution.py:24
  170.5 4.1 %collective-permute-done.19 = bf16[2,2,16,2048]{3,2,0,1:T(8,128)(2,1)S(1)} collective-permute-done((bf16[2,2,16,2048]{3,2,0,1:T(8,128)(2,1)S(1)}, bf16[2,2,16,2048]{3,2,0,1:T(8,128)(2,1)S(1)}, u32[]{:S(2)}, u32[]{:S(2)}) %collective-permute-start.19) | collective-permute-done | bytes 262176 | tf_op jit(solution)/shard_map/ppermute | solution.py:24
  176.6 2.5 %collective-permute-done.16 = bf16[2,16,4096]{2,1,0:T(8,128)(2,1)S(1)} collective-permute-done((bf16[2,16,4096]{2,1,0:T(8,128)(2,1)S(1)}, bf16[2,16,4096]{2,1,0:T(8,128)(2,1)S(1)}, u32[]{:S(2)}, u32[]{:S(2)}) %collective-permute-start.16) | collective-permute-done | bytes 262176 | tf_op jit(solution)/shard_map/ppermute | solution.py:24
  179.3 5.2 %collective-permute-done.20 = bf16[2,16,4096]{2,1,0:T(8,128)(2,1)S(1)} collective-permute-done((bf16[2,16,4096]{2,1,0:T(8,128)(2,1)S(1)}, bf16[2,16,4096]{2,1,0:T(8,128)(2,1)S(1)}, u32[]{:S(2)}, u32[]{:S(2)}) %collective-permute-start.20) | collective-permute-done | bytes 262176 | tf_op jit(solution)/shard_map/ppermute | solution.py:24
  184.9 5.3 %collective-permute-done.17 = bf16[16,4096]{1,0:T(8,128)(2,1)S(1)} collective-permute-done((bf16[16,4096]{1,0:T(8,128)(2,1)S(1)}, bf16[16,4096]{1,0:T(8,128)(2,1)S(1)}, u32[]{:S(2)}, u32[]{:S(2)}) %collective-permute-start.17) | collective-permute-done | bytes 131104 | tf_op jit(solution)/shard_map/ppermute | solution.py:24
  (142 shorter events, 49.1 us)
Async XLA Ops:
  4.4 50.7 %all-to-all-start = ((bf16[32,32,896]{2,1,0:T(8,128)(2,1)}), bf16[32,32,896]{2,1,0:T(8,128)(2,1)}, u32[]{:S(2)}, u32[]{:S(2)}) async-start(bf16[32,32,896]{2,1,0:T(8,128)(2,1)} %copy.49), calls=%async_computation | async-start | bytes 3670016 | tf_op jit(solution)/shard_map/all_to_all | solution.py:86
  16.5 1.4 collective-permute-start
  18.0 11.1 %collective-permute-start.1 = (f32[256,128]{0,1:T(8,128)S(1)}, f32[256,128]{0,1:T(8,128)S(1)}, u32[]{:S(2)}, u32[]{:S(2)}) collective-permute-start(f32[256,128]{0,1:T(8,128)S(1)} %bitcast_add_fusion.10), channel_id=1, source_target_pairs={{0,2},{2,0},{4,6},{6,4},{8,10},{10,8},{12,14},{14,12},{16,18},{18,... | collective-permute-start | bytes 393224 | tf_op jit(solution)/shard_map/ppermute | solution.py:24
  29.1 22.4 %collective-permute-start.2 = (f32[256,128]{0,1:T(8,128)S(1)}, f32[256,128]{0,1:T(8,128)S(1)}, u32[]{:S(2)}, u32[]{:S(2)}) collective-permute-start(f32[256,128]{0,1:T(8,128)S(1)} %add.141), channel_id=1, source_target_pairs={{0,4},{2,6},{4,0},{6,2},{8,12},{10,14},{12,8},{14,10},{16,20},{18,... | collective-permute-start | bytes 393224 | tf_op jit(solution)/shard_map/ppermute | solution.py:24
  55.1 5.0 %collective-permute-start.3 = (f32[256,128]{0,1:T(8,128)S(1)}, f32[256,128]{0,1:T(8,128)S(1)}, u32[]{:S(2)}, u32[]{:S(2)}) collective-permute-start(f32[256,128]{0,1:T(8,128)S(1)} %add.142), channel_id=1, source_target_pairs={{0,8},{2,10},{4,12},{6,14},{8,0},{10,2},{12,4},{14,6},{16,24},{18,... | collective-permute-start | bytes 393224 | tf_op jit(solution)/shard_map/ppermute | solution.py:24
  60.1 8.3 %collective-permute-start.4 = (f32[256,128]{0,1:T(8,128)S(1)}, f32[256,128]{0,1:T(8,128)S(1)}, u32[]{:S(2)}, u32[]{:S(2)}) collective-permute-start(f32[256,128]{0,1:T(8,128)S(1)} %add.143), channel_id=1, source_target_pairs={{0,16},{2,18},{4,20},{6,22},{8,24},{10,26},{12,28},{14,30},{16,0},... | collective-permute-start | bytes 393224 | tf_op jit(solution)/shard_map/ppermute | solution.py:24
  68.5 1.4 collective-permute-start.5
  71.8 47.7 %all-to-all-start.1 = ((bf16[32,32,896]{2,1,0:T(8,128)(2,1)}), bf16[32,32,896]{2,1,0:T(8,128)(2,1)S(1)}, u32[]{:S(2)}, u32[]{:S(2)}) async-start(bf16[32,32,896]{2,1,0:T(8,128)(2,1)} %copy.50), calls=%async_computation.1 | async-start | bytes 3670016 | tf_op jit(solution)/shard_map/all_to_all | solution.py:86
  102.3 7.0 %collective-permute-start.6 = (f32[512,896]{1,0:T(8,128)}, f32[512,896]{1,0:T(8,128)}, u32[]{:S(2)}, u32[]{:S(2)}) collective-permute-start(f32[512,896]{1,0:T(8,128)} %slice_select_fusion.1), channel_id=1, source_target_pairs={{0,1},{1,0},{2,3},{3,2},{4,5},{5,4},{6,7},{7,6},{8,9},{9,8},{10,11... | collective-permute-start | bytes 5505032 | tf_op jit(solution)/shard_map/ppermute | solution.py:24
  104.0 9.3 %collective-permute-start.7 = (f32[512,896]{1,0:T(8,128)}, f32[512,896]{1,0:T(8,128)}, u32[]{:S(2)}, u32[]{:S(2)}) collective-permute-start(f32[512,896]{1,0:T(8,128)} %slice_select_fusion), channel_id=1, source_target_pairs={{0,1},{1,0},{2,3},{3,2},{4,5},{5,4},{6,7},{7,6},{8,9},{9,8},{10,11... | collective-permute-start | bytes 5505032 | tf_op jit(solution)/shard_map/ppermute | solution.py:24
  123.6 1.9 collective-permute-start.8
  125.4 10.9 %collective-permute-start.13 = (bf16[256,896]{1,0:T(8,128)(2,1)S(1)}, bf16[256,896]{1,0:T(8,128)(2,1)S(1)}, u32[]{:S(2)}, u32[]{:S(2)}) collective-permute-start(bf16[256,896]{1,0:T(8,128)(2,1)S(1)} %pad_maximum_fusion.1), channel_id=1, source_target_pairs={{0,1},{1,0},{2,3},{3,2},{4,5},{5,4},{6,7},{7,6},{8,9},{9,8},{10,11... | collective-permute-start | bytes 1376264 | tf_op jit(solution)/shard_map/ppermute | solution.py:24
  131.0 14.5 %collective-permute-start.11 = (bf16[2,2,2,16,2048]{4,3,0,1,2:T(8,128)(2,1)S(1)}, bf16[2,2,2,16,2048]{4,3,0,1,2:T(8,128)(2,1)S(1)}, u32[]{:S(2)}, u32[]{:S(2)}) collective-permute-start(bf16[2,2,2,16,2048]{4,3,0,1,2:T(8,128)(2,1)S(1)} %fusion.21), channel_id=1, source_target_pairs={{0,4},{2,6},{4,0},{6,2},{8,12},{10,14},{12,8},{14,10},{16,20},{18,... | collective-permute-start | bytes 1572872 | tf_op jit(solution)/shard_map/ppermute | solution.py:24
  134.6 14.8 %collective-permute-start.9 = (bf16[2,2,2,16,2048]{4,3,0,1,2:T(8,128)(2,1)S(1)}, bf16[2,2,2,16,2048]{4,3,0,1,2:T(8,128)(2,1)S(1)}, u32[]{:S(2)}, u32[]{:S(2)}) collective-permute-start(bf16[2,2,2,16,2048]{4,3,0,1,2:T(8,128)(2,1)S(1)} %fusion.20), channel_id=1, source_target_pairs={{0,2},{2,0},{4,6},{6,4},{8,10},{10,8},{12,14},{14,12},{16,18},{18,... | collective-permute-start | bytes 1572872 | tf_op jit(solution)/shard_map/ppermute | solution.py:24
  145.7 9.4 %collective-permute-start.12 = (bf16[2,2,16,2048]{3,2,0,1:T(8,128)(2,1)S(1)}, bf16[2,2,16,2048]{3,2,0,1:T(8,128)(2,1)S(1)}, u32[]{:S(2)}, u32[]{:S(2)}) collective-permute-start(bf16[2,2,16,2048]{3,2,0,1:T(8,128)(2,1)S(1)} %fusion.43), channel_id=1, source_target_pairs={{0,2},{2,0},{4,6},{6,4},{8,10},{10,8},{12,14},{14,12},{16,18},{18,... | collective-permute-start | bytes 786440 | tf_op jit(solution)/shard_map/ppermute | solution.py:24
  149.6 9.3 %collective-permute-start.10 = (bf16[2,2,16,2048]{3,2,0,1:T(8,128)(2,1)S(1)}, bf16[2,2,16,2048]{3,2,0,1:T(8,128)(2,1)S(1)}, u32[]{:S(2)}, u32[]{:S(2)}) collective-permute-start(bf16[2,2,16,2048]{3,2,0,1:T(8,128)(2,1)S(1)} %fusion.42), channel_id=1, source_target_pairs={{0,4},{2,6},{4,0},{6,2},{8,12},{10,14},{12,8},{14,10},{16,20},{18,... | collective-permute-start | bytes 786440 | tf_op jit(solution)/shard_map/ppermute | solution.py:24
  149.7 18.3 %collective-permute-start.15 = (bf16[2,2,2,16,2048]{4,3,0,1,2:T(8,128)(2,1)S(1)}, bf16[2,2,2,16,2048]{4,3,0,1,2:T(8,128)(2,1)S(1)}, u32[]{:S(2)}, u32[]{:S(2)}) collective-permute-start(bf16[2,2,2,16,2048]{4,3,0,1,2:T(8,128)(2,1)S(1)} %fusion.23), channel_id=1, source_target_pairs={{0,4},{2,6},{4,0},{6,2},{8,12},{10,14},{12,8},{14,10},{16,20},{18,... | collective-permute-start | bytes 1572872 | tf_op jit(solution)/shard_map/ppermute | solution.py:24
  151.7 18.1 %collective-permute-start.14 = (bf16[2,2,2,16,2048]{4,3,0,1,2:T(8,128)(2,1)S(1)}, bf16[2,2,2,16,2048]{4,3,0,1,2:T(8,128)(2,1)S(1)}, u32[]{:S(2)}, u32[]{:S(2)}) collective-permute-start(bf16[2,2,2,16,2048]{4,3,0,1,2:T(8,128)(2,1)S(1)} %fusion.22), channel_id=1, source_target_pairs={{0,2},{2,0},{4,6},{6,4},{8,10},{10,8},{12,14},{14,12},{16,18},{18,... | collective-permute-start | bytes 1572872 | tf_op jit(solution)/shard_map/ppermute | solution.py:24
  168.2 6.4 %collective-permute-start.19 = (bf16[2,2,16,2048]{3,2,0,1:T(8,128)(2,1)S(1)}, bf16[2,2,16,2048]{3,2,0,1:T(8,128)(2,1)S(1)}, u32[]{:S(2)}, u32[]{:S(2)}) collective-permute-start(bf16[2,2,16,2048]{3,2,0,1:T(8,128)(2,1)S(1)} %fusion.45), channel_id=1, source_target_pairs={{0,2},{2,0},{4,6},{6,4},{8,10},{10,8},{12,14},{14,12},{16,18},{18,... | collective-permute-start | bytes 786440 | tf_op jit(solution)/shard_map/ppermute | solution.py:24
  170.0 6.4 %collective-permute-start.18 = (bf16[2,2,16,2048]{3,2,0,1:T(8,128)(2,1)S(1)}, bf16[2,2,16,2048]{3,2,0,1:T(8,128)(2,1)S(1)}, u32[]{:S(2)}, u32[]{:S(2)}) collective-permute-start(bf16[2,2,16,2048]{3,2,0,1:T(8,128)(2,1)S(1)} %fusion.44), channel_id=1, source_target_pairs={{0,4},{2,6},{4,0},{6,2},{8,12},{10,14},{12,8},{14,10},{16,20},{18,... | collective-permute-start | bytes 786440 | tf_op jit(solution)/shard_map/ppermute | solution.py:24
  170.5 8.6 %collective-permute-start.16 = (bf16[2,16,4096]{2,1,0:T(8,128)(2,1)S(1)}, bf16[2,16,4096]{2,1,0:T(8,128)(2,1)S(1)}, u32[]{:S(2)}, u32[]{:S(2)}) collective-permute-start(bf16[2,16,4096]{2,1,0:T(8,128)(2,1)S(1)} %fusion.46), channel_id=1, source_target_pairs={{0,8},{2,10},{4,12},{6,14},{8,0},{10,2},{12,4},{14,6},{16,24},{18,... | collective-permute-start | bytes 786440 | tf_op jit(solution)/shard_map/ppermute | solution.py:24
  176.6 7.9 %collective-permute-start.20 = (bf16[2,16,4096]{2,1,0:T(8,128)(2,1)S(1)}, bf16[2,16,4096]{2,1,0:T(8,128)(2,1)S(1)}, u32[]{:S(2)}, u32[]{:S(2)}) collective-permute-start(bf16[2,16,4096]{2,1,0:T(8,128)(2,1)S(1)} %fusion.47), channel_id=1, source_target_pairs={{0,8},{2,10},{4,12},{6,14},{8,0},{10,2},{12,4},{14,6},{16,24},{18,... | collective-permute-start | bytes 786440 | tf_op jit(solution)/shard_map/ppermute | solution.py:24
  179.2 10.9 %collective-permute-start.17 = (bf16[16,4096]{1,0:T(8,128)(2,1)S(1)}, bf16[16,4096]{1,0:T(8,128)(2,1)S(1)}, u32[]{:S(2)}, u32[]{:S(2)}) collective-permute-start(bf16[16,4096]{1,0:T(8,128)(2,1)S(1)} %fusion.92), channel_id=1, source_target_pairs={{0,16},{2,18},{4,20},{6,22},{8,24},{10,26},{12,28},{14,30},{16,0},... | collective-permute-start | bytes 393224 | tf_op jit(solution)/shard_map/ppermute | solution.py:24
  184.6 7.6 %collective-permute-start.21 = (bf16[16,4096]{1,0:T(8,128)(2,1)S(1)}, bf16[16,4096]{1,0:T(8,128)(2,1)S(1)}, u32[]{:S(2)}, u32[]{:S(2)}) collective-permute-start(bf16[16,4096]{1,0:T(8,128)(2,1)S(1)} %fusion.93), channel_id=1, source_target_pairs={{0,16},{2,18},{4,20},{6,22},{8,24},{10,26},{12,28},{14,30},{16,0},... | collective-permute-start | bytes 393224 | tf_op jit(solution)/shard_map/ppermute | solution.py:24
  (20 other events, 150.8 us)

commit v7 on v6

--- a/solution.py
+++ b/solution.py
@@ -115,12 +115,13 @@
     shrunk, weights, block_slots, _ = lax.optimization_barrier(
         (shrunk, weights, block_slots, pages[0])
     )
-    shrunk = sum_over(shrunk, range(middle, bits_of("pool")))
-    shrunk = gather(shrunk, "tensor", 0)
+    last = bits_of("pool") - 1
+    shrunk = sum_over(shrunk, range(middle, last))
     for kind in range(1, kinds):
         outgoing[kind] = after(outgoing[kind], (shrunk, pages[-1]))
         pages.append(exchange_columns(outgoing[kind]))
 
+    shrunk = gather(sum_over(shrunk, range(last, last + 1)), "tensor", 0)
     flat_tokens = tokens.reshape(steps * total_rows, width_local)
     weights, flat_tokens, _ = lax.optimization_barrier((weights, flat_tokens, outgoing[-1]))
     products = [

time: 193 us -> 201 us (1.041)
  waiting for transfers between devices: 72.4 us -> 78 us
  starting transfers between devices: 28.5 us -> 30.7 us
    ppermute x22, waiting for transfers between devices: 65.6 us -> 74.3 us  [swap(): return lax.ppermute(array, axis_name, bit_pairs(axis_name, bit))]
    all_to_all x2, waiting for transfers between devices: 6.75 us -> 3.74 us  [exchange_columns(): lax.all_to_all(columns, ('pool', 'tensor'), split_axis=0, concat_axis=0,...]
    ppermute x22, starting transfers between devices: 16.6 us -> 18.8 us  [swap(): return lax.ppermute(array, axis_name, bit_pairs(axis_name, bit))]
  transfers between devices with their start and end apart: 24 -> 24, of which waited for: 18 -> 16; matrix products, arithmetic and copies ran while one was open for 41% -> 40% of each run, Pallas kernels for 0% -> 0%
where the time goes in v7:
time: 201 us
  waiting for transfers between devices  78 us (39%)
  matrix products  41.6 us (21%)
  local copies, waits for them, and re-layouts  37 us (18%)
  starting transfers between devices  30.7 us (15%)
  other arithmetic  12.6 us (6%)
    ppermute x22, waiting for transfers between devices, swap(): return lax.ppermute(array, axis_name, bit_pairs(axis_name, bit))  74.3 us
    dot_general x2, matrix products, shards(): jnp.dot(flat_tokens, weights[kind], preferred_element_type=jnp.float32)  23.7 us
    optimization_barrier x2, local copies, waits for them, and re-layouts, after(): return lax.optimization_barrier((array, arrived))[0]  22.1 us
    ppermute x22, starting transfers between devices, swap(): return lax.ppermute(array, axis_name, bit_pairs(axis_name, bit))  18.8 us
    dot_general x4, matrix products, shards(): jnp.dot(hidden, down_weight[:, piece * half:(piece + 1) * half], preferre...  11.9 us
    all_to_all x2, starting transfers between devices, exchange_columns(): lax.all_to_all(columns, ('pool', 'tensor'), split_axis=0, concat_axis=0,...  11.8 us
    add x2, other arithmetic, shards(): jnp.where(core == 0, low_share[rows], high_share[rows]) + got[rows]  6.98 us
    squeeze x2, local copies, waits for them, and re-layouts, shards(): lax.dynamic_index_in_dim(one, block_slots[step][block], 0, keepdims=False)  6.51 us
  transfers between devices with their start and end apart: 24, of which 16 were waited for; matrix products, arithmetic and copies ran while one was open for 40% of the time, Pallas kernels for 0%

profile of v7, /device:TPU:0, one launch (start us, length us, event | category | flops | bytes accessed | tf_op | source)
XLA Modules:
  0.0 200.5 jit_solution(16548660823026403236)
XLA Ops:
  4.4 7.4 %all-to-all-start = ((bf16[32,32,896]{2,1,0:T(8,128)(2,1)}), bf16[32,32,896]{2,1,0:T(8,128)(2,1)}, u32[]{:S(2)}, u32[]{:S(2)}) async-start(bf16[32,32,896]{2,1,0:T(8,128)(2,1)} %copy.49), calls=%async_computation | async-start | bytes 3670016 | tf_op jit(solution)/shard_map/all_to_all | solution.py:86
  12.8 3.7 %fusion.16 = f32[2,256,2,64]{1,3,2,0:T(8,128)S(1)} fusion(bf16[2,256,4096]{2,1,0:T(8,128)(2,1)} %param.8, bf16[1,2,4096,64]{2,3,1,0:T(8,128)(2,1)S(1)} %copy-done, f32[2,256]{1,0:T(2,128)S(1)} %bitcast.160), kind=kOutput, calls=%fused_computation.28 | convolution fusion | flops 536936448 | bytes 5507072 | tf_op jit(solution)/shard_map/snd,kdc->snkc/dot_general | solution.py:92
  19.7 9.3 %collective-permute-done.1 = f32[256,128]{0,1:T(8,128)S(1)} collective-permute-done((f32[256,128]{0,1:T(8,128)S(1)}, f32[256,128]{0,1:T(8,128)S(1)}, u32[]{:S(2)}, u32[]{:S(2)}) %collective-permute-start.1) | collective-permute-done | bytes 131104 | tf_op jit(solution)/shard_map/ppermute | solution.py:24
  30.4 20.3 %copy.85 = bf16[4096,2,1792]{2,0,1:T(8,128)(2,1)} copy(bf16[4096,2,1792]{2,1,0:T(2,128)(2,1)} %param.9) | data formatting | bytes 58720256 | tf_op jit(solution)/shard_map/optimization_barrier | solution.py:55
  51.4 3.7 %all-to-all-done = bf16[32,32,896]{2,1,0:T(8,128)(2,1)} async-done(((bf16[32,32,896]{2,1,0:T(8,128)(2,1)}), bf16[32,32,896]{2,1,0:T(8,128)(2,1)}, u32[]{:S(2)}, u32[]{:S(2)}) %all-to-all-start) | async-done | bytes 1835040 | tf_op jit(solution)/shard_map/all_to_all | solution.py:86
  55.4 4.8 %collective-permute-done.3 = f32[256,128]{0,1:T(8,128)S(1)} collective-permute-done((f32[256,128]{0,1:T(8,128)S(1)}, f32[256,128]{0,1:T(8,128)S(1)}, u32[]{:S(2)}, u32[]{:S(2)}) %collective-permute-start.3) | collective-permute-done | bytes 131104 | tf_op jit(solution)/shard_map/ppermute | solution.py:24
  62.0 4.4 %all-to-all-start.1 = ((bf16[32,32,896]{2,1,0:T(8,128)(2,1)}), bf16[32,32,896]{2,1,0:T(8,128)(2,1)S(1)}, u32[]{:S(2)}, u32[]{:S(2)}) async-start(bf16[32,32,896]{2,1,0:T(8,128)(2,1)} %copy.50), calls=%async_computation.1 | async-start | bytes 3670016 | tf_op jit(solution)/shard_map/all_to_all | solution.py:86
  66.4 11.8 %fusion = f32[512,1792]{1,0:T(8,128)S(1)} fusion(bf16[512,4096]{1,0:T(8,128)(2,1)} %bitcast.163, bf16[2,4096,1792]{2,1,0:T(8,128)(2,1)} %bitcast.143), kind=kOutput, calls=%fused_computation.2 | convolution fusion | flops 7516192768 | bytes 22544384 | tf_op jit(solution)/shard_map/dot_general | solution.py:128
  78.3 11.9 %fusion.2 = f32[512,1792]{1,0:T(8,128)S(1)} fusion(bf16[512,4096]{1,0:T(8,128)(2,1)S(1)} %bitcast.164, bf16[2,4096,1792]{2,1,0:T(8,128)(2,1)} %bitcast.144), kind=kOutput, calls=%fused_computation.4 | convolution fusion | flops 7516192768 | bytes 22544384 | tf_op jit(solution)/shard_map/dot_general | solution.py:128
  94.5 2.7 %collective-permute-start.5 = (f32[256,128]{0,1:T(8,128)S(1)}, f32[256,128]{0,1:T(8,128)S(1)}, u32[]{:S(2)}, u32[]{:S(2)}) collective-permute-start(f32[256,128]{0,1:T(8,128)S(1)} %add.143), channel_id=1, source_target_pairs={{0,16},{2,18},{4,20},{6,22},{8,24},{10,26},{12,28},{14,30},{16,0},... | collective-permute-start | bytes 393224 | tf_op jit(solution)/shard_map/ppermute | solution.py:24
  97.2 18.0 %collective-permute-done.5 = f32[256,128]{0,1:T(8,128)S(1)} collective-permute-done((f32[256,128]{0,1:T(8,128)S(1)}, f32[256,128]{0,1:T(8,128)S(1)}, u32[]{:S(2)}, u32[]{:S(2)}) %collective-permute-start.5) | collective-permute-done | bytes 131104 | tf_op jit(solution)/shard_map/ppermute | solution.py:24
  115.9 3.7 %dynamic-slice_bitcast_fusion.8 = (bf16[64,896]{1,0:T(8,128)(2,1)S(1)}, bf16[64,896]{1,0:T(8,128)(2,1)S(1)}, bf16[64,896]{1,0:T(8,128)(2,1)S(1)}, bf16[64,896]{1,0:T(8,128)(2,1)S(1)}) fusion(bf16[16,64,896]{2,1,0:T(8,128)(2,1)} %bitcast.13, u32[]{:T(128)} %bitcast.9, u32[]{:T(128)} %bitcast.12, u32[]{:T(128)} %bitcast.11, u32[]{:T(128)} %bitcast.10), kind=kLoop, calls=%fused_computation.147 | loop fusion | bytes 917520 | tf_op jit(solution)/shard_map/jit(dynamic_index_in_dim)/squeeze | solution.py:161
  120.4 3.9 %slice_add_fusion.3 = (f32[256,896]{1,0:T(8,128)}, f32[256,896]{1,0:T(8,128)S(1)}) fusion(f32[512,896]{1,0:T(8,128)} %collective-permute-done.4, f32[512,1792]{1,0:T(8,128)} %copy-done.5, pred[]{:T(512)S(6)} %eq.17), kind=kLoop, calls=%fused_computation.41 | loop fusion | flops 917504 | bytes 7340033 | tf_op jit(solution)/shard_map/add | solution.py:140
  124.3 3.1 %slice_add_fusion.2 = (f32[256,896]{1,0:T(8,128)}, f32[256,896]{1,0:T(8,128)}) fusion(f32[512,896]{1,0:T(8,128)} %collective-permute-done.7, f32[512,1792]{1,0:T(8,128)S(1)} %copy-done.4, pred[]{:T(512)S(6)} %eq.17), kind=kLoop, calls=%fused_computation.40 | loop fusion | flops 917504 | bytes 7340033 | tf_op jit(solution)/shard_map/add | solution.py:140
  127.4 2.8 %dynamic-slice_bitcast_fusion.7 = (bf16[64,896]{1,0:T(8,128)(2,1)S(1)}, bf16[64,896]{1,0:T(8,128)(2,1)S(1)}, bf16[64,896]{1,0:T(8,128)(2,1)S(1)}, bf16[64,896]{1,0:T(8,128)(2,1)S(1)}) fusion(bf16[16,64,896]{2,1,0:T(8,128)(2,1)S(1)} %bitcast.149, u32[]{:T(128)} %bitcast.9, u32[]{:T(128)} %bitcast.12, u32[]{:T(128)} %bitcast.11, u32[]{:T(128)} %bitcast.10), kind=kLoop, calls=%fused_computation.146 | loop fusion | bytes 917520 | tf_op jit(solution)/shard_map/jit(dynamic_index_in_dim)/squeeze | solution.py:161
  133.9 5.6 %fusion.8 = f32[256,2048]{1,0:T(8,128)S(1)} fusion(bf16[1792,4096]{1,0:T(8,128)(2,1)} %param.10, bf16[256,896]{1,0:T(8,128)(2,1)S(1)} %collective-permute-done.8, bf16[128,896]{1,0:T(8,128)(2,1)S(1)} %fusion.39, bf16[128,896]{1,0:T(8,128)(2,1)S(1)} %fusion.41, pred[]{:T(512)S(6)} %eq.16), kind=kOutput, calls=%fused_computation.10 | convolution fusion | flops 1885011968 | bytes 10354689 | tf_op jit(solution)/shard_map/dot_general | solution.py:180
  149.2 4.2 %collective-permute-done.11 = bf16[2,2,2,16,2048]{4,3,0,1,2:T(8,128)(2,1)S(1)} collective-permute-done((bf16[2,2,2,16,2048]{4,3,0,1,2:T(8,128)(2,1)S(1)}, bf16[2,2,2,16,2048]{4,3,0,1,2:T(8,128)(2,1)S(1)}, u32[]{:S(2)}, u32[]{:S(2)}) %collective-permute-start.11) | collective-permute-done | bytes 524320 | tf_op jit(solution)/shard_map/ppermute | solution.py:24
  154.9 3.1 %collective-permute-done.9 = bf16[2,2,2,16,2048]{4,3,0,1,2:T(8,128)(2,1)S(1)} collective-permute-done((bf16[2,2,2,16,2048]{4,3,0,1,2:T(8,128)(2,1)S(1)}, bf16[2,2,2,16,2048]{4,3,0,1,2:T(8,128)(2,1)S(1)}, u32[]{:S(2)}, u32[]{:S(2)}) %collective-permute-start.9) | collective-permute-done | bytes 524320 | tf_op jit(solution)/shard_map/ppermute | solution.py:24
  163.7 3.8 %collective-permute-done.10 = bf16[2,2,16,2048]{3,2,0,1:T(8,128)(2,1)S(1)} collective-permute-done((bf16[2,2,16,2048]{3,2,0,1:T(8,128)(2,1)S(1)}, bf16[2,2,16,2048]{3,2,0,1:T(8,128)(2,1)S(1)}, u32[]{:S(2)}, u32[]{:S(2)}) %collective-permute-start.10) | collective-permute-done | bytes 262176 | tf_op jit(solution)/shard_map/ppermute | solution.py:24
  167.6 7.5 %collective-permute-done.15 = bf16[2,2,2,16,2048]{4,3,0,1,2:T(8,128)(2,1)S(1)} collective-permute-done((bf16[2,2,2,16,2048]{4,3,0,1,2:T(8,128)(2,1)S(1)}, bf16[2,2,2,16,2048]{4,3,0,1,2:T(8,128)(2,1)S(1)}, u32[]{:S(2)}, u32[]{:S(2)}) %collective-permute-start.15) | collective-permute-done | bytes 524320 | tf_op jit(solution)/shard_map/ppermute | solution.py:24
  177.6 4.1 %collective-permute-done.19 = bf16[2,2,16,2048]{3,2,0,1:T(8,128)(2,1)S(1)} collective-permute-done((bf16[2,2,16,2048]{3,2,0,1:T(8,128)(2,1)S(1)}, bf16[2,2,16,2048]{3,2,0,1:T(8,128)(2,1)S(1)}, u32[]{:S(2)}, u32[]{:S(2)}) %collective-permute-start.19) | collective-permute-done | bytes 262176 | tf_op jit(solution)/shard_map/ppermute | solution.py:24
  183.9 4.2 %collective-permute-done.16 = bf16[2,16,4096]{2,1,0:T(8,128)(2,1)S(1)} collective-permute-done((bf16[2,16,4096]{2,1,0:T(8,128)(2,1)S(1)}, bf16[2,16,4096]{2,1,0:T(8,128)(2,1)S(1)}, u32[]{:S(2)}, u32[]{:S(2)}) %collective-permute-start.16) | collective-permute-done | bytes 262176 | tf_op jit(solution)/shard_map/ppermute | solution.py:24
  188.5 2.6 %collective-permute-done.20 = bf16[2,16,4096]{2,1,0:T(8,128)(2,1)S(1)} collective-permute-done((bf16[2,16,4096]{2,1,0:T(8,128)(2,1)S(1)}, bf16[2,16,4096]{2,1,0:T(8,128)(2,1)S(1)}, u32[]{:S(2)}, u32[]{:S(2)}) %collective-permute-start.20) | collective-permute-done | bytes 262176 | tf_op jit(solution)/shard_map/ppermute | solution.py:24
  191.7 6.5 %collective-permute-done.17 = bf16[16,4096]{1,0:T(8,128)(2,1)S(1)} collective-permute-done((bf16[16,4096]{1,0:T(8,128)(2,1)S(1)}, bf16[16,4096]{1,0:T(8,128)(2,1)S(1)}, u32[]{:S(2)}, u32[]{:S(2)}) %collective-permute-start.17) | collective-permute-done | bytes 131104 | tf_op jit(solution)/shard_map/ppermute | solution.py:24
  (143 shorter events, 46.8 us)
Async XLA Ops:
  4.4 50.7 %all-to-all-start = ((bf16[32,32,896]{2,1,0:T(8,128)(2,1)}), bf16[32,32,896]{2,1,0:T(8,128)(2,1)}, u32[]{:S(2)}, u32[]{:S(2)}) async-start(bf16[32,32,896]{2,1,0:T(8,128)(2,1)} %copy.49), calls=%async_computation | async-start | bytes 3670016 | tf_op jit(solution)/shard_map/all_to_all | solution.py:86
  16.5 1.4 collective-permute-start
  18.0 11.1 %collective-permute-start.1 = (f32[256,128]{0,1:T(8,128)S(1)}, f32[256,128]{0,1:T(8,128)S(1)}, u32[]{:S(2)}, u32[]{:S(2)}) collective-permute-start(f32[256,128]{0,1:T(8,128)S(1)} %bitcast_add_fusion.10), channel_id=1, source_target_pairs={{0,2},{2,0},{4,6},{6,4},{8,10},{10,8},{12,14},{14,12},{16,18},{18,... | collective-permute-start | bytes 393224 | tf_op jit(solution)/shard_map/ppermute | solution.py:24
  29.1 22.2 %collective-permute-start.2 = (f32[256,128]{0,1:T(8,128)S(1)}, f32[256,128]{0,1:T(8,128)S(1)}, u32[]{:S(2)}, u32[]{:S(2)}) collective-permute-start(f32[256,128]{0,1:T(8,128)S(1)} %add.141), channel_id=1, source_target_pairs={{0,4},{2,6},{4,0},{6,2},{8,12},{10,14},{12,8},{14,10},{16,20},{18,... | collective-permute-start | bytes 393224 | tf_op jit(solution)/shard_map/ppermute | solution.py:24
  55.1 5.0 %collective-permute-start.3 = (f32[256,128]{0,1:T(8,128)S(1)}, f32[256,128]{0,1:T(8,128)S(1)}, u32[]{:S(2)}, u32[]{:S(2)}) collective-permute-start(f32[256,128]{0,1:T(8,128)S(1)} %add.142), channel_id=1, source_target_pairs={{0,8},{2,10},{4,12},{6,14},{8,0},{10,2},{12,4},{14,6},{16,24},{18,... | collective-permute-start | bytes 393224 | tf_op jit(solution)/shard_map/ppermute | solution.py:24
  62.0 65.4 %all-to-all-start.1 = ((bf16[32,32,896]{2,1,0:T(8,128)(2,1)}), bf16[32,32,896]{2,1,0:T(8,128)(2,1)S(1)}, u32[]{:S(2)}, u32[]{:S(2)}) async-start(bf16[32,32,896]{2,1,0:T(8,128)(2,1)} %copy.50), calls=%async_computation.1 | async-start | bytes 3670016 | tf_op jit(solution)/shard_map/all_to_all | solution.py:86
  92.5 27.9 %collective-permute-start.4 = (f32[512,896]{1,0:T(8,128)}, f32[512,896]{1,0:T(8,128)}, u32[]{:S(2)}, u32[]{:S(2)}) collective-permute-start(f32[512,896]{1,0:T(8,128)} %slice_select_fusion.1), channel_id=1, source_target_pairs={{0,1},{1,0},{2,3},{3,2},{4,5},{5,4},{6,7},{7,6},{8,9},{9,8},{10,11... | collective-permute-start | bytes 5505032 | tf_op jit(solution)/shard_map/ppermute | solution.py:24
  94.2 30.1 %collective-permute-start.7 = (f32[512,896]{1,0:T(8,128)}, f32[512,896]{1,0:T(8,128)}, u32[]{:S(2)}, u32[]{:S(2)}) collective-permute-start(f32[512,896]{1,0:T(8,128)} %slice_select_fusion), channel_id=1, source_target_pairs={{0,1},{1,0},{2,3},{3,2},{4,5},{5,4},{6,7},{7,6},{8,9},{9,8},{10,11... | collective-permute-start | bytes 5505032 | tf_op jit(solution)/shard_map/ppermute | solution.py:24
  94.5 20.8 %collective-permute-start.5 = (f32[256,128]{0,1:T(8,128)S(1)}, f32[256,128]{0,1:T(8,128)S(1)}, u32[]{:S(2)}, u32[]{:S(2)}) collective-permute-start(f32[256,128]{0,1:T(8,128)S(1)} %add.143), channel_id=1, source_target_pairs={{0,16},{2,18},{4,20},{6,22},{8,24},{10,26},{12,28},{14,30},{16,0},... | collective-permute-start | bytes 393224 | tf_op jit(solution)/shard_map/ppermute | solution.py:24
  115.3 4.4 %collective-permute-start.6 = (f32[256,128]{0,1:T(8,128)S(1)}, f32[256,128]{0,1:T(8,128)S(1)}, u32[]{:S(2)}, u32[]{:S(2)}) collective-permute-start(f32[256,128]{0,1:T(8,128)S(1)} %add.145), channel_id=1, source_target_pairs={{0,1},{1,0},{2,3},{3,2},{4,5},{5,4},{6,7},{7,6},{8,9},{9,8},{10,11... | collective-permute-start | bytes 393224 | tf_op jit(solution)/shard_map/ppermute | solution.py:24
  131.5 2.3 %collective-permute-start.8 = (bf16[256,896]{1,0:T(8,128)(2,1)S(1)}, bf16[256,896]{1,0:T(8,128)(2,1)S(1)}, u32[]{:S(2)}, u32[]{:S(2)}) collective-permute-start(bf16[256,896]{1,0:T(8,128)(2,1)S(1)} %pad_maximum_fusion), channel_id=1, source_target_pairs={{0,1},{1,0},{2,3},{3,2},{4,5},{5,4},{6,7},{7,6},{8,9},{9,8},{10,11... | collective-permute-start | bytes 1376264 | tf_op jit(solution)/shard_map/ppermute | solution.py:24
  133.4 11.4 %collective-permute-start.13 = (bf16[256,896]{1,0:T(8,128)(2,1)S(1)}, bf16[256,896]{1,0:T(8,128)(2,1)S(1)}, u32[]{:S(2)}, u32[]{:S(2)}) collective-permute-start(bf16[256,896]{1,0:T(8,128)(2,1)S(1)} %pad_maximum_fusion.1), channel_id=1, source_target_pairs={{0,1},{1,0},{2,3},{3,2},{4,5},{5,4},{6,7},{7,6},{8,9},{9,8},{10,11... | collective-permute-start | bytes 1376264 | tf_op jit(solution)/shard_map/ppermute | solution.py:24
  139.5 13.8 %collective-permute-start.11 = (bf16[2,2,2,16,2048]{4,3,0,1,2:T(8,128)(2,1)S(1)}, bf16[2,2,2,16,2048]{4,3,0,1,2:T(8,128)(2,1)S(1)}, u32[]{:S(2)}, u32[]{:S(2)}) collective-permute-start(bf16[2,2,2,16,2048]{4,3,0,1,2:T(8,128)(2,1)S(1)} %fusion.21), channel_id=1, source_target_pairs={{0,4},{2,6},{4,0},{6,2},{8,12},{10,14},{12,8},{14,10},{16,20},{18,... | collective-permute-start | bytes 1572872 | tf_op jit(solution)/shard_map/ppermute | solution.py:24
  143.2 14.9 %collective-permute-start.9 = (bf16[2,2,2,16,2048]{4,3,0,1,2:T(8,128)(2,1)S(1)}, bf16[2,2,2,16,2048]{4,3,0,1,2:T(8,128)(2,1)S(1)}, u32[]{:S(2)}, u32[]{:S(2)}) collective-permute-start(bf16[2,2,2,16,2048]{4,3,0,1,2:T(8,128)(2,1)S(1)} %fusion.20), channel_id=1, source_target_pairs={{0,2},{2,0},{4,6},{6,4},{8,10},{10,8},{12,14},{14,12},{16,18},{18,... | collective-permute-start | bytes 1572872 | tf_op jit(solution)/shard_map/ppermute | solution.py:24
  153.5 10.2 %collective-permute-start.12 = (bf16[2,2,16,2048]{3,2,0,1:T(8,128)(2,1)S(1)}, bf16[2,2,16,2048]{3,2,0,1:T(8,128)(2,1)S(1)}, u32[]{:S(2)}, u32[]{:S(2)}) collective-permute-start(bf16[2,2,16,2048]{3,2,0,1:T(8,128)(2,1)S(1)} %fusion.43), channel_id=1, source_target_pairs={{0,2},{2,0},{4,6},{6,4},{8,10},{10,8},{12,14},{14,12},{16,18},{18,... | collective-permute-start | bytes 786440 | tf_op jit(solution)/shard_map/ppermute | solution.py:24
  158.2 9.3 %collective-permute-start.10 = (bf16[2,2,16,2048]{3,2,0,1:T(8,128)(2,1)S(1)}, bf16[2,2,16,2048]{3,2,0,1:T(8,128)(2,1)S(1)}, u32[]{:S(2)}, u32[]{:S(2)}) collective-permute-start(bf16[2,2,16,2048]{3,2,0,1:T(8,128)(2,1)S(1)} %fusion.42), channel_id=1, source_target_pairs={{0,4},{2,6},{4,0},{6,2},{8,12},{10,14},{12,8},{14,10},{16,20},{18,... | collective-permute-start | bytes 786440 | tf_op jit(solution)/shard_map/ppermute | solution.py:24
  158.3 16.8 %collective-permute-start.15 = (bf16[2,2,2,16,2048]{4,3,0,1,2:T(8,128)(2,1)S(1)}, bf16[2,2,2,16,2048]{4,3,0,1,2:T(8,128)(2,1)S(1)}, u32[]{:S(2)}, u32[]{:S(2)}) collective-permute-start(bf16[2,2,2,16,2048]{4,3,0,1,2:T(8,128)(2,1)S(1)} %fusion.23), channel_id=1, source_target_pairs={{0,4},{2,6},{4,0},{6,2},{8,12},{10,14},{12,8},{14,10},{16,20},{18,... | collective-permute-start | bytes 1572872 | tf_op jit(solution)/shard_map/ppermute | solution.py:24
  160.3 16.8 %collective-permute-start.14 = (bf16[2,2,2,16,2048]{4,3,0,1,2:T(8,128)(2,1)S(1)}, bf16[2,2,2,16,2048]{4,3,0,1,2:T(8,128)(2,1)S(1)}, u32[]{:S(2)}, u32[]{:S(2)}) collective-permute-start(bf16[2,2,2,16,2048]{4,3,0,1,2:T(8,128)(2,1)S(1)} %fusion.22), channel_id=1, source_target_pairs={{0,2},{2,0},{4,6},{6,4},{8,10},{10,8},{12,14},{14,12},{16,18},{18,... | collective-permute-start | bytes 1572872 | tf_op jit(solution)/shard_map/ppermute | solution.py:24
  175.3 6.4 %collective-permute-start.19 = (bf16[2,2,16,2048]{3,2,0,1:T(8,128)(2,1)S(1)}, bf16[2,2,16,2048]{3,2,0,1:T(8,128)(2,1)S(1)}, u32[]{:S(2)}, u32[]{:S(2)}) collective-permute-start(bf16[2,2,16,2048]{3,2,0,1:T(8,128)(2,1)S(1)} %fusion.45), channel_id=1, source_target_pairs={{0,2},{2,0},{4,6},{6,4},{8,10},{10,8},{12,14},{14,12},{16,18},{18,... | collective-permute-start | bytes 786440 | tf_op jit(solution)/shard_map/ppermute | solution.py:24
  177.2 6.4 %collective-permute-start.18 = (bf16[2,2,16,2048]{3,2,0,1:T(8,128)(2,1)S(1)}, bf16[2,2,16,2048]{3,2,0,1:T(8,128)(2,1)S(1)}, u32[]{:S(2)}, u32[]{:S(2)}) collective-permute-start(bf16[2,2,16,2048]{3,2,0,1:T(8,128)(2,1)S(1)} %fusion.44), channel_id=1, source_target_pairs={{0,4},{2,6},{4,0},{6,2},{8,12},{10,14},{12,8},{14,10},{16,20},{18,... | collective-permute-start | bytes 786440 | tf_op jit(solution)/shard_map/ppermute | solution.py:24
  177.6 10.5 %collective-permute-start.16 = (bf16[2,16,4096]{2,1,0:T(8,128)(2,1)S(1)}, bf16[2,16,4096]{2,1,0:T(8,128)(2,1)S(1)}, u32[]{:S(2)}, u32[]{:S(2)}) collective-permute-start(bf16[2,16,4096]{2,1,0:T(8,128)(2,1)S(1)} %fusion.46), channel_id=1, source_target_pairs={{0,8},{2,10},{4,12},{6,14},{8,0},{10,2},{12,4},{14,6},{16,24},{18,... | collective-permute-start | bytes 786440 | tf_op jit(solution)/shard_map/ppermute | solution.py:24
  183.8 7.2 %collective-permute-start.20 = (bf16[2,16,4096]{2,1,0:T(8,128)(2,1)S(1)}, bf16[2,16,4096]{2,1,0:T(8,128)(2,1)S(1)}, u32[]{:S(2)}, u32[]{:S(2)}) collective-permute-start(bf16[2,16,4096]{2,1,0:T(8,128)(2,1)S(1)} %fusion.47), channel_id=1, source_target_pairs={{0,8},{2,10},{4,12},{6,14},{8,0},{10,2},{12,4},{14,6},{16,24},{18,... | collective-permute-start | bytes 786440 | tf_op jit(solution)/shard_map/ppermute | solution.py:24
  188.2 10.1 %collective-permute-start.17 = (bf16[16,4096]{1,0:T(8,128)(2,1)S(1)}, bf16[16,4096]{1,0:T(8,128)(2,1)S(1)}, u32[]{:S(2)}, u32[]{:S(2)}) collective-permute-start(bf16[16,4096]{1,0:T(8,128)(2,1)S(1)} %fusion.93), channel_id=1, source_target_pairs={{0,16},{2,18},{4,20},{6,22},{8,24},{10,26},{12,28},{14,30},{16,0},... | collective-permute-start | bytes 393224 | tf_op jit(solution)/shard_map/ppermute | solution.py:24
  191.1 8.6 %collective-permute-start.21 = (bf16[16,4096]{1,0:T(8,128)(2,1)S(1)}, bf16[16,4096]{1,0:T(8,128)(2,1)S(1)}, u32[]{:S(2)}, u32[]{:S(2)}) collective-permute-start(bf16[16,4096]{1,0:T(8,128)(2,1)S(1)} %fusion.94), channel_id=1, source_target_pairs={{0,16},{2,18},{4,20},{6,22},{8,24},{10,26},{12,28},{14,30},{16,0},... | collective-permute-start | bytes 393224 | tf_op jit(solution)/shard_map/ppermute | solution.py:24
  (20 other events, 152.7 us)
